TPU v7x, 32 devices: a whole 2x2x4 slice. The times are simulated.
32 devices in a mesh: label: 8 (over z, y), dp: 4 (over x, core).
Axes of the slice: x: 2, y: 2, z: 4, core: 2. Of those that a mesh axis runs over, the one named last changes fastest.
Arguments:
- queries: bfloat16 [4096, 768], P(('label', 'dp')), may hold values from -320 to 320
- weights: bfloat16 [5120, 768], P('label'), may hold values from -0.21875 to 0.21875
- counts: int32 [5120], P('label'), may hold values from 1 to 4096
- hits: int32 [4096, 4], P(('label', 'dp')), may hold values from 0 to 7, all different within a row; in each aligned block of 128 rows (0 to 127, 128 to 255, ...) at most 96 rows name the same one
- positive_offset: int32 [4096], P(('label', 'dp')), may hold values from 0 to 639
- cluster_shard: int32 [8], replicated, may hold values from 0 to 7, each once
Outputs:
- query_loss: float32 [4096], P(('label', 'dp'))
- query_grad: bfloat16 [4096, 768], P(('label', 'dp'))
- weight_grad: bfloat16 [5120, 768], P(('label', 'dp'))
Inputs may be any that keep to these rules, and one draw needn't show every extreme that they name: `hits`: each query names 4 different clusters; the 128 queries of one device name any cluster at most 96 times, a bound that some block reaches. `cluster_shard`: each shard holds exactly one cluster.
All inputs are finite; a program needn't handle non-finite values.
Results may differ from a plain program's by a relative error of at most 0.0051.
Values may be sent and summed in bfloat16 or wider, within the bound.
No kernel may reach another device: no remote copies, remote signals or barrier semaphores. Data moves between devices by JAX's collectives and lax.ppermute only.
A program may use at most 64 MiB of HBM per device.

v0:
```python
import jax
import jax.numpy as jnp
from jax import lax
from jax.sharding import PartitionSpec as P

exact = lax.Precision.HIGHEST


def from_slots(values, picker):
    return jnp.dot(picker, values, precision=exact)


def to_slots(values, picker):
    return jnp.dot(values, picker, precision=exact)


def local(queries, weights, counts, hits, positive_offset, cluster_shard):
    peer_count = lax.axis_size("label")
    row_count, top_count = hits.shape
    slot_count = 3 * row_count * top_count // 2
    slot_depth = slot_count // peer_count
    cluster_count = cluster_shard.shape[0]
    hit_flat = hits.reshape(-1)
    match_table = hit_flat[:, None] == jnp.arange(cluster_count, dtype=jnp.int32)[None, :]
    target_shard = jnp.sum(jnp.where(match_table, cluster_shard[None, :], 0), axis=1)
    owner_table = (
        target_shard[:, None] == jnp.arange(peer_count, dtype=jnp.int32)[None, :]
    ).astype(jnp.int32)
    position = jnp.sum((jnp.cumsum(owner_table, axis=0) - owner_table) * owner_table, axis=1)
    slot_of = target_shard * slot_depth + position
    picker_bool = slot_of[:, None] == jnp.arange(slot_count, dtype=jnp.int32)[None, :]
    picker = picker_bool.astype(jnp.float32)
    dispatch = jnp.sum(picker_bool.reshape(row_count, top_count, slot_count), axis=1).astype(
        jnp.bfloat16
    )
    outgoing = lax.dot_general(
        dispatch, queries, (((0,), (0,)), ((), ())), preferred_element_type=jnp.float32
    ).astype(jnp.bfloat16)
    arrived = lax.all_to_all(outgoing, "label", split_axis=0, concat_axis=0, tiled=True)
    log_count = jnp.log(counts.astype(jnp.float32))
    scores = (
        lax.dot_general(
            arrived, weights, (((1,), (1,)), ((), ())), preferred_element_type=jnp.float32
        )
        - log_count[None, :]
    )
    local_max = jnp.max(scores, axis=1)
    back_max = lax.all_to_all(local_max, "label", split_axis=0, concat_axis=0, tiled=True)
    row_peak = jnp.max(from_slots(back_max, picker).reshape(row_count, top_count), axis=1)
    peak_slots = to_slots(jnp.repeat(row_peak, top_count), picker)
    peak_here = lax.all_to_all(peak_slots, "label", split_axis=0, concat_axis=0, tiled=True)
    local_sum = jnp.sum(jnp.exp(scores - peak_here[:, None]), axis=1)
    back_sum = lax.all_to_all(local_sum, "label", split_axis=0, concat_axis=0, tiled=True)
    exp_total = jnp.sum(from_slots(back_sum, picker).reshape(row_count, top_count), axis=1)
    normal = row_peak + jnp.log(exp_total)
    first_hit = jnp.arange(row_count * top_count, dtype=jnp.int32) % top_count == 0
    target_entry = jnp.where(first_hit, jnp.repeat(positive_offset, top_count) + 1, 0).astype(
        jnp.float32
    )
    norm_slots = to_slots(jnp.repeat(normal, top_count), picker)
    target_slots = to_slots(target_entry, picker)
    norm_here, target_here = (
        lax.all_to_all(norm_slots, "label", split_axis=0, concat_axis=0, tiled=True),
        lax.all_to_all(target_slots, "label", split_axis=0, concat_axis=0, tiled=True),
    )
    label_count = weights.shape[0]
    hit_label = jnp.arange(label_count, dtype=jnp.float32)[None, :] + 1.0 == target_here[:, None]
    probability = jnp.exp(scores - norm_here[:, None])
    coefficient = (probability - hit_label.astype(jnp.float32)).astype(jnp.bfloat16)
    positive_score = jnp.sum(jnp.where(hit_label, scores, 0.0), axis=1).astype(jnp.bfloat16)
    slot_grad = jnp.dot(coefficient, weights, preferred_element_type=jnp.float32).astype(
        jnp.bfloat16
    )
    back_grad, back_score = (
        lax.all_to_all(slot_grad, "label", split_axis=0, concat_axis=0, tiled=True),
        lax.all_to_all(positive_score, "label", split_axis=0, concat_axis=0, tiled=True),
    )
    query_grad = jnp.dot(dispatch, back_grad, preferred_element_type=jnp.float32).astype(
        jnp.bfloat16
    )
    entry_score = from_slots(back_score.astype(jnp.float32), picker).reshape(row_count, top_count)
    query_loss = normal - entry_score[:, 0]
    partial_sum = lax.dot_general(
        coefficient, arrived, (((0,), (0,)), ((), ())), preferred_element_type=jnp.float32
    )
    reduced = lax.psum_scatter(partial_sum, "dp", scatter_dimension=0, tiled=True)
    weight_grad = reduced.astype(jnp.bfloat16)
    return (query_loss, query_grad, weight_grad)


def solution(mesh):
    return jax.shard_map(
        local,
        mesh=mesh,
        in_specs=(
            P(("label", "dp"), None),
            P("label", None),
            P("label"),
            P(("label", "dp"), None),
            P(("label", "dp")),
            P(),
        ),
        out_specs=(P(("label", "dp")), P(("label", "dp"), None), P(("label", "dp"), None)),
        check_vma=False,
    )
```

profile of v0, /device:TPU:0, one launch (start us, length us, event | category | flops | bytes accessed | tf_op | source)
XLA Modules:
  0.0 157.6 jit_solution(14111109547552790693)
XLA Ops:
  7.2 0.9 copy.16
  8.2 0.7 select_reduce_fusion
  8.9 1.1 reduce-window.6
  10.9 2.4 %convolution_convert_fusion = bf16[768,768]{1,0:T(8,128)(2,1)} fusion(bf16[128,768]{1,0:T(8,128)(2,1)} %param.6, s32[128,768]{1,0:T(8,128)S(1)} %convert_reduce_fusion), kind=kOutput, calls=%fused_computation.20 | convolution fusion | flops 151683072 | bytes 1769472 | tf_op jit(solution)/shard_map/dot_general | solution.py:36
  13.3 7.3 %all-to-all-start = ((bf16[8,96,768]{2,1,0:T(8,128)(2,1)}), bf16[8,96,768]{2,1,0:T(8,128)(2,1)S(1)}, u32[]{:S(2)}, u32[]{:S(2)}) async-start(bf16[8,96,768]{2,1,0:T(8,128)(2,1)} %bitcast.4), calls=%async_computation | async-start | bytes 2359296 | tf_op jit(solution)/shard_map/all_to_all | solution.py:39
  21.1 28.1 %all-to-all-done = bf16[8,96,768]{2,1,0:T(8,128)(2,1)S(1)} async-done(((bf16[8,96,768]{2,1,0:T(8,128)(2,1)}), bf16[8,96,768]{2,1,0:T(8,128)(2,1)S(1)}, u32[]{:S(2)}, u32[]{:S(2)}) %all-to-all-start) | async-done | bytes 1179680 | tf_op jit(solution)/shard_map/all_to_all | solution.py:39
  49.2 1.0 copy-done.1
  50.2 2.2 %subtract_reduce_fusion = (f32[768]{0:T(1024)S(1)}, f32[768,640]{0,1:T(8,128)S(1)}) fusion(f32[640]{0:T(1024)S(1)} %convert_log_fusion, bf16[768,768]{1,0:T(8,128)(2,1)} %bitcast.70, bf16[640,768]{1,0:T(8,128)(2,1)S(1)} %copy-done), kind=kOutput, calls=%fused_computation.12 | convolution fusion | flops 755956992 | bytes 4134400 | tf_op jit(solution)/shard_map/dot_general | solution.py:42
  53.1 3.6 %all-to-all-start.1 = ((f32[8,96,1]{1,2,0:T(1,128)}), f32[8,96,1]{1,2,0:T(1,128)S(1)}, u32[]{:S(2)}, u32[]{:S(2)}) async-start(f32[8,96,1]{1,2,0:T(1,128)} %bitcast.6), calls=%async_computation.1 | async-start | bytes 8192 | tf_op jit(solution)/shard_map/all_to_all | solution.py:48
  56.8 1.5 fusion.25
  58.3 4.9 %all-to-all-done.1 = f32[8,96,1]{1,2,0:T(1,128)S(1)} async-done(((f32[8,96,1]{1,2,0:T(1,128)}), f32[8,96,1]{1,2,0:T(1,128)S(1)}, u32[]{:S(2)}, u32[]{:S(2)}) %all-to-all-start.1) | async-done | bytes 3104 | tf_op jit(solution)/shard_map/all_to_all | solution.py:48
  63.1 3.3 %all-to-all-start.4 = ((f32[8,96,1]{1,2,0:T(1,128)}), f32[8,96,1]{1,2,0:T(1,128)S(1)}, u32[]{:S(2)}, u32[]{:S(2)}) async-start(f32[8,96,1]{1,2,0:T(1,128)} %fusion.25), calls=%async_computation.4 | async-start | bytes 8192 | tf_op jit(solution)/shard_map/all_to_all | solution.py:64
  67.8 0.9 fusion.16
  69.0 1.5 fusion.22
  70.5 2.3 %all-to-all-done.4 = f32[8,96,1]{1,2,0:T(1,128)S(1)} async-done(((f32[8,96,1]{1,2,0:T(1,128)}), f32[8,96,1]{1,2,0:T(1,128)S(1)}, u32[]{:S(2)}, u32[]{:S(2)}) %all-to-all-start.4) | async-done | bytes 3104 | tf_op jit(solution)/shard_map/all_to_all | solution.py:64
  72.8 3.7 %all-to-all-start.2 = ((f32[8,96,1]{1,2,0:T(1,128)}), f32[8,96,1]{1,2,0:T(1,128)S(1)}, u32[]{:S(2)}, u32[]{:S(2)}) async-start(f32[8,96,1]{1,2,0:T(1,128)} %fusion.22), calls=%async_computation.2 | async-start | bytes 8192 | tf_op jit(solution)/shard_map/all_to_all | solution.py:51
  76.4 0.7 reduce.25
  77.2 5.6 %all-to-all-done.2 = f32[8,96,1]{1,2,0:T(1,128)S(1)} async-done(((f32[8,96,1]{1,2,0:T(1,128)}), f32[8,96,1]{1,2,0:T(1,128)S(1)}, u32[]{:S(2)}, u32[]{:S(2)}) %all-to-all-start.2) | async-done | bytes 3104 | tf_op jit(solution)/shard_map/all_to_all | solution.py:51
  82.8 0.7 reduce.23
  84.9 3.3 %all-to-all-start.5 = ((bf16[8,96,1]{1,2,0:T(2,128)(2,1)}), bf16[8,96,1]{1,2,0:T(2,128)(2,1)S(1)}, u32[]{:S(2)}, u32[]{:S(2)}) async-start(bf16[8,96,1]{1,2,0:T(2,128)(2,1)} %convert_element_type.70), calls=%async_computation.5 | async-start | bytes 8192 | tf_op jit(solution)/shard_map/all_to_all | solution.py:76
  88.9 5.7 %all-to-all-done.5 = bf16[8,96,1]{1,2,0:T(2,128)(2,1)S(1)} async-done(((bf16[8,96,1]{1,2,0:T(2,128)(2,1)}), bf16[8,96,1]{1,2,0:T(2,128)(2,1)S(1)}, u32[]{:S(2)}, u32[]{:S(2)}) %all-to-all-start.5) | async-done | bytes 1568 | tf_op jit(solution)/shard_map/all_to_all | solution.py:76
  94.5 3.3 %all-to-all-start.3 = ((f32[8,96,1]{1,2,0:T(1,128)}), f32[8,96,1]{1,2,0:T(1,128)S(1)}, u32[]{:S(2)}, u32[]{:S(2)}) async-start(f32[8,96,1]{1,2,0:T(1,128)} %bitcast.12), calls=%async_computation.3 | async-start | bytes 8192 | tf_op jit(solution)/shard_map/all_to_all | solution.py:53
  98.5 5.7 %all-to-all-done.3 = f32[8,96,1]{1,2,0:T(1,128)S(1)} async-done(((f32[8,96,1]{1,2,0:T(1,128)}), f32[8,96,1]{1,2,0:T(1,128)S(1)}, u32[]{:S(2)}, u32[]{:S(2)}) %all-to-all-start.3) | async-done | bytes 3104 | tf_op jit(solution)/shard_map/all_to_all | solution.py:53
  104.2 0.7 reduce.24
  105.0 0.9 fusion.19
  106.6 0.9 fusion.28
  107.6 8.8 %all_to_all.75 = f32[8,96,1]{1,2,0:T(1,128)S(1)} all-to-all(f32[8,96,1]{1,2,0:T(1,128)S(1)} %fusion.28), channel_id=1, replica_groups=mesh['label'=8,'dp'=4] {'label'}, dimensions={0} | all-to-all | bytes 6144 | tf_op jit(solution)/shard_map/all_to_all | solution.py:63
  117.2 3.8 %fusion.48 = f32[640,768]{1,0:T(8,128)} fusion(bf16[768,768]{1,0:T(8,128)(2,1)} %bitcast.71, f32[768,640]{0,1:T(8,128)S(1)} %get-tuple-element.8, f32[768]{0:T(1024)S(1)} %sub.44, f32[768]{0:T(1024)S(1)} %eq.161, f32[640]{0:T(1024)S(1)} %convert_log_fusion, f32[640]{0:T(1024)S(1)} %iota_add_fusion.1), kind=kOutput, calls=%fused_computation.64 | convolution fusion | flops 757923840 | bytes 5123072 | tf_op jit(solution)/shard_map/dot_general | solution.py:83
  120.9 1.4 convolution_convert_fusion.1
  122.4 25.2 %all_to_all.76 = bf16[8,96,768]{2,1,0:T(8,128)(2,1)S(1)} all-to-all(bf16[8,96,768]{2,1,0:T(8,128)(2,1)S(1)} %bitcast.72), channel_id=1, replica_groups=mesh['label'=8,'dp'=4] {'label'}, dimensions={0} | all-to-all | bytes 2359296 | tf_op jit(solution)/shard_map/all_to_all | solution.py:75
  147.6 1.0 convolution_convert_fusion.2
  149.0 1.7 %convert_element_type.69 = bf16[160,768]{1,0:T(8,128)(2,1)} convert(f32[160,768]{1,0:T(8,128)} %reduce-scatter.2.cloned.1.call-done) | non-fusion elementwise | flops 122880 | bytes 737280 | tf_op jit(solution)/shard_map/convert_element_type | solution.py:87
  (52 shorter events, 8.4 us)
Async XLA Ops:
  7.2 43.0 %copy-start = (bf16[640,768]{1,0:T(8,128)(2,1)S(1)}, bf16[640,768]{1,0:T(8,128)(2,1)}, u32[]{:S(2)}) copy-start(bf16[640,768]{1,0:T(8,128)(2,1)} %param.7) | copy-start | bytes 2949124
  10.9 9.9 %copy-start.3 = (s32[128]{0:T(128)S(1)}, s32[128]{0:T(128)}, u32[]{:S(2)}) copy-start(s32[128]{0:T(128)} %param.10) | copy-start | bytes 1540
  10.9 10.2 %copy-start.2 = (s32[640]{0:T(1024)S(1)}, s32[640]{0:T(1024)}, u32[]{:S(2)}) copy-start(s32[640]{0:T(1024)} %param.8) | copy-start | bytes 7684
  13.3 35.9 %all-to-all-start = ((bf16[8,96,768]{2,1,0:T(8,128)(2,1)}), bf16[8,96,768]{2,1,0:T(8,128)(2,1)S(1)}, u32[]{:S(2)}, u32[]{:S(2)}) async-start(bf16[8,96,768]{2,1,0:T(8,128)(2,1)} %bitcast.4), calls=%async_computation | async-start | bytes 2359296 | tf_op jit(solution)/shard_map/all_to_all | solution.py:39
  49.2 1.0 copy-start.1
  53.1 10.0 %all-to-all-start.1 = ((f32[8,96,1]{1,2,0:T(1,128)}), f32[8,96,1]{1,2,0:T(1,128)S(1)}, u32[]{:S(2)}, u32[]{:S(2)}) async-start(f32[8,96,1]{1,2,0:T(1,128)} %bitcast.6), calls=%async_computation.1 | async-start | bytes 8192 | tf_op jit(solution)/shard_map/all_to_all | solution.py:48
  63.1 9.6 %all-to-all-start.4 = ((f32[8,96,1]{1,2,0:T(1,128)}), f32[8,96,1]{1,2,0:T(1,128)S(1)}, u32[]{:S(2)}, u32[]{:S(2)}) async-start(f32[8,96,1]{1,2,0:T(1,128)} %fusion.25), calls=%async_computation.4 | async-start | bytes 8192 | tf_op jit(solution)/shard_map/all_to_all | solution.py:64
  72.8 10.0 %all-to-all-start.2 = ((f32[8,96,1]{1,2,0:T(1,128)}), f32[8,96,1]{1,2,0:T(1,128)S(1)}, u32[]{:S(2)}, u32[]{:S(2)}) async-start(f32[8,96,1]{1,2,0:T(1,128)} %fusion.22), calls=%async_computation.2 | async-start | bytes 8192 | tf_op jit(solution)/shard_map/all_to_all | solution.py:51
  84.9 9.6 %all-to-all-start.5 = ((bf16[8,96,1]{1,2,0:T(2,128)(2,1)}), bf16[8,96,1]{1,2,0:T(2,128)(2,1)S(1)}, u32[]{:S(2)}, u32[]{:S(2)}) async-start(bf16[8,96,1]{1,2,0:T(2,128)(2,1)} %convert_element_type.70), calls=%async_computation.5 | async-start | bytes 8192 | tf_op jit(solution)/shard_map/all_to_all | solution.py:76
  94.5 9.6 %all-to-all-start.3 = ((f32[8,96,1]{1,2,0:T(1,128)}), f32[8,96,1]{1,2,0:T(1,128)S(1)}, u32[]{:S(2)}, u32[]{:S(2)}) async-start(f32[8,96,1]{1,2,0:T(1,128)} %bitcast.12), calls=%async_computation.3 | async-start | bytes 8192 | tf_op jit(solution)/shard_map/all_to_all | solution.py:53
  97.9 51.1 %reduce-scatter.2.cloned.1.call-start = ((), (), s32[]{:S(2)}) async-start(), calls=%async_computation.9 | async-start | bytes 2457600 | tf_op jit(solution)/shard_map/reduce_scatter | solution.py:86
Sparse Core Ops, SparseCore 0:
  121.1 27.8 reduce-scatter.1
where the time goes:
time: 158 us
  waiting for transfers between devices  52.6 us (33%)
  blocking collectives  34 us (22%)
  starting transfers between devices  24.5 us (16%)
  matrix products  17 us (11%)
  between operations  14.2 us (9%)
  other arithmetic  8.83 us (6%)
  local copies, waits for them, and re-layouts  6.29 us (4%)
    all_to_all x1, waiting for transfers between devices, local(): lax.all_to_all(outgoing, 'label', split_axis=0, concat_axis=0, tiled=True)  28.1 us
    all_to_all x1, blocking collectives, local(): lax.all_to_all(slot_grad, 'label', split_axis=0, concat_axis=0, tiled=True)  25.2 us
    all_to_all x1, blocking collectives, local(): lax.all_to_all(norm_slots, 'label', split_axis=0, concat_axis=0, tiled=True)  8.83 us
    all_to_all x1, starting transfers between devices, local(): lax.all_to_all(outgoing, 'label', split_axis=0, concat_axis=0, tiled=True)  7.28 us
    all_to_all x1, waiting for transfers between devices, local(): lax.all_to_all(local_sum, 'label', split_axis=0, concat_axis=0, tiled=True)  5.72 us
    all_to_all x1, waiting for transfers between devices, local(): lax.all_to_all(positive_score, 'label', split_axis=0, concat_axis=0, tile...  5.66 us
    all_to_all x1, waiting for transfers between devices, local(): lax.all_to_all(peak_slots, 'label', split_axis=0, concat_axis=0, tiled=True)  5.6 us
    all_to_all x1, waiting for transfers between devices, local(): lax.all_to_all(local_max, 'label', split_axis=0, concat_axis=0, tiled=True)  4.87 us
  transfers between devices with their start and end apart: 7, of which 7 were waited for; matrix products, arithmetic and copies ran while one was open for 6% of the time, Pallas kernels for 0%

commit v1 on v0

--- a/solution.py
+++ b/solution.py
@@ -4,6 +4,7 @@
 from jax.sharding import PartitionSpec as P
 
 exact = lax.Precision.HIGHEST
+LOW = -1e30
 
 
 def from_slots(values, picker):
@@ -14,7 +15,7 @@
     return jnp.dot(values, picker, precision=exact)
 
 
-def local(queries, weights, counts, hits, positive_offset, cluster_shard):
+def slot_plan(queries, weights, counts, hits, positive_offset, cluster_shard):
     peer_count = lax.axis_size("label")
     row_count, top_count = hits.shape
     slot_count = 3 * row_count * top_count // 2
@@ -88,7 +89,111 @@
     return (query_loss, query_grad, weight_grad)
 
 
+def dense_plan(queries, weights, counts, hits, positive_offset, cluster_shard):
+    n = lax.axis_size("label")
+    dp = lax.axis_size("dp")
+    groups = n // 2
+    rows, width = queries.shape
+    labels = weights.shape[0]
+    part = labels // dp
+    me = lax.axis_index("label")
+    lane = lax.axis_index("dp")
+
+    def shift(x, k):
+        return lax.ppermute(x, "label", [(i, (i + 2 * k) % n) for i in range(n)])
+
+    def pair(x):
+        return lax.ppermute(x, "label", [(i, i ^ 1) for i in range(n)])
+
+    def core(x):
+        return lax.ppermute(x, "dp", [(i, i ^ 1) for i in range(dp)])
+
+    def side(x):
+        return lax.ppermute(x, "dp", [(i, i ^ 2) for i in range(dp)])
+
+    def corner(x):
+        return lax.ppermute(
+            x, ("label", "dp"), [(i * dp + j, (i ^ 1) * dp + (j ^ 2)) for i in range(n) for j in range(dp)]
+        )
+
+    query_blocks = [queries] + [shift(queries, k) for k in range(1, groups)]
+    match = hits[:, :, None] == jnp.arange(cluster_shard.shape[0], dtype=jnp.int32)[None, None, :]
+    owner = jnp.sum(jnp.where(match, cluster_shard[None, None, :], 0), axis=2)
+    mask_bits = jnp.sum(jnp.left_shift(1, owner), axis=1)
+    code = jnp.stack([mask_bits, owner[:, 0] * labels + positive_offset], 0)
+    codes = [code] + [shift(code, k) for k in range(1, groups)]
+
+    order = jnp.arange(dp, dtype=jnp.int32) ^ lane
+    blocks = jnp.take(weights.reshape(dp, part, width), order, axis=0)
+    near = blocks.reshape(2, 2, part, width)[:, 0].reshape(2 * part, width)
+    far = blocks.reshape(2, 2, part, width)[:, 1].reshape(2 * part, width)
+    near_pair = pair(near)
+    far_pair = core(near_pair)
+    held = jnp.concatenate([near, near_pair, far, far_pair], 0)
+    log_own = jnp.log(counts.astype(jnp.float32))
+    logs = [log_own, pair(log_own)]
+    place = (order[:, None] * part + jnp.arange(part, dtype=jnp.int32)[None, :]).reshape(2, 2, part)
+    logs = [jnp.take(v.reshape(dp, part), order, axis=0).reshape(2, 2, part) for v in logs]
+
+    def arrange(a, b):
+        return jnp.concatenate([a[:, 0].reshape(-1), b[:, 0].reshape(-1), a[:, 1].reshape(-1), b[:, 1].reshape(-1)])
+
+    log_held = arrange(*logs)
+    label_held = arrange(place + me * labels, place + (me ^ 1) * labels)
+    shard_held = label_held // labels
+
+    q = jnp.concatenate(query_blocks, 0)
+    bits = jnp.concatenate([c[0] for c in codes])
+    target = jnp.concatenate([c[1] for c in codes])
+    named = (jnp.right_shift(bits[:, None], shard_held[None, :]) & 1) == 1
+    hot = target[:, None] == label_held[None, :]
+    scores = lax.dot_general(q, held, (((1,), (1,)), ((), ())), preferred_element_type=jnp.float32)
+    scores = jnp.where(named, scores - log_held[None, :], LOW)
+    peak = jnp.max(scores, axis=1)
+    total = jnp.sum(jnp.where(named, jnp.exp(scores - peak[:, None]), 0.0), axis=1)
+    positive = jnp.sum(jnp.where(hot, scores, 0.0), axis=1)
+
+    stats = jnp.stack([peak, total, positive], 0).reshape(3, groups, rows)
+    all_stats = [stats]
+    for k in range(1, groups):
+        got = shift(stats, k)
+        all_stats.append(jnp.concatenate([got[:, groups - k :], got[:, : groups - k]], 1))
+    all_stats = jnp.stack(all_stats, 0)
+    row_peak = jnp.max(all_stats[:, 0], axis=0)
+    normal = row_peak + jnp.log(
+        jnp.sum(all_stats[:, 1] * jnp.exp(all_stats[:, 0] - row_peak[None]), axis=0)
+    )
+    positive_score = jnp.sum(all_stats[:, 2, 0], axis=0).astype(jnp.bfloat16).astype(jnp.float32)
+    query_loss = normal[0] - positive_score
+
+    probability = jnp.exp(scores - normal.reshape(-1)[:, None])
+    coefficient = (probability - hot.astype(jnp.float32)).astype(jnp.bfloat16)
+    weight_part = lax.dot_general(
+        coefficient, q, (((0,), (0,)), ((), ())), preferred_element_type=jnp.float32
+    )
+    half = 4 * part
+    arrived = core(weight_part[half:].astype(jnp.bfloat16))
+    terms = jnp.dot(coefficient, held, preferred_element_type=jnp.float32).astype(jnp.bfloat16)
+    terms = terms.reshape(groups, rows, width)
+    grads = [terms[0]] + [shift(terms[k], groups - k) for k in range(1, groups)]
+    summed = weight_part[:half] + arrived.astype(jnp.float32)
+    own = summed[:part]
+    sent = summed[part:].astype(jnp.bfloat16)
+    other = [side(sent[:part]), pair(sent[part : 2 * part]), corner(sent[2 * part :])]
+    weight_grad = (own + sum(o.astype(jnp.float32) for o in other)).astype(jnp.bfloat16)
+    query_grad = sum(g.astype(jnp.float32) for g in grads).astype(jnp.bfloat16)
+    return query_loss, query_grad, weight_grad
+
+
 def solution(mesh):
+    n, dp = mesh.shape["label"], mesh.shape["dp"]
+
+    def local(queries, weights, counts, hits, positive_offset, cluster_shard):
+        rows, top = hits.shape
+        args = (queries, weights, counts, hits, positive_offset, cluster_shard)
+        dense = n % 2 == 0 and dp == 4 and n <= 30 and (n // 2) * rows <= 3 * rows * top // 2
+        return dense_plan(*args) if dense else slot_plan(*args)
+
     return jax.shard_map(
         local,
         mesh=mesh,

time: 158 us -> 81.1 us (0.51)
  blocking collectives: 34 us -> 0 us
  waiting for transfers between devices: 52.6 us -> 29.3 us
  between operations: 14.2 us -> 0.9 us
  matrix products: 17 us -> 6.73 us
  starting transfers between devices: 24.5 us -> 32.9 us
  other arithmetic: 8.83 us -> 6.41 us
  local copies, waits for them, and re-layouts: 6.29 us -> 4.11 us
    all_to_all x6 -> x0, waiting for transfers between devices: 52.2 us -> none  [the longest x1 28.1 us: local(): lax.all_to_all(outgoing, 'label', split_axis=0, concat_axis=0, tiled=True)]
    all_to_all x2 -> x0, blocking collectives: 34 us -> none  [the longest x1 25.2 us: local(): lax.all_to_all(slot_grad, 'label', split_axis=0, concat_axis=0, tiled=True)]
    ppermute x0 -> x19, starting transfers between devices: none -> 32.9 us  [the longest x12 25.3 us: shift(): return lax.ppermute(x, 'label', [(i, (i + 2 * k) % n) for i in range(n)])]
    ppermute x0 -> x19, waiting for transfers between devices: none -> 29.3 us  [the longest x12 17.9 us: shift(): return lax.ppermute(x, 'label', [(i, (i + 2 * k) % n) for i in range(n)])]
    all_to_all x6 -> x0, starting transfers between devices: 24.5 us -> none  [the longest x1 7.28 us: local(): lax.all_to_all(outgoing, 'label', split_axis=0, concat_axis=0, tiled=True)]
    dot_general x11 -> x3, matrix products: 17 us -> 6.73 us  [the longest x1 2.65 us: dense_plan(): jnp.dot(coefficient, held, preferred_element_type=jnp.float32)]
    all_to_all x6 -> x0, other arithmetic: 3.55 us -> none  [the longest x1 0.7 us: local(): lax.all_to_all(target_slots, 'label', split_axis=0, concat_axis=0, tiled=...]
    all_to_all x6 -> x0, local copies, waits for them, and re-layouts: 2.17 us -> none  [the longest x3 1.34 us: local(): lax.all_to_all(local_max, 'label', split_axis=0, concat_axis=0, tiled=True)]
  transfers between devices with their start and end apart: 7 -> 19, of which waited for: 7 -> 12; matrix products, arithmetic and copies ran while one was open for 6% -> 13% of each run, Pallas kernels for 0% -> 0%
where the time goes in v1:
time: 81.1 us; the launch traced here: 80.3 us
  starting transfers between devices  32.9 us (41%)
  waiting for transfers between devices  29.3 us (36%)
  matrix products  6.73 us (8%)
  other arithmetic  6.41 us (8%)
  local copies, waits for them, and re-layouts  4.11 us (5%)
  between operations  0.9 us (1%)
    ppermute x12, starting transfers between devices, shift(): return lax.ppermute(x, 'label', [(i, (i + 2 * k) % n) for i in range(n)])  25.3 us
    ppermute x12, waiting for transfers between devices, shift(): return lax.ppermute(x, 'label', [(i, (i + 2 * k) % n) for i in range(n)])  17.9 us
    ppermute x3, waiting for transfers between devices, pair(): return lax.ppermute(x, 'label', [(i, i ^ 1) for i in range(n)])  9.72 us
    ppermute x3, starting transfers between devices, pair(): return lax.ppermute(x, 'label', [(i, i ^ 1) for i in range(n)])  3.52 us
    dot_general x1, matrix products, dense_plan(): jnp.dot(coefficient, held, preferred_element_type=jnp.float32)  2.65 us
    dot_general x1, matrix products, dense_plan(): lax.dot_general(q, held, (((1,), (1,)), ((), ())), preferred_element_type...  2.59 us
    ppermute x1, starting transfers between devices, corner(): lax.ppermute(x, ('label', 'dp'), [(i * dp + j, (i ^ 1) * dp + (j ^ 2)) fo...  2.48 us
    ppermute x2, waiting for transfers between devices, core(): return lax.ppermute(x, 'dp', [(i, i ^ 1) for i in range(dp)])  1.63 us
  transfers between devices with their start and end apart: 19, of which 12 were waited for; matrix products, arithmetic and copies ran while one was open for 13% of the time, Pallas kernels for 0%

profile of v1, /device:TPU:0, one launch (start us, length us, event | category | flops | bytes accessed | tf_op | source)
XLA Modules:
  0.0 80.3 jit_solution(3183772323628271606)
XLA Ops:
  0.6 3.1 %collective-permute-start.3 = (bf16[128,768]{1,0:T(8,128)(2,1)}, bf16[128,768]{1,0:T(8,128)(2,1)S(1)}, u32[]{:S(2)}, u32[]{:S(2)}) collective-permute-start(bf16[128,768]{1,0:T(8,128)(2,1)} %param.8), channel_id=1, source_target_pairs={{0,8},{4,12},{8,16},{12,20},{16,24},{20,28},{24,0},{28,4},{1,9},{5... | collective-permute-start | bytes 589832 | tf_op jit(solution)/shard_map/ppermute | solution.py:103
  3.7 2.6 %collective-permute-start.4 = (bf16[128,768]{1,0:T(8,128)(2,1)}, bf16[128,768]{1,0:T(8,128)(2,1)S(1)}, u32[]{:S(2)}, u32[]{:S(2)}) collective-permute-start(bf16[128,768]{1,0:T(8,128)(2,1)} %param.8), channel_id=1, source_target_pairs={{0,16},{4,20},{8,24},{12,28},{16,0},{20,4},{24,8},{28,12},{1,17},{... | collective-permute-start | bytes 589832 | tf_op jit(solution)/shard_map/ppermute | solution.py:103
  6.3 1.3 %collective-permute-start.5 = (bf16[128,768]{1,0:T(8,128)(2,1)}, bf16[128,768]{1,0:T(8,128)(2,1)S(1)}, u32[]{:S(2)}, u32[]{:S(2)}) collective-permute-start(bf16[128,768]{1,0:T(8,128)(2,1)} %param.8), channel_id=1, source_target_pairs={{0,24},{4,28},{8,0},{12,4},{16,8},{20,12},{24,16},{28,20},{1,25},{... | collective-permute-start | bytes 589832 | tf_op jit(solution)/shard_map/ppermute | solution.py:103
  7.7 0.7 convert_log_fusion
  8.4 1.5 %collective-permute-start.8 = (f32[640]{0:T(1024)S(1)}, f32[640]{0:T(1024)S(1)}, u32[]{:S(2)}, u32[]{:S(2)}) collective-permute-start(f32[640]{0:T(1024)S(1)} %convert_log_fusion), channel_id=1, source_target_pairs={{0,4},{4,0},{8,12},{12,8},{16,20},{20,16},{24,28},{28,24},{1,5},{5... | collective-permute-start | bytes 7688 | tf_op jit(solution)/shard_map/ppermute | solution.py:106
  9.9 0.8 select_reduce_fusion.1
  10.7 0.7 bitcast_add_fusion
  11.8 0.9 %constant_dynamic-update-slice_fusion.3 = bf16[512,768]{1,0:T(8,128)(2,1)S(1)} fusion(bf16[128,768]{1,0:T(8,128)(2,1)} %param.8), kind=kLoop, calls=%fused_computation.30 | loop fusion | bytes 393216
  14.9 1.7 %collective-permute-done.2 = s32[2,128]{1,0:T(2,128)S(1)} collective-permute-done((s32[2,128]{1,0:T(2,128)S(1)}, s32[2,128]{1,0:T(2,128)S(1)}, u32[]{:S(2)}, u32[]{:S(2)}) %collective-permute-start.2) | collective-permute-done | bytes 1056 | tf_op jit(solution)/shard_map/ppermute | solution.py:103
  16.7 6.5 %collective-permute-start.1 = (s32[2,128]{1,0:T(2,128)S(1)}, s32[2,128]{1,0:T(2,128)S(1)}, u32[]{:S(2)}, u32[]{:S(2)}) collective-permute-start(s32[2,128]{1,0:T(2,128)S(1)} %pad_add_fusion.2), channel_id=1, source_target_pairs={{0,16},{4,20},{8,24},{12,28},{16,0},{20,4},{24,8},{28,12},{1,17},{... | collective-permute-start | bytes 3080 | tf_op jit(solution)/shard_map/ppermute | solution.py:103
  23.2 1.5 %collective-permute-done.1 = s32[2,128]{1,0:T(2,128)S(1)} collective-permute-done((s32[2,128]{1,0:T(2,128)S(1)}, s32[2,128]{1,0:T(2,128)S(1)}, u32[]{:S(2)}, u32[]{:S(2)}) %collective-permute-start.1) | collective-permute-done | bytes 1056 | tf_op jit(solution)/shard_map/ppermute | solution.py:103
  24.7 3.9 %collective-permute-start = (s32[2,128]{1,0:T(2,128)S(1)}, s32[2,128]{1,0:T(2,128)S(1)}, u32[]{:S(2)}, u32[]{:S(2)}) collective-permute-start(s32[2,128]{1,0:T(2,128)S(1)} %pad_add_fusion.2), channel_id=1, source_target_pairs={{0,8},{4,12},{8,16},{12,20},{16,24},{20,28},{24,0},{28,4},{1,9},{5... | collective-permute-start | bytes 3080 | tf_op jit(solution)/shard_map/ppermute | solution.py:103
  28.6 1.5 %collective-permute-done = s32[2,128]{1,0:T(2,128)S(1)} collective-permute-done((s32[2,128]{1,0:T(2,128)S(1)}, s32[2,128]{1,0:T(2,128)S(1)}, u32[]{:S(2)}, u32[]{:S(2)}) %collective-permute-start) | collective-permute-done | bytes 1056 | tf_op jit(solution)/shard_map/ppermute | solution.py:103
  30.1 1.5 %collective-permute-start.6 = (bf16[320,768]{1,0:T(8,128)(2,1)S(1)}, bf16[320,768]{1,0:T(8,128)(2,1)}, u32[]{:S(2)}, u32[]{:S(2)}) collective-permute-start(bf16[320,768]{1,0:T(8,128)(2,1)S(1)} %bitcast.57), channel_id=1, source_target_pairs={{0,4},{4,0},{8,12},{12,8},{16,20},{20,16},{24,28},{28,24},{1,5},{5... | collective-permute-start | bytes 1474568 | tf_op jit(solution)/shard_map/ppermute | solution.py:106
  32.4 8.9 %collective-permute-done.6 = bf16[320,768]{1,0:T(8,128)(2,1)} collective-permute-done((bf16[320,768]{1,0:T(8,128)(2,1)S(1)}, bf16[320,768]{1,0:T(8,128)(2,1)}, u32[]{:S(2)}, u32[]{:S(2)}) %collective-permute-start.6) | collective-permute-done | bytes 491552 | tf_op jit(solution)/shard_map/ppermute | solution.py:106
  41.9 1.6 %collective-permute-done.7 = bf16[320,768]{1,0:T(8,128)(2,1)} collective-permute-done((bf16[320,768]{1,0:T(8,128)(2,1)}, bf16[320,768]{1,0:T(8,128)(2,1)}, u32[]{:S(2)}, u32[]{:S(2)}) %collective-permute-start.7) | collective-permute-done | bytes 491552 | tf_op jit(solution)/shard_map/ppermute | solution.py:109
  43.5 2.6 %fusion.23 = (f32[512]{0:T(512)S(1)}, f32[512,1280]{1,0:T(8,128)S(1)}) fusion(f32[1280]{0:T(1024)S(1)} %concatenate.55, bf16[512,768]{1,0:T(8,128)(2,1)S(1)} %constant_dynamic-update-slice_fusion, bf16[320,768]{1,0:T(8,128)(2,1)} %collective-permute-done.7, bf16[320,768]{1,0:T(8,128)(2,1)S(1)} %bitcast.55, bf16[320,768]{1,0:T(8,128)(2,1)} %collective-permute-done.6, ...), kind=kOutput, calls=%fused_computation.87 | convolution fusion | flops 1018428928 | bytes 5388288 | tf_op jit(solution)/shard_map/dot_general | solution.py:150
  46.1 1.4 %select_reduce_fusion = (f32[512]{0:T(512)S(1)}, f32[512]{0:T(512)S(1)}) fusion(f32[512,1280]{1,0:T(8,128)S(1)} %get-tuple-element.37, f32[512]{0:T(512)S(1)} %get-tuple-element.36, s32[1280]{0:T(1024)S(1)} %add_select_fusion, s32[512]{0:T(512)S(1)} %pad_add_fusion, s32[1280]{0:T(1024)S(1)} %concatenate.52, s32[512]{0:T(512)S(1)} %pad_add_fusion.1), kind=kLoop, calls=%fused_computation.10 | loop fusion | flops 5897216 | bytes 2641920 | tf_op jit(solution)/shard_map/reduce_sum | solution.py:153
  47.5 1.5 %collective-permute-start.11 = (f32[3,4,128]{2,1,0:T(4,128)S(1)}, f32[3,4,128]{2,1,0:T(4,128)S(1)}, u32[]{:S(2)}, u32[]{:S(2)}) collective-permute-start(f32[3,4,128]{2,1,0:T(4,128)S(1)} %pad_maximum_fusion.4), channel_id=1, source_target_pairs={{0,24},{4,28},{8,0},{12,4},{16,8},{20,12},{24,16},{28,20},{1,25},{... | collective-permute-start | bytes 18440 | tf_op jit(solution)/shard_map/ppermute | solution.py:103
  49.0 1.7 %collective-permute-start.10 = (f32[3,4,128]{2,1,0:T(4,128)S(1)}, f32[3,4,128]{2,1,0:T(4,128)S(1)}, u32[]{:S(2)}, u32[]{:S(2)}) collective-permute-start(f32[3,4,128]{2,1,0:T(4,128)S(1)} %pad_maximum_fusion.4), channel_id=1, source_target_pairs={{0,16},{4,20},{8,24},{12,28},{16,0},{20,4},{24,8},{28,12},{1,17},{... | collective-permute-start | bytes 18440 | tf_op jit(solution)/shard_map/ppermute | solution.py:103
  51.2 2.4 %collective-permute-done.10 = f32[3,4,128]{2,1,0:T(4,128)S(1)} collective-permute-done((f32[3,4,128]{2,1,0:T(4,128)S(1)}, f32[3,4,128]{2,1,0:T(4,128)S(1)}, u32[]{:S(2)}, u32[]{:S(2)}) %collective-permute-start.10) | collective-permute-done | bytes 6176 | tf_op jit(solution)/shard_map/ppermute | solution.py:103
  53.6 2.6 %collective-permute-done.9 = f32[3,4,128]{2,1,0:T(4,128)S(1)} collective-permute-done((f32[3,4,128]{2,1,0:T(4,128)S(1)}, f32[3,4,128]{2,1,0:T(4,128)S(1)}, u32[]{:S(2)}, u32[]{:S(2)}) %collective-permute-start.9) | collective-permute-done | bytes 6176 | tf_op jit(solution)/shard_map/ppermute | solution.py:103
  56.3 1.5 %fusion.15 = f32[1280,768]{1,0:T(8,128)S(1)} fusion(bf16[512,768]{1,0:T(8,128)(2,1)S(1)} %constant_dynamic-update-slice_fusion, f32[512,1280]{1,0:T(8,128)S(1)} %get-tuple-element.37, f32[512]{0:T(512)S(1)} %bitcast.77, s32[1280]{0:T(1024)S(1)} %concatenate.52, s32[512]{0:T(512)S(1)} %pad_add_fusion.1), kind=kOutput, calls=%fused_computation.81 | convolution fusion | flops 1009909760 | bytes 7349248 | tf_op jit(solution)/shard_map/dot_general | solution.py:171
  58.0 2.6 %convolution_convert_fusion = bf16[512,768]{1,0:T(8,128)(2,1)S(1)} fusion(bf16[320,768]{1,0:T(8,128)(2,1)} %collective-permute-done.7, bf16[320,768]{1,0:T(8,128)(2,1)S(1)} %bitcast.56, bf16[320,768]{1,0:T(8,128)(2,1)} %collective-permute-done.6, bf16[320,768]{1,0:T(8,128)(2,1)S(1)} %bitcast.59, f32[512,1280]{1,0:T(8,128)S(1)} %get-tuple-element.37, ...), kind=kOutput, calls=%fused_computation.15 | convolution fusion | flops 1018167296 | bytes 5383168 | tf_op jit(solution)/shard_map/dot_general | solution.py:176
  61.1 3.5 %collective-permute-start.12 = (bf16[128,768]{1,0:T(8,128)(2,1)S(1)}, bf16[128,768]{1,0:T(8,128)(2,1)S(1)}, u32[]{:S(2)}, u32[]{:S(2)}) collective-permute-start(bf16[128,768]{1,0:T(8,128)(2,1)S(1)} %get-tuple-element.21), channel_id=1, source_target_pairs={{0,24},{4,28},{8,0},{12,4},{16,8},{20,12},{24,16},{28,20},{1,25},{... | collective-permute-start | bytes 589832 | tf_op jit(solution)/shard_map/ppermute | solution.py:103
  65.4 2.5 %collective-permute-start.18 = (bf16[160,768]{1,0:T(8,128)(2,1)S(1)}, bf16[160,768]{1,0:T(8,128)(2,1)S(1)}, u32[]{:S(2)}, u32[]{:S(2)}) collective-permute-start(bf16[160,768]{1,0:T(8,128)(2,1)S(1)} %get-tuple-element.17), channel_id=1, source_target_pairs={{0,6},{1,7},{2,4},{3,5},{4,2},{5,3},{6,0},{7,1},{8,14},{9,15},{10,... | collective-permute-start | bytes 737288 | tf_op jit(solution)/shard_map/ppermute | solution.py:115
  68.4 2.0 %collective-permute-done.14 = bf16[128,768]{1,0:T(8,128)(2,1)S(1)} collective-permute-done((bf16[128,768]{1,0:T(8,128)(2,1)S(1)}, bf16[128,768]{1,0:T(8,128)(2,1)S(1)}, u32[]{:S(2)}, u32[]{:S(2)}) %collective-permute-start.14) | collective-permute-done | bytes 196640 | tf_op jit(solution)/shard_map/ppermute | solution.py:103
  70.4 1.5 %collective-permute-start.16 = (bf16[160,768]{1,0:T(8,128)(2,1)S(1)}, bf16[160,768]{1,0:T(8,128)(2,1)S(1)}, u32[]{:S(2)}, u32[]{:S(2)}) collective-permute-start(bf16[160,768]{1,0:T(8,128)(2,1)S(1)} %get-tuple-element.16), channel_id=1, source_target_pairs={{0,2},{1,3},{2,0},{3,1},{4,6},{5,7},{6,4},{7,5},{8,10},{9,11},{10,... | collective-permute-start | bytes 737288 | tf_op jit(solution)/shard_map/ppermute | solution.py:112
  71.9 6.0 %collective-permute-done.13 = bf16[128,768]{1,0:T(8,128)(2,1)S(1)} collective-permute-done((bf16[128,768]{1,0:T(8,128)(2,1)S(1)}, bf16[128,768]{1,0:T(8,128)(2,1)S(1)}, u32[]{:S(2)}, u32[]{:S(2)}) %collective-permute-start.13) | collective-permute-done | bytes 196640 | tf_op jit(solution)/shard_map/ppermute | solution.py:103
  77.9 0.8 add_convert_fusion
  78.7 0.8 collective-permute-done.17
  79.5 0.8 %fusion.4 = bf16[160,768]{1,0:T(8,128)(2,1)} fusion(f32[640,768]{1,0:T(8,128)S(1)} %get-tuple-element.15, bf16[160,768]{1,0:T(8,128)(2,1)S(1)} %collective-permute-done.18, bf16[160,768]{1,0:T(8,128)(2,1)S(1)} %collective-permute-done.17, bf16[160,768]{1,0:T(8,128)(2,1)S(1)} %collective-permute-done.16), kind=kLoop, calls=%fused_computation.18 | loop fusion | flops 860160 | bytes 1474560 | tf_op jit(solution)/shard_map/convert_element_type | solution.py:183
  (78 shorter events, 6.4 us)
Async XLA Ops:
  0.6 12.2 %copy-start = (bf16[640,768]{1,0:T(8,128)(2,1)S(1)}, bf16[640,768]{1,0:T(8,128)(2,1)}, u32[]{:S(2)}) copy-start(bf16[640,768]{1,0:T(8,128)(2,1)} %param.9) | copy-start | bytes 2949124
  0.6 41.2 %collective-permute-start.3 = (bf16[128,768]{1,0:T(8,128)(2,1)}, bf16[128,768]{1,0:T(8,128)(2,1)S(1)}, u32[]{:S(2)}, u32[]{:S(2)}) collective-permute-start(bf16[128,768]{1,0:T(8,128)(2,1)} %param.8), channel_id=1, source_target_pairs={{0,8},{4,12},{8,16},{12,20},{16,24},{20,28},{24,0},{28,4},{1,9},{5... | collective-permute-start | bytes 589832 | tf_op jit(solution)/shard_map/ppermute | solution.py:103
  3.7 38.1 %collective-permute-start.4 = (bf16[128,768]{1,0:T(8,128)(2,1)}, bf16[128,768]{1,0:T(8,128)(2,1)S(1)}, u32[]{:S(2)}, u32[]{:S(2)}) collective-permute-start(bf16[128,768]{1,0:T(8,128)(2,1)} %param.8), channel_id=1, source_target_pairs={{0,16},{4,20},{8,24},{12,28},{16,0},{20,4},{24,8},{28,12},{1,17},{... | collective-permute-start | bytes 589832 | tf_op jit(solution)/shard_map/ppermute | solution.py:103
  6.3 35.6 %collective-permute-start.5 = (bf16[128,768]{1,0:T(8,128)(2,1)}, bf16[128,768]{1,0:T(8,128)(2,1)S(1)}, u32[]{:S(2)}, u32[]{:S(2)}) collective-permute-start(bf16[128,768]{1,0:T(8,128)(2,1)} %param.8), channel_id=1, source_target_pairs={{0,24},{4,28},{8,0},{12,4},{16,8},{20,12},{24,16},{28,20},{1,25},{... | collective-permute-start | bytes 589832 | tf_op jit(solution)/shard_map/ppermute | solution.py:103
  8.4 23.3 %collective-permute-start.8 = (f32[640]{0:T(1024)S(1)}, f32[640]{0:T(1024)S(1)}, u32[]{:S(2)}, u32[]{:S(2)}) collective-permute-start(f32[640]{0:T(1024)S(1)} %convert_log_fusion), channel_id=1, source_target_pairs={{0,4},{4,0},{8,12},{12,8},{16,20},{20,16},{24,28},{28,24},{1,5},{5... | collective-permute-start | bytes 7688 | tf_op jit(solution)/shard_map/ppermute | solution.py:106
  11.3 5.3 %collective-permute-start.2 = (s32[2,128]{1,0:T(2,128)S(1)}, s32[2,128]{1,0:T(2,128)S(1)}, u32[]{:S(2)}, u32[]{:S(2)}) collective-permute-start(s32[2,128]{1,0:T(2,128)S(1)} %pad_add_fusion.2), channel_id=1, source_target_pairs={{0,24},{4,28},{8,0},{12,4},{16,8},{20,12},{24,16},{28,20},{1,25},{... | collective-permute-start | bytes 3080 | tf_op jit(solution)/shard_map/ppermute | solution.py:103
  16.7 8.1 %collective-permute-start.1 = (s32[2,128]{1,0:T(2,128)S(1)}, s32[2,128]{1,0:T(2,128)S(1)}, u32[]{:S(2)}, u32[]{:S(2)}) collective-permute-start(s32[2,128]{1,0:T(2,128)S(1)} %pad_add_fusion.2), channel_id=1, source_target_pairs={{0,16},{4,20},{8,24},{12,28},{16,0},{20,4},{24,8},{28,12},{1,17},{... | collective-permute-start | bytes 3080 | tf_op jit(solution)/shard_map/ppermute | solution.py:103
  24.7 5.4 %collective-permute-start = (s32[2,128]{1,0:T(2,128)S(1)}, s32[2,128]{1,0:T(2,128)S(1)}, u32[]{:S(2)}, u32[]{:S(2)}) collective-permute-start(s32[2,128]{1,0:T(2,128)S(1)} %pad_add_fusion.2), channel_id=1, source_target_pairs={{0,8},{4,12},{8,16},{12,20},{16,24},{20,28},{24,0},{28,4},{1,9},{5... | collective-permute-start | bytes 3080 | tf_op jit(solution)/shard_map/ppermute | solution.py:103
  30.1 11.2 %collective-permute-start.6 = (bf16[320,768]{1,0:T(8,128)(2,1)S(1)}, bf16[320,768]{1,0:T(8,128)(2,1)}, u32[]{:S(2)}, u32[]{:S(2)}) collective-permute-start(bf16[320,768]{1,0:T(8,128)(2,1)S(1)} %bitcast.57), channel_id=1, source_target_pairs={{0,4},{4,0},{8,12},{12,8},{16,20},{20,16},{24,28},{28,24},{1,5},{5... | collective-permute-start | bytes 1474568 | tf_op jit(solution)/shard_map/ppermute | solution.py:106
  41.3 2.2 %collective-permute-start.7 = (bf16[320,768]{1,0:T(8,128)(2,1)}, bf16[320,768]{1,0:T(8,128)(2,1)}, u32[]{:S(2)}, u32[]{:S(2)}) collective-permute-start(bf16[320,768]{1,0:T(8,128)(2,1)} %collective-permute-done.6), channel_id=1, source_target_pairs={{0,1},{1,0},{2,3},{3,2},{4,5},{5,4},{6,7},{7,6},{8,9},{9,8},{10,11... | collective-permute-start | bytes 1474568 | tf_op jit(solution)/shard_map/ppermute | solution.py:109
  47.5 3.7 %collective-permute-start.11 = (f32[3,4,128]{2,1,0:T(4,128)S(1)}, f32[3,4,128]{2,1,0:T(4,128)S(1)}, u32[]{:S(2)}, u32[]{:S(2)}) collective-permute-start(f32[3,4,128]{2,1,0:T(4,128)S(1)} %pad_maximum_fusion.4), channel_id=1, source_target_pairs={{0,24},{4,28},{8,0},{12,4},{16,8},{20,12},{24,16},{28,20},{1,25},{... | collective-permute-start | bytes 18440 | tf_op jit(solution)/shard_map/ppermute | solution.py:103
  49.0 4.6 %collective-permute-start.10 = (f32[3,4,128]{2,1,0:T(4,128)S(1)}, f32[3,4,128]{2,1,0:T(4,128)S(1)}, u32[]{:S(2)}, u32[]{:S(2)}) collective-permute-start(f32[3,4,128]{2,1,0:T(4,128)S(1)} %pad_maximum_fusion.4), channel_id=1, source_target_pairs={{0,16},{4,20},{8,24},{12,28},{16,0},{20,4},{24,8},{28,12},{1,17},{... | collective-permute-start | bytes 18440 | tf_op jit(solution)/shard_map/ppermute | solution.py:103
  50.8 5.4 %collective-permute-start.9 = (f32[3,4,128]{2,1,0:T(4,128)S(1)}, f32[3,4,128]{2,1,0:T(4,128)S(1)}, u32[]{:S(2)}, u32[]{:S(2)}) collective-permute-start(f32[3,4,128]{2,1,0:T(4,128)S(1)} %pad_maximum_fusion.4), channel_id=1, source_target_pairs={{0,8},{4,12},{8,16},{12,20},{16,24},{20,28},{24,0},{28,4},{1,9},{5... | collective-permute-start | bytes 18440 | tf_op jit(solution)/shard_map/ppermute | solution.py:103
  57.9 7.2 %collective-permute-start.15 = (bf16[640,768]{1,0:T(8,128)(2,1)S(1)}, bf16[640,768]{1,0:T(8,128)(2,1)S(1)}, u32[]{:S(2)}, u32[]{:S(2)}) collective-permute-start(bf16[640,768]{1,0:T(8,128)(2,1)S(1)} %slice.222), channel_id=1, source_target_pairs={{0,1},{1,0},{2,3},{3,2},{4,5},{5,4},{6,7},{7,6},{8,9},{9,8},{10,11... | collective-permute-start | bytes 2949128 | tf_op jit(solution)/shard_map/ppermute | solution.py:109
  60.7 9.7 %collective-permute-start.14 = (bf16[128,768]{1,0:T(8,128)(2,1)S(1)}, bf16[128,768]{1,0:T(8,128)(2,1)S(1)}, u32[]{:S(2)}, u32[]{:S(2)}) collective-permute-start(bf16[128,768]{1,0:T(8,128)(2,1)S(1)} %get-tuple-element.22), channel_id=1, source_target_pairs={{0,8},{4,12},{8,16},{12,20},{16,24},{20,28},{24,0},{28,4},{1,9},{5... | collective-permute-start | bytes 589832 | tf_op jit(solution)/shard_map/ppermute | solution.py:103
  60.8 17.1 %collective-permute-start.13 = (bf16[128,768]{1,0:T(8,128)(2,1)S(1)}, bf16[128,768]{1,0:T(8,128)(2,1)S(1)}, u32[]{:S(2)}, u32[]{:S(2)}) collective-permute-start(bf16[128,768]{1,0:T(8,128)(2,1)S(1)} %get-tuple-element.23), channel_id=1, source_target_pairs={{0,16},{4,20},{8,24},{12,28},{16,0},{20,4},{24,8},{28,12},{1,17},{... | collective-permute-start | bytes 589832 | tf_op jit(solution)/shard_map/ppermute | solution.py:103
  61.1 16.8 %collective-permute-start.12 = (bf16[128,768]{1,0:T(8,128)(2,1)S(1)}, bf16[128,768]{1,0:T(8,128)(2,1)S(1)}, u32[]{:S(2)}, u32[]{:S(2)}) collective-permute-start(bf16[128,768]{1,0:T(8,128)(2,1)S(1)} %get-tuple-element.21), channel_id=1, source_target_pairs={{0,24},{4,28},{8,0},{12,4},{16,8},{20,12},{24,16},{28,20},{1,25},{... | collective-permute-start | bytes 589832 | tf_op jit(solution)/shard_map/ppermute | solution.py:103
  65.4 13.3 %collective-permute-start.18 = (bf16[160,768]{1,0:T(8,128)(2,1)S(1)}, bf16[160,768]{1,0:T(8,128)(2,1)S(1)}, u32[]{:S(2)}, u32[]{:S(2)}) collective-permute-start(bf16[160,768]{1,0:T(8,128)(2,1)S(1)} %get-tuple-element.17), channel_id=1, source_target_pairs={{0,6},{1,7},{2,4},{3,5},{4,2},{5,3},{6,0},{7,1},{8,14},{9,15},{10,... | collective-permute-start | bytes 737288 | tf_op jit(solution)/shard_map/ppermute | solution.py:115
  67.9 11.5 %collective-permute-start.17 = (bf16[160,768]{1,0:T(8,128)(2,1)S(1)}, bf16[160,768]{1,0:T(8,128)(2,1)S(1)}, u32[]{:S(2)}, u32[]{:S(2)}) collective-permute-start(bf16[160,768]{1,0:T(8,128)(2,1)S(1)} %get-tuple-element.18), channel_id=1, source_target_pairs={{0,4},{4,0},{8,12},{12,8},{16,20},{20,16},{24,28},{28,24},{1,5},{5... | collective-permute-start | bytes 737288 | tf_op jit(solution)/shard_map/ppermute | solution.py:106
  70.4 9.1 %collective-permute-start.16 = (bf16[160,768]{1,0:T(8,128)(2,1)S(1)}, bf16[160,768]{1,0:T(8,128)(2,1)S(1)}, u32[]{:S(2)}, u32[]{:S(2)}) collective-permute-start(bf16[160,768]{1,0:T(8,128)(2,1)S(1)} %get-tuple-element.16), channel_id=1, source_target_pairs={{0,2},{1,3},{2,0},{3,1},{4,6},{5,7},{6,4},{7,5},{8,10},{9,11},{10,... | collective-permute-start | bytes 737288 | tf_op jit(solution)/shard_map/ppermute | solution.py:112

commit v2 on v0

--- a/solution.py
+++ b/solution.py
@@ -1,9 +1,14 @@
+import functools
+
 import jax
 import jax.numpy as jnp
 from jax import lax
+from jax.experimental import pallas as pl
+from jax.experimental.pallas import tpu as pltpu
 from jax.sharding import PartitionSpec as P
 
 exact = lax.Precision.HIGHEST
+LOW = -1e30
 
 
 def from_slots(values, picker):
@@ -14,7 +19,7 @@
     return jnp.dot(values, picker, precision=exact)
 
 
-def local(queries, weights, counts, hits, positive_offset, cluster_shard):
+def slot_plan(queries, weights, counts, hits, positive_offset, cluster_shard):
     peer_count = lax.axis_size("label")
     row_count, top_count = hits.shape
     slot_count = 3 * row_count * top_count // 2
@@ -88,7 +93,224 @@
     return (query_loss, query_grad, weight_grad)
 
 
+FAR = 1e30
+NT = (((1,), (1,)), ((), ()))
+TN = (((0,), (0,)), ((), ()))
+ROOM = pltpu.CompilerParams(vmem_limit_bytes=48 * 1024 * 1024)
+
+
+def score(held, q, logs, s_ref):
+    quarter = held.shape[0] // 4
+    peaks = []
+    for c in range(4):
+        rows = pl.ds(c * quarter, quarter)
+        s = lax.dot_general(held[rows, :], q, NT, preferred_element_type=jnp.float32) - logs[rows, :]
+        s_ref[rows, :] = s
+        peaks.append(jnp.max(s, axis=0, keepdims=True))
+    peaks = [jnp.maximum(peaks[0], peaks[2]), jnp.maximum(peaks[1], peaks[3])]
+    totals = []
+    for c in range(4):
+        e = jnp.exp(s_ref[pl.ds(c * quarter, quarter), :] - peaks[c % 2])
+        totals.append(jnp.sum(e, axis=0, keepdims=True))
+    return peaks[0], totals[0] + totals[2], peaks[1], totals[1] + totals[3]
+
+
+def first_scores(qa, qb, near, near_pair, far, far_pair, logs, held, q, s_ref, stats):
+    rows, quarter = qa.shape[0], near.shape[0]
+    q[pl.ds(0, rows), :] = qa[...]
+    q[pl.ds(rows, rows), :] = qb[...]
+    for c, ref in enumerate((near, near_pair, far, far_pair)):
+        held[pl.ds(c * quarter, quarter), :] = ref[pl.ds(0, quarter), :]
+    for i, v in enumerate(score(held, q[...], logs, s_ref)):
+        stats[2 * i : 2 * i + 1, :] = v[:, :rows]
+        stats[2 * i + 1 : 2 * i + 2, :] = v[:, rows:]
+
+
+def last_scores(qa, qb, held, logs, stats, meta, q, s_ref, message):
+    rows = qa.shape[0]
+    q[pl.ds(0, rows), :] = qa[...]
+    q[pl.ds(rows, rows), :] = qb[...]
+    for i, v in enumerate(score(held, q[...], logs, s_ref)):
+        message[4 * i : 4 * i + 2, :] = stats[2 * i : 2 * i + 2, :]
+        message[4 * i + 2 : 4 * i + 3, :] = v[:, :rows]
+        message[4 * i + 3 : 4 * i + 4, :] = v[:, rows:]
+    message[16:24, :] = meta[...]
+
+
+def terms(blocks, labels, where, m0, m1, m2, m3, s_ref, held, coef, out_a, out_b, normals):
+    messages = (m0, m1, m2, m3)
+    me, lane = where[0], where[1]
+    rows = m0.shape[1]
+    part = labels // 4
+    lines = {"normal": [], "near": [], "pair": [], "target": []}
+    for j in blocks:
+        bits = messages[j][16:17, :].astype(jnp.int32)
+        pairs = []
+        for k in range(4):
+            for side in range(2):
+                shard = (me ^ (2 * k)) ^ side
+                named = (jnp.right_shift(bits, shard) & 1) == 1
+                i = 8 * side + (j ^ k)
+                pairs.append((named, messages[k][i : i + 1, :], messages[k][i + 4 : i + 5, :]))
+        peak = functools.reduce(jnp.maximum, [jnp.where(n, m, LOW) for n, m, _ in pairs])
+        total = sum(jnp.where(n, t * jnp.exp(jnp.where(n, m - peak, 0.0)), 0.0) for n, m, t in pairs)
+        normal = peak + jnp.log(total)
+        lines["normal"].append(normal)
+        lines["near"].append(jnp.where(pairs[0][0], normal, FAR))
+        lines["pair"].append(jnp.where(pairs[1][0], normal, FAR))
+        lines["target"].append(messages[j][17:18, :].astype(jnp.int32))
+    lines = {name: jnp.concatenate(v, 1) for name, v in lines.items()}
+    normals[0:1, :] = lines["normal"][:, :rows]
+    normals[1:2, :] = lines["normal"][:, rows:]
+    index = lax.broadcasted_iota(jnp.int32, (part, 2 * rows), 0)
+    positive = jnp.zeros((1, 2 * rows), jnp.float32)
+    for c in range(4):
+        side, core = c % 2, c // 2
+        for x in range(2):
+            at = pl.ds((2 * c + x) * part, part)
+            base = (me ^ side) * labels + ((2 * x + core) ^ lane) * part
+            s = s_ref[at, :]
+            hot = index == lines["target"] - base
+            p = jnp.exp(s - lines["pair" if side else "near"])
+            coef[at, :] = (p - jnp.where(hot, 1.0, 0.0)).astype(jnp.bfloat16)
+            positive += jnp.sum(jnp.where(hot, s, 0.0), axis=0, keepdims=True)
+    grad = lax.dot_general(coef[...], held[...], TN, preferred_element_type=jnp.float32)
+    grad = grad.astype(jnp.bfloat16)
+    for i, out in enumerate((out_a, out_b)):
+        out[pl.ds(0, rows), :] = grad[i * rows : (i + 1) * rows]
+        line = positive[:, i * rows : (i + 1) * rows]
+        line = jnp.broadcast_to(line, (16, rows)).astype(jnp.bfloat16)
+        out[pl.ds(rows, 16), :] = jnp.zeros((16, out.shape[1]), jnp.bfloat16)
+        out[pl.ds(rows, 16), pl.ds(0, rows)] = line
+
+
+def label_terms(coef_a, coef_b, qa, qb, kept, sent):
+    half = kept.shape[0]
+    for i, out in enumerate((sent, kept)):
+        at = pl.ds((1 - i) * half, half)
+        out[...] = (
+            jnp.dot(coef_a[at, :], qa[...], preferred_element_type=jnp.float32)
+            + jnp.dot(coef_b[at, :], qb[...], preferred_element_type=jnp.float32)
+        ).astype(out.dtype)
+
+
+def dense_plan(queries, weights, counts, hits, positive_offset, cluster_shard):
+    n = lax.axis_size("label")
+    dp = lax.axis_size("dp")
+    rows, width = queries.shape
+    labels = weights.shape[0]
+    part = labels // dp
+    me = lax.axis_index("label")
+    lane = lax.axis_index("dp")
+    f32, bf16 = jnp.float32, jnp.bfloat16
+    shape = jax.ShapeDtypeStruct
+
+    def swap(x, k):
+        return lax.ppermute(x, "label", [(i, i ^ (2 * k)) for i in range(n)])
+
+    def pair(x):
+        return lax.ppermute(x, "label", [(i, i ^ 1) for i in range(n)])
+
+    def core(x):
+        return lax.ppermute(x, "dp", [(i, i ^ 1) for i in range(dp)])
+
+    def side(x):
+        return lax.ppermute(x, "dp", [(i, i ^ 2) for i in range(dp)])
+
+    def corner(x):
+        return lax.ppermute(
+            x, ("label", "dp"), [(i * dp + j, (i ^ 1) * dp + (j ^ 2)) for i in range(n) for j in range(dp)]
+        )
+
+    order = jnp.arange(dp, dtype=jnp.int32) ^ lane
+    blocks = jnp.take(weights.reshape(dp, part, width), order, axis=0)
+    blocks = blocks.reshape(2, 2, part, width)
+    near = blocks[:, 0].reshape(2 * part, width)
+    far = blocks[:, 1].reshape(2 * part, width)
+    count = jnp.take(counts.reshape(dp, part), order, axis=0).reshape(2, 2, part)
+    count_near, count_far = count[:, 0].reshape(-1), count[:, 1].reshape(-1)
+    line = jnp.concatenate([count_near >> 6, count_near & 63, jnp.zeros((width - 4 * part,), jnp.int32)])
+    line = jnp.pad(line.astype(bf16)[None, :], ((0, 15), (0, 0)))
+    near_pair = pair(jnp.concatenate([near, line], 0))
+    q2, q3, q1 = swap(queries, 2), swap(queries, 3), swap(queries, 1)
+    far_pair = core(near_pair)
+
+    def carried(x):
+        digits = x[2 * part, : 4 * part].astype(jnp.int32)
+        return digits[: 2 * part] * 64 + digits[2 * part :]
+
+    count_held = jnp.concatenate([count_near, carried(near_pair), count_far, carried(far_pair)])
+    logs = jnp.log(count_held.astype(f32))[:, None]
+
+    match = hits[:, :, None] == jnp.arange(cluster_shard.shape[0], dtype=jnp.int32)[None, None, :]
+    owner = jnp.sum(jnp.where(match, cluster_shard[None, None, :], 0), axis=2)
+    bits = jnp.sum(jnp.left_shift(1, owner), axis=1)
+    target = owner[:, 0] * labels + positive_offset
+    meta = jnp.pad(jnp.stack([bits, target]).astype(f32), ((0, 6), (0, 0)))
+
+    held, qa, sa, stats = pl.pallas_call(
+        first_scores,
+        out_shape=(
+            shape((2 * labels, width), bf16),
+            shape((2 * rows, width), bf16),
+            shape((2 * labels, 2 * rows), f32),
+            shape((8, rows), f32),
+        ),
+        compiler_params=ROOM,
+        name="first_scores",
+    )(queries, q1, near, near_pair, far, far_pair, logs)
+    qb, sb, message = pl.pallas_call(
+        last_scores,
+        out_shape=(shape((2 * rows, width), bf16), shape((2 * labels, 2 * rows), f32), shape((24, rows), f32)),
+        compiler_params=ROOM,
+        name="last_scores",
+    )(q2, q3, held, logs, stats, meta)
+
+    m3, m2, m1 = swap(message, 3), swap(message, 2), swap(message, 1)
+    where = jnp.stack([me, lane]).astype(jnp.int32)
+
+    def gradient(pairing, s):
+        spec = pl.BlockSpec(memory_space=pltpu.VMEM)
+        return pl.pallas_call(
+            functools.partial(terms, pairing, labels),
+            out_shape=(
+                shape((2 * labels, 2 * rows), bf16),
+                shape((rows + 16, width), bf16),
+                shape((rows + 16, width), bf16),
+                shape((2, rows), f32),
+            ),
+            in_specs=[pl.BlockSpec(memory_space=pltpu.SMEM)] + [spec] * 6,
+            compiler_params=ROOM,
+            name="terms",
+        )(where, message, m1, m2, m3, s, held)
+
+    coef_b, t2, t3, _ = gradient((2, 3), sb)
+    coef_a, t0, t1, normals = gradient((0, 1), sa)
+    kept, sent = pl.pallas_call(
+        label_terms,
+        out_shape=(shape((labels, width), f32), shape((labels, width), bf16)),
+        compiler_params=ROOM,
+        name="label_terms",
+    )(coef_a, coef_b, qa, qb)
+    arrived = core(sent)
+    g3, g2, g1 = swap(t3, 3), swap(t2, 2), swap(t1, 1)
+    summed = kept + arrived.astype(f32)
+    sent = summed[part:].astype(bf16)
+    other = [side(sent[:part]), pair(sent[part : 2 * part]), corner(sent[2 * part :])]
+    weight_grad = (summed[:part] + sum(o.astype(f32) for o in other)).astype(bf16)
+    grads = sum(g.astype(f32) for g in (t0, g1, g2, g3))
+    return normals[0] - grads[rows, :rows], grads[:rows].astype(bf16), weight_grad
+
+
 def solution(mesh):
+    n, dp = mesh.shape["label"], mesh.shape["dp"]
+
+    def local(queries, weights, counts, hits, positive_offset, cluster_shard):
+        rows, top = hits.shape
+        args = (queries, weights, counts, hits, positive_offset, cluster_shard)
+        dense = n == 8 and dp == 4 and (n // 2) * rows <= 3 * rows * top // 2
+        return dense_plan(*args) if dense else slot_plan(*args)
+
     return jax.shard_map(
         local,
         mesh=mesh,

time: 158 us -> 69.4 us (0.44)
  blocking collectives: 34 us -> 0 us
  waiting for transfers between devices: 52.6 us -> 27 us
  matrix products: 17 us -> 0 us
  between operations: 14.2 us -> 0.85 us
  Pallas kernels: 0 us -> 9.4 us
  other arithmetic: 8.83 us -> 2.47 us
  starting transfers between devices: 24.5 us -> 22.1 us
    all_to_all x6 -> x0, waiting for transfers between devices: 52.2 us -> none  [the longest x1 28.1 us: local(): lax.all_to_all(outgoing, 'label', split_axis=0, concat_axis=0, tiled=True)]
    all_to_all x2 -> x0, blocking collectives: 34 us -> none  [the longest x1 25.2 us: local(): lax.all_to_all(slot_grad, 'label', split_axis=0, concat_axis=0, tiled=True)]
    ppermute x0 -> x15, waiting for transfers between devices: none -> 27 us  [the longest x9 18.1 us: swap(): return lax.ppermute(x, 'label', [(i, i ^ 2 * k) for i in range(n)])]
    all_to_all x6 -> x0, starting transfers between devices: 24.5 us -> none  [the longest x1 7.28 us: local(): lax.all_to_all(outgoing, 'label', split_axis=0, concat_axis=0, tiled=True)]
    ppermute x0 -> x15, starting transfers between devices: none -> 22.1 us  [the longest x9 13.4 us: swap(): return lax.ppermute(x, 'label', [(i, i ^ 2 * k) for i in range(n)])]
    dot_general x11 -> x0, matrix products: 17 us -> none  [the longest x3 3.95 us: to_slots(): return jnp.dot(values, picker, precision=exact)]
    pallas_call x0 -> x5, Pallas kernels: none -> 9.4 us  [the longest x2 3.41 us: gradient(): pl.pallas_call(functools.partial(terms, pairing, labels), out_shape=(shap...]
    all_to_all x6 -> x0, other arithmetic: 3.55 us -> none  [the longest x1 0.7 us: local(): lax.all_to_all(target_slots, 'label', split_axis=0, concat_axis=0, tiled=...]
  transfers between devices with their start and end apart: 7 -> 15, of which waited for: 7 -> 6; matrix products, arithmetic and copies ran while one was open for 6% -> 7% of each run, Pallas kernels for 0% -> 4%
where the time goes in v2:
time: 69.4 us; the launch traced here: 69.1 us
  waiting for transfers between devices  27 us (39%)
  starting transfers between devices  22.1 us (32%)
  Pallas kernels  9.4 us (14%)
  local copies, waits for them, and re-layouts  7.31 us (11%)
  other arithmetic  2.47 us (4%)
  between operations  0.85 us (1%)
    ppermute x9, waiting for transfers between devices, swap(): return lax.ppermute(x, 'label', [(i, i ^ 2 * k) for i in range(n)])  18.1 us
    ppermute x9, starting transfers between devices, swap(): return lax.ppermute(x, 'label', [(i, i ^ 2 * k) for i in range(n)])  13.4 us
    ppermute x2, waiting for transfers between devices, pair(): return lax.ppermute(x, 'label', [(i, i ^ 1) for i in range(n)])  7.07 us
    ppermute x2, starting transfers between devices, pair(): return lax.ppermute(x, 'label', [(i, i ^ 1) for i in range(n)])  4.57 us
    pallas_call x2, Pallas kernels, gradient(): pl.pallas_call(functools.partial(terms, pairing, labels), out_shape=(shap...  3.41 us
    pallas_call x1, Pallas kernels, dense_plan(): pl.pallas_call(first_scores, out_shape=(shape((2 * labels, width), bf16),...  2.77 us
    ppermute x1, starting transfers between devices, corner(): lax.ppermute(x, ('label', 'dp'), [(i * dp + j, (i ^ 1) * dp + (j ^ 2)) fo...  2.47 us
    pallas_call x1, Pallas kernels, dense_plan(): pl.pallas_call(last_scores, out_shape=(shape((2 * rows, width), bf16), sh...  2.02 us
  transfers between devices with their start and end apart: 15, of which 6 were waited for; matrix products, arithmetic and copies ran while one was open for 7% of the time, Pallas kernels for 4%

profile of v2, /device:TPU:0, one launch (start us, length us, event | category | flops | bytes accessed | tf_op | source)
XLA Modules:
  0.0 69.1 jit_solution(2234291934514383122)
XLA Ops:
  0.7 0.8 %reshape.167 = s32[4,160]{1,0:T(4,128)S(1)} reshape(s32[640]{0:T(1024)} %param.8) | data formatting | bytes 5120 | tf_op jit(solution)/shard_map/reshape | solution.py:230
  1.5 0.6 gather_fusion.1
  2.5 0.6 gather_fusion
  3.5 3.0 %collective-permute-start.3 = (bf16[336,768]{1,0:T(8,128)(2,1)S(1)}, bf16[336,768]{1,0:T(8,128)(2,1)S(1)}, u32[]{:S(2)}, u32[]{:S(2)}) collective-permute-start(bf16[336,768]{1,0:T(8,128)(2,1)S(1)} %fusion.1), channel_id=1, source_target_pairs={{0,4},{4,0},{8,12},{12,8},{16,20},{20,16},{24,28},{28,24},{1,5},{5... | collective-permute-start | bytes 1548296 | tf_op jit(solution)/shard_map/ppermute | solution.py:212
  6.6 1.6 %collective-permute-start.2 = (bf16[128,768]{1,0:T(8,128)(2,1)S(1)}, bf16[128,768]{1,0:T(8,128)(2,1)}, u32[]{:S(2)}, u32[]{:S(2)}) collective-permute-start(bf16[128,768]{1,0:T(8,128)(2,1)S(1)} %copy-done.3), channel_id=1, source_target_pairs={{0,8},{4,12},{8,0},{12,4},{16,24},{20,28},{24,16},{28,20},{1,9},{5... | collective-permute-start | bytes 589832 | tf_op jit(solution)/shard_map/ppermute | solution.py:209
  8.2 2.6 %collective-permute-start = (bf16[128,768]{1,0:T(8,128)(2,1)S(1)}, bf16[128,768]{1,0:T(8,128)(2,1)S(1)}, u32[]{:S(2)}, u32[]{:S(2)}) collective-permute-start(bf16[128,768]{1,0:T(8,128)(2,1)S(1)} %copy-done.3), channel_id=1, source_target_pairs={{0,16},{4,20},{8,24},{12,28},{16,0},{20,4},{24,8},{28,12},{1,17},{... | collective-permute-start | bytes 589832 | tf_op jit(solution)/shard_map/ppermute | solution.py:209
  11.3 7.1 %collective-permute-done.3.near_pair = bf16[336,768]{1,0:T(8,128)(2,1)S(1)} collective-permute-done((bf16[336,768]{1,0:T(8,128)(2,1)S(1)}, bf16[336,768]{1,0:T(8,128)(2,1)S(1)}, u32[]{:S(2)}, u32[]{:S(2)}) %collective-permute-start.3) | collective-permute-done | bytes 516128 | tf_op jit(solution)/shard_map/ppermute | solution.py:212
  18.4 1.8 %collective-permute-done.4.far_pair = bf16[336,768]{1,0:T(8,128)(2,1)S(1)} collective-permute-done((bf16[336,768]{1,0:T(8,128)(2,1)S(1)}, bf16[336,768]{1,0:T(8,128)(2,1)S(1)}, u32[]{:S(2)}, u32[]{:S(2)}) %collective-permute-start.4) | collective-permute-done | bytes 516128 | tf_op jit(solution)/shard_map/ppermute | solution.py:215
  20.4 1.1 %copy.24 = f32[1280,1]{1,0:T(8,128)} copy(f32[1280,1]{0,1:T(1,128)S(1)} %convert_element_type.64) | data formatting | bytes 10240 | tf_op jit(solution)/shard_map/convert_element_type | solution.py:243
  21.5 1.2 %log.10.logs = f32[1280,1]{1,0:T(8,128)S(1)} log(f32[1280,1]{1,0:T(8,128)} %copy.24) | non-fusion elementwise | bytes 10240 | tf_op jit(solution)/shard_map/log | solution.py:243
  22.7 2.8 %first_scores.1 = (bf16[1280,768]{1,0:T(8,128)(2,1)}, bf16[256,768]{1,0:T(8,128)(2,1)S(1)}, f32[1280,256]{1,0:T(8,128)S(1)}, f32[8,128]{1,0:T(8,128)S(1)}) custom-call(bf16[128,768]{1,0:T(8,128)(2,1)S(1)} %copy-done.3, bf16[128,768]{1,0:T(8,128)(2,1)} %collective-permute-done.2.qb, bf16[320,768]{1,0:T(8,128)(2,1)S(1)} %bitcast.31, ...), custom_call_target="tpu_custom_call" | custom-call | tf_op jit(solution)/shard_map/first_scores/pallas_call | solution.py:251
  25.5 1.5 %copy-done.1 = bf16[1280,768]{1,0:T(8,128)(2,1)S(1)} copy-done((bf16[1280,768]{1,0:T(8,128)(2,1)S(1)}, bf16[1280,768]{1,0:T(8,128)(2,1)}, u32[]{:S(2)}) %copy-start.1) | copy-done | bytes 1966104
  27.1 2.0 %last_scores.1 = (bf16[256,768]{1,0:T(8,128)(2,1)S(1)}, f32[1280,256]{1,0:T(8,128)S(1)}, f32[24,128]{1,0:T(8,128)S(1)}) custom-call(bf16[128,768]{1,0:T(8,128)(2,1)S(1)} %collective-permute-done.qa, bf16[128,768]{1,0:T(8,128)(2,1)} %collective-permute-done.1.qb, bf16[1280,768]{1,0:T(8,128)(2,1)S(1)} %copy-done.1, f32[1280,1]{1,0:T(8,128)S(1)} %log.10.logs, ...), custom_call_target="tpu_custom_call" | custom-call | tf_op jit(solution)/shard_map/last_scores/pallas_call | solution.py:262
  29.1 3.0 %collective-permute-start.5 = (f32[24,128]{1,0:T(8,128)S(1)}, f32[24,128]{1,0:T(8,128)S(1)}, u32[]{:S(2)}, u32[]{:S(2)}) collective-permute-start(f32[24,128]{1,0:T(8,128)S(1)} %get-tuple-element.21.m0), channel_id=1, source_target_pairs={{0,8},{4,12},{8,0},{12,4},{16,24},{20,28},{24,16},{28,20},{1,9},{5... | collective-permute-start | bytes 36872 | tf_op jit(solution)/shard_map/ppermute | solution.py:209
  32.1 1.4 %collective-permute-start.6 = (f32[24,128]{1,0:T(8,128)S(1)}, f32[24,128]{1,0:T(8,128)S(1)}, u32[]{:S(2)}, u32[]{:S(2)}) collective-permute-start(f32[24,128]{1,0:T(8,128)S(1)} %get-tuple-element.21.m0), channel_id=1, source_target_pairs={{0,16},{4,20},{8,24},{12,28},{16,0},{20,4},{24,8},{28,12},{1,17},{... | collective-permute-start | bytes 36872 | tf_op jit(solution)/shard_map/ppermute | solution.py:209
  33.5 1.1 %collective-permute-start.7 = (f32[24,128]{1,0:T(8,128)S(1)}, f32[24,128]{1,0:T(8,128)S(1)}, u32[]{:S(2)}, u32[]{:S(2)}) collective-permute-start(f32[24,128]{1,0:T(8,128)S(1)} %get-tuple-element.21.m0), channel_id=1, source_target_pairs={{0,24},{4,28},{8,16},{12,20},{16,8},{20,12},{24,0},{28,4},{1,25},{... | collective-permute-start | bytes 36872 | tf_op jit(solution)/shard_map/ppermute | solution.py:209
  34.7 2.0 %collective-permute-done.6.m2 = f32[24,128]{1,0:T(8,128)S(1)} collective-permute-done((f32[24,128]{1,0:T(8,128)S(1)}, f32[24,128]{1,0:T(8,128)S(1)}, u32[]{:S(2)}, u32[]{:S(2)}) %collective-permute-start.6) | collective-permute-done | bytes 12320 | tf_op jit(solution)/shard_map/ppermute | solution.py:209
  36.7 2.3 %collective-permute-done.7.m3 = f32[24,128]{1,0:T(8,128)S(1)} collective-permute-done((f32[24,128]{1,0:T(8,128)S(1)}, f32[24,128]{1,0:T(8,128)S(1)}, u32[]{:S(2)}, u32[]{:S(2)}) %collective-permute-start.7) | collective-permute-done | bytes 12320 | tf_op jit(solution)/shard_map/ppermute | solution.py:209
  39.0 1.7 %terms.2 = (bf16[1280,256]{1,0:T(8,128)(2,1)S(1)}, bf16[144,768]{1,0:T(8,128)(2,1)S(1)}, bf16[144,768]{1,0:T(8,128)(2,1)S(1)}, f32[2,128]{1,0:T(2,128)S(1)}) custom-call(s32[2]{0:T(128)S(1)} %pad_add_fusion.where, f32[24,128]{1,0:T(8,128)S(1)} %get-tuple-element.21.m0, f32[24,128]{1,0:T(8,128)S(1)} %collective-permute-done.5.m1, ...), custom_call_target="tpu_custom_call" | custom-call | tf_op jit(solution)/shard_map/terms/pallas_call | solution.py:274
  40.7 1.7 %terms.3 = (bf16[1280,256]{1,0:T(8,128)(2,1)S(1)}, bf16[144,768]{1,0:T(8,128)(2,1)S(1)}, bf16[144,768]{1,0:T(8,128)(2,1)S(1)}, f32[2,128]{1,0:T(2,128)}) custom-call(s32[2]{0:T(128)S(1)} %pad_add_fusion.where, f32[24,128]{1,0:T(8,128)S(1)} %get-tuple-element.21.m0, f32[24,128]{1,0:T(8,128)S(1)} %collective-permute-done.5.m1, ...), custom_call_target="tpu_custom_call" | custom-call | tf_op jit(solution)/shard_map/terms/pallas_call | solution.py:274
  42.4 1.2 %label_terms.1 = (f32[640,768]{1,0:T(8,128)S(1)}, bf16[640,768]{1,0:T(8,128)(2,1)S(1)}) custom-call(bf16[1280,256]{1,0:T(8,128)(2,1)S(1)} %get-tuple-element.29.coef_a, bf16[1280,256]{1,0:T(8,128)(2,1)S(1)} %get-tuple-element.30.coef_b, bf16[256,768]{1,0:T(8,128)(2,1)S(1)} %get-tuple-element.31.qa, bf16[256,768]{1,0:T(8,128)(2,1)S(1)} %get-tuple-element.32.qb), custom_call_target="tpu_custom_call" | custom-call | tf_op jit(solution)/shard_map/label_terms/pallas_call | solution.py:289
  43.8 1.2 %collective-permute-start.10 = (bf16[144,768]{1,0:T(8,128)(2,1)S(1)}, bf16[144,768]{1,0:T(8,128)(2,1)S(1)}, u32[]{:S(2)}, u32[]{:S(2)}) collective-permute-start(bf16[144,768]{1,0:T(8,128)(2,1)S(1)} %get-tuple-element.28), channel_id=1, source_target_pairs={{0,24},{4,28},{8,16},{12,20},{16,8},{20,12},{24,0},{28,4},{1,25},{... | collective-permute-start | bytes 663560 | tf_op jit(solution)/shard_map/ppermute | solution.py:209
  45.0 2.3 %collective-permute-start.9 = (bf16[144,768]{1,0:T(8,128)(2,1)S(1)}, bf16[144,768]{1,0:T(8,128)(2,1)S(1)}, u32[]{:S(2)}, u32[]{:S(2)}) collective-permute-start(bf16[144,768]{1,0:T(8,128)(2,1)S(1)} %get-tuple-element.27), channel_id=1, source_target_pairs={{0,16},{4,20},{8,24},{12,28},{16,0},{20,4},{24,8},{28,12},{1,17},{... | collective-permute-start | bytes 663560 | tf_op jit(solution)/shard_map/ppermute | solution.py:209
  47.3 0.3 fusion.8
  47.6 1.6 %collective-permute-start.12 = (bf16[160,768]{1,0:T(8,128)(2,1)S(1)}, bf16[160,768]{1,0:T(8,128)(2,1)S(1)}, u32[]{:S(2)}, u32[]{:S(2)}) collective-permute-start(bf16[160,768]{1,0:T(8,128)(2,1)S(1)} %get-tuple-element.37), channel_id=1, source_target_pairs={{0,2},{1,3},{2,0},{3,1},{4,6},{5,7},{6,4},{7,5},{8,10},{9,11},{10,... | collective-permute-start | bytes 737288 | tf_op jit(solution)/shard_map/ppermute | solution.py:218
  49.2 1.5 %collective-permute-start.13 = (bf16[160,768]{1,0:T(8,128)(2,1)S(1)}, bf16[160,768]{1,0:T(8,128)(2,1)S(1)}, u32[]{:S(2)}, u32[]{:S(2)}) collective-permute-start(bf16[160,768]{1,0:T(8,128)(2,1)S(1)} %get-tuple-element.39), channel_id=1, source_target_pairs={{0,4},{4,0},{8,12},{12,8},{16,20},{20,16},{24,28},{28,24},{1,5},{5... | collective-permute-start | bytes 737288 | tf_op jit(solution)/shard_map/ppermute | solution.py:212
  50.7 5.6 %collective-permute-done.8 = bf16[144,768]{1,0:T(8,128)(2,1)S(1)} collective-permute-done((bf16[144,768]{1,0:T(8,128)(2,1)S(1)}, bf16[144,768]{1,0:T(8,128)(2,1)S(1)}, u32[]{:S(2)}, u32[]{:S(2)}) %collective-permute-start.8) | collective-permute-done | bytes 221216 | tf_op jit(solution)/shard_map/ppermute | solution.py:209
  56.3 2.5 %collective-permute-start.14 = (bf16[160,768]{1,0:T(8,128)(2,1)S(1)}, bf16[160,768]{1,0:T(8,128)(2,1)S(1)}, u32[]{:S(2)}, u32[]{:S(2)}) collective-permute-start(bf16[160,768]{1,0:T(8,128)(2,1)S(1)} %get-tuple-element.38), channel_id=1, source_target_pairs={{0,6},{1,7},{2,4},{3,5},{4,2},{5,3},{6,0},{7,1},{8,14},{9,15},{10,... | collective-permute-start | bytes 737288 | tf_op jit(solution)/shard_map/ppermute | solution.py:221
  58.8 8.2 %collective-permute-done.9 = bf16[144,768]{1,0:T(8,128)(2,1)S(1)} collective-permute-done((bf16[144,768]{1,0:T(8,128)(2,1)S(1)}, bf16[144,768]{1,0:T(8,128)(2,1)S(1)}, u32[]{:S(2)}, u32[]{:S(2)}) %collective-permute-start.9) | collective-permute-done | bytes 221216 | tf_op jit(solution)/shard_map/ppermute | solution.py:209
  67.1 0.7 %slice.127 = bf16[128,768]{1,0:T(8,128)(2,1)} slice(f32[144,768]{1,0:T(8,128)S(1)} %convert_add_fusion.1), slice={[0:128], [0:768]} | slice | bytes 393216 | tf_op jit(solution)/shard_map/slice | solution.py:302
  67.8 0.5 fusion.6
  68.3 0.8 %fusion.2 = bf16[160,768]{1,0:T(8,128)(2,1)} fusion(f32[640,768]{1,0:T(8,128)S(1)} %get-tuple-element.36, bf16[160,768]{1,0:T(8,128)(2,1)S(1)} %collective-permute-done.14, bf16[160,768]{1,0:T(8,128)(2,1)S(1)} %collective-permute-done.13, bf16[160,768]{1,0:T(8,128)(2,1)S(1)} %collective-permute-done.12), kind=kLoop, calls=%fused_computation.8 | loop fusion | flops 860160 | bytes 1474560 | tf_op jit(solution)/shard_map/convert_element_type | solution.py:300
  (57 shorter events, 2.0 us)
Async XLA Ops:
  0.6 1.9 %copy-start = (bf16[640,768]{1,0:T(8,128)(2,1)S(1)}, bf16[640,768]{1,0:T(8,128)(2,1)}, u32[]{:S(2)}) copy-start(bf16[640,768]{1,0:T(8,128)(2,1)} %param.7) | copy-start | bytes 2949124
  3.3 3.3 %copy-start.3 = (bf16[128,768]{1,0:T(8,128)(2,1)S(1)}, bf16[128,768]{1,0:T(8,128)(2,1)}, u32[]{:S(2)}) copy-start(bf16[128,768]{1,0:T(8,128)(2,1)} %qa.1) | copy-start | bytes 589828
  3.3 7.8 %copy-start.4 = (s32[128,4]{0,1:T(4,128)S(1)}, s32[128,4]{0,1:T(4,128)}, u32[]{:S(2)}) copy-start(s32[128,4]{0,1:T(4,128)} %param.9) | copy-start | bytes 6148
  3.3 7.8 %copy-start.5 = (s32[8]{0:T(128)S(1)}, s32[8]{0:T(128)}, u32[]{:S(2)}) copy-start(s32[8]{0:T(128)} %param.11) | copy-start | bytes 100
  3.3 7.9 %copy-start.6 = (s32[128]{0:T(128)S(1)}, s32[128]{0:T(128)}, u32[]{:S(2)}) copy-start(s32[128]{0:T(128)} %param.10) | copy-start | bytes 1540
  3.5 14.8 %collective-permute-start.3 = (bf16[336,768]{1,0:T(8,128)(2,1)S(1)}, bf16[336,768]{1,0:T(8,128)(2,1)S(1)}, u32[]{:S(2)}, u32[]{:S(2)}) collective-permute-start(bf16[336,768]{1,0:T(8,128)(2,1)S(1)} %fusion.1), channel_id=1, source_target_pairs={{0,4},{4,0},{8,12},{12,8},{16,20},{20,16},{24,28},{28,24},{1,5},{5... | collective-permute-start | bytes 1548296 | tf_op jit(solution)/shard_map/ppermute | solution.py:212
  6.6 16.2 %collective-permute-start.2 = (bf16[128,768]{1,0:T(8,128)(2,1)S(1)}, bf16[128,768]{1,0:T(8,128)(2,1)}, u32[]{:S(2)}, u32[]{:S(2)}) collective-permute-start(bf16[128,768]{1,0:T(8,128)(2,1)S(1)} %copy-done.3), channel_id=1, source_target_pairs={{0,8},{4,12},{8,0},{12,4},{16,24},{20,28},{24,16},{28,20},{1,9},{5... | collective-permute-start | bytes 589832 | tf_op jit(solution)/shard_map/ppermute | solution.py:209
  8.2 17.4 %collective-permute-start = (bf16[128,768]{1,0:T(8,128)(2,1)S(1)}, bf16[128,768]{1,0:T(8,128)(2,1)S(1)}, u32[]{:S(2)}, u32[]{:S(2)}) collective-permute-start(bf16[128,768]{1,0:T(8,128)(2,1)S(1)} %copy-done.3), channel_id=1, source_target_pairs={{0,16},{4,20},{8,24},{12,28},{16,0},{20,4},{24,8},{28,12},{1,17},{... | collective-permute-start | bytes 589832 | tf_op jit(solution)/shard_map/ppermute | solution.py:209
  10.7 14.8 %collective-permute-start.1 = (bf16[128,768]{1,0:T(8,128)(2,1)S(1)}, bf16[128,768]{1,0:T(8,128)(2,1)}, u32[]{:S(2)}, u32[]{:S(2)}) collective-permute-start(bf16[128,768]{1,0:T(8,128)(2,1)S(1)} %copy-done.3), channel_id=1, source_target_pairs={{0,24},{4,28},{8,16},{12,20},{16,8},{20,12},{24,0},{28,4},{1,25},{... | collective-permute-start | bytes 589832 | tf_op jit(solution)/shard_map/ppermute | solution.py:209
  18.3 1.9 %collective-permute-start.4 = (bf16[336,768]{1,0:T(8,128)(2,1)S(1)}, bf16[336,768]{1,0:T(8,128)(2,1)S(1)}, u32[]{:S(2)}, u32[]{:S(2)}) collective-permute-start(bf16[336,768]{1,0:T(8,128)(2,1)S(1)} %collective-permute-done.3.near_pair), channel_id=1, source_target_pairs={{0,1},{1,0},{2,3},{3,2},{4,5},{5,4},{6,7},{7,6},{8,9},{9,8},{10,11... | collective-permute-start | bytes 1548296 | tf_op jit(solution)/shard_map/ppermute | solution.py:215
  25.5 1.5 %copy-start.1 = (bf16[1280,768]{1,0:T(8,128)(2,1)S(1)}, bf16[1280,768]{1,0:T(8,128)(2,1)}, u32[]{:S(2)}) copy-start(bf16[1280,768]{1,0:T(8,128)(2,1)} %get-tuple-element.19.held) | copy-start | bytes 5898244
  27.1 12.0 %copy-start.2 = (bf16[1280,768]{1,0:T(8,128)(2,1)S(1)}, bf16[1280,768]{1,0:T(8,128)(2,1)}, u32[]{:S(2)}) copy-start(bf16[1280,768]{1,0:T(8,128)(2,1)} %get-tuple-element.19.held) | copy-start | bytes 5898244
  29.1 5.6 %collective-permute-start.5 = (f32[24,128]{1,0:T(8,128)S(1)}, f32[24,128]{1,0:T(8,128)S(1)}, u32[]{:S(2)}, u32[]{:S(2)}) collective-permute-start(f32[24,128]{1,0:T(8,128)S(1)} %get-tuple-element.21.m0), channel_id=1, source_target_pairs={{0,8},{4,12},{8,0},{12,4},{16,24},{20,28},{24,16},{28,20},{1,9},{5... | collective-permute-start | bytes 36872 | tf_op jit(solution)/shard_map/ppermute | solution.py:209
  32.1 4.6 %collective-permute-start.6 = (f32[24,128]{1,0:T(8,128)S(1)}, f32[24,128]{1,0:T(8,128)S(1)}, u32[]{:S(2)}, u32[]{:S(2)}) collective-permute-start(f32[24,128]{1,0:T(8,128)S(1)} %get-tuple-element.21.m0), channel_id=1, source_target_pairs={{0,16},{4,20},{8,24},{12,28},{16,0},{20,4},{24,8},{28,12},{1,17},{... | collective-permute-start | bytes 36872 | tf_op jit(solution)/shard_map/ppermute | solution.py:209
  33.5 5.5 %collective-permute-start.7 = (f32[24,128]{1,0:T(8,128)S(1)}, f32[24,128]{1,0:T(8,128)S(1)}, u32[]{:S(2)}, u32[]{:S(2)}) collective-permute-start(f32[24,128]{1,0:T(8,128)S(1)} %get-tuple-element.21.m0), channel_id=1, source_target_pairs={{0,24},{4,28},{8,16},{12,20},{16,8},{20,12},{24,0},{28,4},{1,25},{... | collective-permute-start | bytes 36872 | tf_op jit(solution)/shard_map/ppermute | solution.py:209
  43.7 3.6 %collective-permute-start.11 = (bf16[640,768]{1,0:T(8,128)(2,1)S(1)}, bf16[640,768]{1,0:T(8,128)(2,1)S(1)}, u32[]{:S(2)}, u32[]{:S(2)}) collective-permute-start(bf16[640,768]{1,0:T(8,128)(2,1)S(1)} %get-tuple-element.34), channel_id=1, source_target_pairs={{0,1},{1,0},{2,3},{3,2},{4,5},{5,4},{6,7},{7,6},{8,9},{9,8},{10,11... | collective-permute-start | bytes 2949128 | tf_op jit(solution)/shard_map/ppermute | solution.py:215
  43.7 12.6 %collective-permute-start.8 = (bf16[144,768]{1,0:T(8,128)(2,1)S(1)}, bf16[144,768]{1,0:T(8,128)(2,1)S(1)}, u32[]{:S(2)}, u32[]{:S(2)}) collective-permute-start(bf16[144,768]{1,0:T(8,128)(2,1)S(1)} %get-tuple-element.25), channel_id=1, source_target_pairs={{0,8},{4,12},{8,0},{12,4},{16,24},{20,28},{24,16},{28,20},{1,9},{5... | collective-permute-start | bytes 663560 | tf_op jit(solution)/shard_map/ppermute | solution.py:209
  43.8 15.0 %collective-permute-start.10 = (bf16[144,768]{1,0:T(8,128)(2,1)S(1)}, bf16[144,768]{1,0:T(8,128)(2,1)S(1)}, u32[]{:S(2)}, u32[]{:S(2)}) collective-permute-start(bf16[144,768]{1,0:T(8,128)(2,1)S(1)} %get-tuple-element.28), channel_id=1, source_target_pairs={{0,24},{4,28},{8,16},{12,20},{16,8},{20,12},{24,0},{28,4},{1,25},{... | collective-permute-start | bytes 663560 | tf_op jit(solution)/shard_map/ppermute | solution.py:209
  45.0 22.0 %collective-permute-start.9 = (bf16[144,768]{1,0:T(8,128)(2,1)S(1)}, bf16[144,768]{1,0:T(8,128)(2,1)S(1)}, u32[]{:S(2)}, u32[]{:S(2)}) collective-permute-start(bf16[144,768]{1,0:T(8,128)(2,1)S(1)} %get-tuple-element.27), channel_id=1, source_target_pairs={{0,16},{4,20},{8,24},{12,28},{16,0},{20,4},{24,8},{28,12},{1,17},{... | collective-permute-start | bytes 663560 | tf_op jit(solution)/shard_map/ppermute | solution.py:209
  47.6 20.7 %collective-permute-start.12 = (bf16[160,768]{1,0:T(8,128)(2,1)S(1)}, bf16[160,768]{1,0:T(8,128)(2,1)S(1)}, u32[]{:S(2)}, u32[]{:S(2)}) collective-permute-start(bf16[160,768]{1,0:T(8,128)(2,1)S(1)} %get-tuple-element.37), channel_id=1, source_target_pairs={{0,2},{1,3},{2,0},{3,1},{4,6},{5,7},{6,4},{7,5},{8,10},{9,11},{10,... | collective-permute-start | bytes 737288 | tf_op jit(solution)/shard_map/ppermute | solution.py:218
  49.2 19.1 %collective-permute-start.13 = (bf16[160,768]{1,0:T(8,128)(2,1)S(1)}, bf16[160,768]{1,0:T(8,128)(2,1)S(1)}, u32[]{:S(2)}, u32[]{:S(2)}) collective-permute-start(bf16[160,768]{1,0:T(8,128)(2,1)S(1)} %get-tuple-element.39), channel_id=1, source_target_pairs={{0,4},{4,0},{8,12},{12,8},{16,20},{20,16},{24,28},{28,24},{1,5},{5... | collective-permute-start | bytes 737288 | tf_op jit(solution)/shard_map/ppermute | solution.py:212
  56.3 12.0 %collective-permute-start.14 = (bf16[160,768]{1,0:T(8,128)(2,1)S(1)}, bf16[160,768]{1,0:T(8,128)(2,1)S(1)}, u32[]{:S(2)}, u32[]{:S(2)}) collective-permute-start(bf16[160,768]{1,0:T(8,128)(2,1)S(1)} %get-tuple-element.38), channel_id=1, source_target_pairs={{0,6},{1,7},{2,4},{3,5},{4,2},{5,3},{6,0},{7,1},{8,14},{9,15},{10,... | collective-permute-start | bytes 737288 | tf_op jit(solution)/shard_map/ppermute | solution.py:221

commit v3 on v2

--- a/solution.py
+++ b/solution.py
@@ -96,7 +96,25 @@
 FAR = 1e30
 NT = (((1,), (1,)), ((), ()))
 TN = (((0,), (0,)), ((), ()))
-ROOM = pltpu.CompilerParams(vmem_limit_bytes=48 * 1024 * 1024)
+ROOM = pltpu.CompilerParams(vmem_limit_bytes=20 * 1024 * 1024)
+
+
+def cost(flops, size, exps=0):
+    return pl.CostEstimate(flops=int(flops), bytes_accessed=int(size), transcendentals=int(exps))
+
+
+def pack(where, weights, counts, out):
+    lane = where[1]
+    part = weights.shape[0] // 4
+    for x in range(2):
+        base = pl.multiple_of(((2 * x) ^ lane) * part, part)
+        out[pl.ds(x * part, part), :] = weights[pl.ds(base, part), :]
+    row = lax.broadcasted_iota(jnp.int32, (16, counts.shape[1]), 0)
+    count = counts[...]
+    high, low = jnp.right_shift(count, 6), count & 63
+    digits = jnp.where(row == 0, high, jnp.where(row == 1, low, 0)).astype(jnp.float32)
+    out[pl.ds(2 * part, 16), :] = jnp.zeros((16, out.shape[1]), jnp.bfloat16)
+    out[pl.ds(2 * part, 16), pl.ds(0, counts.shape[1])] = digits.astype(jnp.bfloat16)
 
 
 def score(held, q, logs, s_ref):
@@ -115,12 +133,25 @@
     return peaks[0], totals[0] + totals[2], peaks[1], totals[1] + totals[3]
 
 
-def first_scores(qa, qb, near, near_pair, far, far_pair, logs, held, q, s_ref, stats):
-    rows, quarter = qa.shape[0], near.shape[0]
+def first_scores(where, qa, qb, weights, counts, near_pair, far_pair, held, q, s_ref, stats, logs, column):
+    lane = where[1]
+    rows, labels = qa.shape[0], weights.shape[0]
+    part, half = labels // 4, labels // 2
     q[pl.ds(0, rows), :] = qa[...]
     q[pl.ds(rows, rows), :] = qb[...]
-    for c, ref in enumerate((near, near_pair, far, far_pair)):
-        held[pl.ds(c * quarter, quarter), :] = ref[pl.ds(0, quarter), :]
+    digits = near_pair[pl.ds(half, 16), :].astype(jnp.float32)[:, :labels]
+    lines = (counts[...].astype(jnp.float32), digits[0:1] * 64.0 + digits[1:2])
+    for side, line in enumerate(lines):
+        column[...] = jnp.transpose(jnp.broadcast_to(jnp.log(line), (8, labels)))
+        for core in range(2):
+            for x in range(2):
+                at = pl.ds((4 * core + 2 * side + x) * part, part)
+                base = pl.multiple_of(((2 * x + core) ^ lane) * part, part)
+                logs[at, :] = column[pl.ds(base, part), 0:1]
+                if side:
+                    held[at, :] = (far_pair if core else near_pair)[pl.ds(x * part, part), :]
+                else:
+                    held[at, :] = weights[pl.ds(base, part), :]
     for i, v in enumerate(score(held, q[...], logs, s_ref)):
         stats[2 * i : 2 * i + 1, :] = v[:, :rows]
         stats[2 * i + 1 : 2 * i + 2, :] = v[:, rows:]
@@ -194,6 +225,17 @@
         ).astype(out.dtype)
 
 
+def finish(normals, t0, t1, t2, t3, own, s0, s1, s2, loss, query_grad, weight_grad):
+    f32 = jnp.float32
+    rows = query_grad.shape[0]
+    total = sum(t[pl.ds(0, rows), :].astype(f32) for t in (t0, t1, t2, t3))
+    query_grad[...] = total.astype(query_grad.dtype)
+    line = sum(t[pl.ds(rows, 16), pl.ds(0, rows)].astype(f32) for t in (t0, t1, t2, t3))
+    loss[...] = normals[0:1, :] - line[0:1]
+    total = own[...] + sum(s[...].astype(f32) for s in (s0, s1, s2))
+    weight_grad[...] = total.astype(weight_grad.dtype)
+
+
 def dense_plan(queries, weights, counts, hits, positive_offset, cluster_shard):
     n = lax.axis_size("label")
     dp = lax.axis_size("dp")
@@ -222,25 +264,22 @@
             x, ("label", "dp"), [(i * dp + j, (i ^ 1) * dp + (j ^ 2)) for i in range(n) for j in range(dp)]
         )
 
-    order = jnp.arange(dp, dtype=jnp.int32) ^ lane
-    blocks = jnp.take(weights.reshape(dp, part, width), order, axis=0)
-    blocks = blocks.reshape(2, 2, part, width)
-    near = blocks[:, 0].reshape(2 * part, width)
-    far = blocks[:, 1].reshape(2 * part, width)
-    count = jnp.take(counts.reshape(dp, part), order, axis=0).reshape(2, 2, part)
-    count_near, count_far = count[:, 0].reshape(-1), count[:, 1].reshape(-1)
-    line = jnp.concatenate([count_near >> 6, count_near & 63, jnp.zeros((width - 4 * part,), jnp.int32)])
-    line = jnp.pad(line.astype(bf16)[None, :], ((0, 15), (0, 0)))
-    near_pair = pair(jnp.concatenate([near, line], 0))
+    def specs(scalars, arrays):
+        return [pl.BlockSpec(memory_space=pltpu.SMEM)] * scalars + [pl.BlockSpec(memory_space=pltpu.VMEM)] * arrays
+
+    where = jnp.stack([me, lane]).astype(jnp.int32)
+    count_line = counts.reshape(1, labels)
+    packed = pl.pallas_call(
+        pack,
+        out_shape=shape((labels // 2 + 16, width), bf16),
+        in_specs=specs(1, 2),
+        cost_estimate=cost(0, labels * width * 3),
+        compiler_params=ROOM,
+        name="pack",
+    )(where, weights, count_line)
+    near_pair = pair(packed)
     q2, q3, q1 = swap(queries, 2), swap(queries, 3), swap(queries, 1)
     far_pair = core(near_pair)
-
-    def carried(x):
-        digits = x[2 * part, : 4 * part].astype(jnp.int32)
-        return digits[: 2 * part] * 64 + digits[2 * part :]
-
-    count_held = jnp.concatenate([count_near, carried(near_pair), count_far, carried(far_pair)])
-    logs = jnp.log(count_held.astype(f32))[:, None]
 
     match = hits[:, :, None] == jnp.arange(cluster_shard.shape[0], dtype=jnp.int32)[None, None, :]
     owner = jnp.sum(jnp.where(match, cluster_shard[None, None, :], 0), axis=2)
@@ -248,29 +287,34 @@
     target = owner[:, 0] * labels + positive_offset
     meta = jnp.pad(jnp.stack([bits, target]).astype(f32), ((0, 6), (0, 0)))
 
-    held, qa, sa, stats = pl.pallas_call(
+    block_flops = 2 * (2 * labels) * (2 * rows) * width
+    score_cost = cost(block_flops, 2 * labels * (width * 2 + rows * 8), 4 * labels * rows)
+    held, qa, sa, stats, logs = pl.pallas_call(
         first_scores,
         out_shape=(
             shape((2 * labels, width), bf16),
             shape((2 * rows, width), bf16),
             shape((2 * labels, 2 * rows), f32),
             shape((8, rows), f32),
+            shape((2 * labels, 1), f32),
         ),
+        in_specs=specs(1, 6),
+        scratch_shapes=[pltpu.VMEM((labels, 8), f32)],
+        cost_estimate=score_cost,
         compiler_params=ROOM,
         name="first_scores",
-    )(queries, q1, near, near_pair, far, far_pair, logs)
+    )(where, queries, q1, weights, count_line, near_pair, far_pair)
     qb, sb, message = pl.pallas_call(
         last_scores,
         out_shape=(shape((2 * rows, width), bf16), shape((2 * labels, 2 * rows), f32), shape((24, rows), f32)),
+        cost_estimate=score_cost,
         compiler_params=ROOM,
         name="last_scores",
     )(q2, q3, held, logs, stats, meta)
 
     m3, m2, m1 = swap(message, 3), swap(message, 2), swap(message, 1)
-    where = jnp.stack([me, lane]).astype(jnp.int32)
 
     def gradient(pairing, s):
-        spec = pl.BlockSpec(memory_space=pltpu.VMEM)
         return pl.pallas_call(
             functools.partial(terms, pairing, labels),
             out_shape=(
@@ -279,7 +323,8 @@
                 shape((rows + 16, width), bf16),
                 shape((2, rows), f32),
             ),
-            in_specs=[pl.BlockSpec(memory_space=pltpu.SMEM)] + [spec] * 6,
+            in_specs=specs(1, 6),
+            cost_estimate=score_cost,
             compiler_params=ROOM,
             name="terms",
         )(where, message, m1, m2, m3, s, held)
@@ -289,6 +334,7 @@
     kept, sent = pl.pallas_call(
         label_terms,
         out_shape=(shape((labels, width), f32), shape((labels, width), bf16)),
+        cost_estimate=cost(2 * block_flops, labels * (width * 6 + rows * 16)),
         compiler_params=ROOM,
         name="label_terms",
     )(coef_a, coef_b, qa, qb)
@@ -296,10 +342,15 @@
     g3, g2, g1 = swap(t3, 3), swap(t2, 2), swap(t1, 1)
     summed = kept + arrived.astype(f32)
     sent = summed[part:].astype(bf16)
-    other = [side(sent[:part]), pair(sent[part : 2 * part]), corner(sent[2 * part :])]
-    weight_grad = (summed[:part] + sum(o.astype(f32) for o in other)).astype(bf16)
-    grads = sum(g.astype(f32) for g in (t0, g1, g2, g3))
-    return normals[0] - grads[rows, :rows], grads[:rows].astype(bf16), weight_grad
+    s0, s1, s2 = side(sent[:part]), pair(sent[part : 2 * part]), corner(sent[2 * part :])
+    loss, query_grad, weight_grad = pl.pallas_call(
+        finish,
+        out_shape=(shape((1, rows), f32), shape((rows, width), bf16), shape((part, width), bf16)),
+        cost_estimate=cost(0, 10 * rows * width + 10 * part * width),
+        compiler_params=ROOM,
+        name="finish",
+    )(normals, t0, g1, g2, g3, summed[:part], s0, s1, s2)
+    return loss[0], query_grad, weight_grad
 
 
 def solution(mesh):

time: 69.4 us -> 66.1 us (0.952)
  the two profiles are of different devices: /device:TPU:0 before, /device:TPU:8 now
where the time goes in v3:
time: 66.1 us; the launch traced here: 65.9 us
  waiting for transfers between devices  35.3 us (53%)
  starting transfers between devices  16.5 us (25%)
  Pallas kernels  8.62 us (13%)
  local copies, waits for them, and re-layouts  2.91 us (4%)
  other arithmetic  1.82 us (3%)
  between operations  0.73 us (1%)
    ppermute x9, waiting for transfers between devices, swap(): return lax.ppermute(x, 'label', [(i, i ^ 2 * k) for i in range(n)])  25.9 us
    ppermute x9, starting transfers between devices, swap(): return lax.ppermute(x, 'label', [(i, i ^ 2 * k) for i in range(n)])  11.3 us
    ppermute x2, waiting for transfers between devices, pair(): return lax.ppermute(x, 'label', [(i, i ^ 1) for i in range(n)])  7.92 us
    pallas_call x2, Pallas kernels, gradient(): pl.pallas_call(functools.partial(terms, pairing, labels), out_shape=(shap...  3.41 us
    ppermute x2, starting transfers between devices, pair(): return lax.ppermute(x, 'label', [(i, i ^ 1) for i in range(n)])  3.1 us
    unnamed x4, local copies, waits for them, and re-layouts  2.13 us
    pallas_call x1, Pallas kernels, dense_plan(): pl.pallas_call(first_scores, out_shape=(shape((2 * labels, width), bf16),...  1.59 us
    ppermute x1, starting transfers between devices, corner(): lax.ppermute(x, ('label', 'dp'), [(i * dp + j, (i ^ 1) * dp + (j ^ 2)) fo...  1.5 us
  transfers between devices with their start and end apart: 15, of which 9 were waited for; matrix products, arithmetic and copies ran while one was open for 3% of the time, Pallas kernels for 2%

profile of v3, /device:TPU:8, one launch (start us, length us, event | category | flops | bytes accessed | tf_op | source)
XLA Modules:
  0.0 65.9 jit_solution(15030819916141532206)
XLA Ops:
  0.6 0.7 %reshape.13.counts = s32[1,640]{1,0:T(1,128)S(1)} reshape(s32[640]{0:T(1024)} %param.8) | data formatting | bytes 5120 | tf_op jit(solution)/shard_map/reshape | solution.py:271
  1.4 1.2 %copy-done = bf16[640,768]{1,0:T(8,128)(2,1)S(1)} copy-done((bf16[640,768]{1,0:T(8,128)(2,1)S(1)}, bf16[640,768]{1,0:T(8,128)(2,1)}, u32[]{:S(2)}) %copy-start) | copy-done | bytes 983064
  2.6 0.6 pack.1
  3.2 1.6 %collective-permute-start.3 = (bf16[336,768]{1,0:T(8,128)(2,1)S(1)}, bf16[336,768]{1,0:T(8,128)(2,1)S(1)}, u32[]{:S(2)}, u32[]{:S(2)}) collective-permute-start(bf16[336,768]{1,0:T(8,128)(2,1)S(1)} %pack.1), channel_id=1, source_target_pairs={{0,4},{4,0},{8,12},{12,8},{16,20},{20,16},{24,28},{28,24},{1,5},{5... | collective-permute-start | bytes 1548296 | tf_op jit(solution)/shard_map/ppermute | solution.py:254
  4.8 1.6 %collective-permute-start.1 = (bf16[128,768]{1,0:T(8,128)(2,1)}, bf16[128,768]{1,0:T(8,128)(2,1)S(1)}, u32[]{:S(2)}, u32[]{:S(2)}) collective-permute-start(bf16[128,768]{1,0:T(8,128)(2,1)} %qa.1), channel_id=1, source_target_pairs={{0,24},{4,28},{8,16},{12,20},{16,8},{20,12},{24,0},{28,4},{1,25},{... | collective-permute-start | bytes 589832 | tf_op jit(solution)/shard_map/ppermute | solution.py:251
  6.4 1.2 %collective-permute-start = (bf16[128,768]{1,0:T(8,128)(2,1)}, bf16[128,768]{1,0:T(8,128)(2,1)S(1)}, u32[]{:S(2)}, u32[]{:S(2)}) collective-permute-start(bf16[128,768]{1,0:T(8,128)(2,1)} %qa.1), channel_id=1, source_target_pairs={{0,16},{4,20},{8,24},{12,28},{16,0},{20,4},{24,8},{28,12},{1,17},{... | collective-permute-start | bytes 589832 | tf_op jit(solution)/shard_map/ppermute | solution.py:251
  7.6 1.2 %collective-permute-start.2 = (bf16[128,768]{1,0:T(8,128)(2,1)}, bf16[128,768]{1,0:T(8,128)(2,1)S(1)}, u32[]{:S(2)}, u32[]{:S(2)}) collective-permute-start(bf16[128,768]{1,0:T(8,128)(2,1)} %qa.1), channel_id=1, source_target_pairs={{0,8},{4,12},{8,0},{12,4},{16,24},{20,28},{24,16},{28,20},{1,9},{5... | collective-permute-start | bytes 589832 | tf_op jit(solution)/shard_map/ppermute | solution.py:251
  8.8 7.9 %collective-permute-done.3.near_pair = bf16[336,768]{1,0:T(8,128)(2,1)S(1)} collective-permute-done((bf16[336,768]{1,0:T(8,128)(2,1)S(1)}, bf16[336,768]{1,0:T(8,128)(2,1)S(1)}, u32[]{:S(2)}, u32[]{:S(2)}) %collective-permute-start.3) | collective-permute-done | bytes 516128 | tf_op jit(solution)/shard_map/ppermute | solution.py:254
  16.7 0.8 %select_reduce_fusion = s32[128,4]{0,1:T(4,128)S(1)} fusion(s32[8]{0:T(128)} %param.11, s32[128,4]{0,1:T(4,128)} %param.9), kind=kLoop, calls=%fused_computation.1 | loop fusion | flops 11776 | bytes 4128 | tf_op jit(solution)/shard_map/reduce_sum | solution.py:285
  17.5 0.7 fusion
  18.2 3.7 %collective-permute-done.2.qb = bf16[128,768]{1,0:T(8,128)(2,1)S(1)} collective-permute-done((bf16[128,768]{1,0:T(8,128)(2,1)}, bf16[128,768]{1,0:T(8,128)(2,1)S(1)}, u32[]{:S(2)}, u32[]{:S(2)}) %collective-permute-start.2) | collective-permute-done | bytes 196640 | tf_op jit(solution)/shard_map/ppermute | solution.py:251
  21.9 0.9 %copy-done.1 = bf16[128,768]{1,0:T(8,128)(2,1)S(1)} copy-done((bf16[128,768]{1,0:T(8,128)(2,1)S(1)}, bf16[128,768]{1,0:T(8,128)(2,1)}, u32[]{:S(2)}) %copy-start.1) | copy-done | bytes 196632
  22.8 1.6 %first_scores.1 = (bf16[1280,768]{1,0:T(8,128)(2,1)S(1)}, bf16[256,768]{1,0:T(8,128)(2,1)S(1)}, f32[1280,256]{1,0:T(8,128)S(1)}, f32[8,128]{1,0:T(8,128)S(1)}, f32[1280,1]{1,0:T(8,128)S(1)}) custom-call(s32[2]{0:T(128)S(1)} %pad_add_fusion.where, bf16[128,768]{1,0:T(8,128)(2,1)S(1)} %copy-done.1, bf16[128,768]{1,0:T(8,128)(2,1)S(1)} %collective-permute-done.2.qb, ...), custom_call_target="tpu_custom_call" | custom-call | flops 503316480 | bytes 3276800 | tf_op jit(solution)/shard_map/first_scores/pallas_call | solution.py:292
  24.4 0.9 %last_scores.1 = (bf16[256,768]{1,0:T(8,128)(2,1)S(1)}, f32[1280,256]{1,0:T(8,128)S(1)}, f32[24,128]{1,0:T(8,128)S(1)}) custom-call(bf16[128,768]{1,0:T(8,128)(2,1)S(1)} %collective-permute-done.qa, bf16[128,768]{1,0:T(8,128)(2,1)S(1)} %collective-permute-done.1.qb, bf16[1280,768]{1,0:T(8,128)(2,1)S(1)} %get-tuple-element.23.held, ...), custom_call_target="tpu_custom_call" | custom-call | flops 503316480 | bytes 3276800 | tf_op jit(solution)/shard_map/last_scores/pallas_call | solution.py:307
  25.4 3.4 %collective-permute-start.6 = (f32[24,128]{1,0:T(8,128)S(1)}, f32[24,128]{1,0:T(8,128)S(1)}, u32[]{:S(2)}, u32[]{:S(2)}) collective-permute-start(f32[24,128]{1,0:T(8,128)S(1)} %get-tuple-element.26.m0), channel_id=1, source_target_pairs={{0,16},{4,20},{8,24},{12,28},{16,0},{20,4},{24,8},{28,12},{1,17},{... | collective-permute-start | bytes 36872 | tf_op jit(solution)/shard_map/ppermute | solution.py:251
  29.1 1.6 %collective-permute-done.6.m2 = f32[24,128]{1,0:T(8,128)S(1)} collective-permute-done((f32[24,128]{1,0:T(8,128)S(1)}, f32[24,128]{1,0:T(8,128)S(1)}, u32[]{:S(2)}, u32[]{:S(2)}) %collective-permute-start.6) | collective-permute-done | bytes 12320 | tf_op jit(solution)/shard_map/ppermute | solution.py:251
  30.7 1.8 %collective-permute-done.5.m1 = f32[24,128]{1,0:T(8,128)S(1)} collective-permute-done((f32[24,128]{1,0:T(8,128)S(1)}, f32[24,128]{1,0:T(8,128)S(1)}, u32[]{:S(2)}, u32[]{:S(2)}) %collective-permute-start.5) | collective-permute-done | bytes 12320 | tf_op jit(solution)/shard_map/ppermute | solution.py:251
  32.5 1.7 %terms.2 = (bf16[1280,256]{1,0:T(8,128)(2,1)S(1)}, bf16[144,768]{1,0:T(8,128)(2,1)S(1)}, bf16[144,768]{1,0:T(8,128)(2,1)S(1)}, f32[2,128]{1,0:T(2,128)S(1)}) custom-call(s32[2]{0:T(128)S(1)} %pad_add_fusion.where, f32[24,128]{1,0:T(8,128)S(1)} %get-tuple-element.26.m0, f32[24,128]{1,0:T(8,128)S(1)} %collective-permute-done.5.m1, ...), custom_call_target="tpu_custom_call" | custom-call | flops 503316480 | bytes 3276800 | tf_op jit(solution)/shard_map/terms/pallas_call | solution.py:318
  34.2 1.7 %terms.3 = (bf16[1280,256]{1,0:T(8,128)(2,1)S(1)}, bf16[144,768]{1,0:T(8,128)(2,1)S(1)}, bf16[144,768]{1,0:T(8,128)(2,1)S(1)}, f32[2,128]{1,0:T(2,128)}) custom-call(s32[2]{0:T(128)S(1)} %pad_add_fusion.where, f32[24,128]{1,0:T(8,128)S(1)} %get-tuple-element.26.m0, f32[24,128]{1,0:T(8,128)S(1)} %collective-permute-done.5.m1, ...), custom_call_target="tpu_custom_call" | custom-call | flops 503316480 | bytes 3276800 | tf_op jit(solution)/shard_map/terms/pallas_call | solution.py:318
  35.9 1.2 %label_terms.1 = (f32[640,768]{1,0:T(8,128)S(1)}, bf16[640,768]{1,0:T(8,128)(2,1)S(1)}) custom-call(bf16[1280,256]{1,0:T(8,128)(2,1)S(1)} %get-tuple-element.34.coef_a, bf16[1280,256]{1,0:T(8,128)(2,1)S(1)} %get-tuple-element.35.coef_b, bf16[256,768]{1,0:T(8,128)(2,1)S(1)} %get-tuple-element.36.qa, bf16[256,768]{1,0:T(8,128)(2,1)S(1)} %get-tuple-element.37.qb), custom_call_target="tpu_custom_call" | custom-call | flops 1006632960 | bytes 4259840 | tf_op jit(solution)/shard_map/label_terms/pallas_call | solution.py:334
  37.2 1.1 %collective-permute-start.8 = (bf16[144,768]{1,0:T(8,128)(2,1)S(1)}, bf16[144,768]{1,0:T(8,128)(2,1)S(1)}, u32[]{:S(2)}, u32[]{:S(2)}) collective-permute-start(bf16[144,768]{1,0:T(8,128)(2,1)S(1)} %get-tuple-element.30), channel_id=1, source_target_pairs={{0,8},{4,12},{8,0},{12,4},{16,24},{20,28},{24,16},{28,20},{1,9},{5... | collective-permute-start | bytes 663560 | tf_op jit(solution)/shard_map/ppermute | solution.py:251
  38.3 1.5 %collective-permute-done.11 = bf16[640,768]{1,0:T(8,128)(2,1)S(1)} collective-permute-done((bf16[640,768]{1,0:T(8,128)(2,1)S(1)}, bf16[640,768]{1,0:T(8,128)(2,1)S(1)}, u32[]{:S(2)}, u32[]{:S(2)}) %collective-permute-start.11) | collective-permute-done | bytes 983072 | tf_op jit(solution)/shard_map/ppermute | solution.py:257
  39.8 0.3 fusion.1
  40.1 1.5 %collective-permute-start.14 = (bf16[160,768]{1,0:T(8,128)(2,1)S(1)}, bf16[160,768]{1,0:T(8,128)(2,1)S(1)}, u32[]{:S(2)}, u32[]{:S(2)}) collective-permute-start(bf16[160,768]{1,0:T(8,128)(2,1)S(1)} %get-tuple-element.45), channel_id=1, source_target_pairs={{0,6},{1,7},{2,4},{3,5},{4,2},{5,3},{6,0},{7,1},{8,14},{9,15},{10,... | collective-permute-start | bytes 737288 | tf_op jit(solution)/shard_map/ppermute | solution.py:263
  41.6 1.5 %collective-permute-start.13 = (bf16[160,768]{1,0:T(8,128)(2,1)S(1)}, bf16[160,768]{1,0:T(8,128)(2,1)S(1)}, u32[]{:S(2)}, u32[]{:S(2)}) collective-permute-start(bf16[160,768]{1,0:T(8,128)(2,1)S(1)} %get-tuple-element.46), channel_id=1, source_target_pairs={{0,4},{4,0},{8,12},{12,8},{16,20},{20,16},{24,28},{28,24},{1,5},{5... | collective-permute-start | bytes 737288 | tf_op jit(solution)/shard_map/ppermute | solution.py:254
  43.1 0.5 collective-permute-start.12
  43.7 1.0 %collective-permute-start.9 = (bf16[144,768]{1,0:T(8,128)(2,1)S(1)}, bf16[144,768]{1,0:T(8,128)(2,1)S(1)}, u32[]{:S(2)}, u32[]{:S(2)}) collective-permute-start(bf16[144,768]{1,0:T(8,128)(2,1)S(1)} %get-tuple-element.32), channel_id=1, source_target_pairs={{0,16},{4,20},{8,24},{12,28},{16,0},{20,4},{24,8},{28,12},{1,17},{... | collective-permute-start | bytes 663560 | tf_op jit(solution)/shard_map/ppermute | solution.py:251
  44.7 0.4 collective-permute-done.8.t1
  45.1 1.6 %collective-permute-start.10 = (bf16[144,768]{1,0:T(8,128)(2,1)S(1)}, bf16[144,768]{1,0:T(8,128)(2,1)S(1)}, u32[]{:S(2)}, u32[]{:S(2)}) collective-permute-start(bf16[144,768]{1,0:T(8,128)(2,1)S(1)} %get-tuple-element.33), channel_id=1, source_target_pairs={{0,24},{4,28},{8,16},{12,20},{16,8},{20,12},{24,0},{28,4},{1,25},{... | collective-permute-start | bytes 663560 | tf_op jit(solution)/shard_map/ppermute | solution.py:251
  46.7 13.3 %collective-permute-done.9.t2 = bf16[144,768]{1,0:T(8,128)(2,1)S(1)} collective-permute-done((bf16[144,768]{1,0:T(8,128)(2,1)S(1)}, bf16[144,768]{1,0:T(8,128)(2,1)S(1)}, u32[]{:S(2)}, u32[]{:S(2)}) %collective-permute-start.9) | collective-permute-done | bytes 221216 | tf_op jit(solution)/shard_map/ppermute | solution.py:251
  59.9 5.0 %collective-permute-done.10.t3 = bf16[144,768]{1,0:T(8,128)(2,1)S(1)} collective-permute-done((bf16[144,768]{1,0:T(8,128)(2,1)S(1)}, bf16[144,768]{1,0:T(8,128)(2,1)S(1)}, u32[]{:S(2)}, u32[]{:S(2)}) %collective-permute-start.10) | collective-permute-done | bytes 221216 | tf_op jit(solution)/shard_map/ppermute | solution.py:251
  65.0 0.9 %finish.1 = (f32[1,128]{1,0:T(1,128)}, bf16[128,768]{1,0:T(8,128)(2,1)}, bf16[160,768]{1,0:T(8,128)(2,1)}) custom-call(f32[2,128]{1,0:T(2,128)S(1)} %get-tuple-element.28.normals, bf16[144,768]{1,0:T(8,128)(2,1)S(1)} %get-tuple-element.29.t0, bf16[144,768]{1,0:T(8,128)(2,1)S(1)} %collective-permute-done.8.t1, ...), custom_call_target="tpu_custom_call" | custom-call | bytes 2211840 | tf_op jit(solution)/shard_map/finish/pallas_call | solution.py:346
  (19 shorter events, 0.7 us)
Async XLA Ops:
  1.4 1.2 %copy-start = (bf16[640,768]{1,0:T(8,128)(2,1)S(1)}, bf16[640,768]{1,0:T(8,128)(2,1)}, u32[]{:S(2)}) copy-start(bf16[640,768]{1,0:T(8,128)(2,1)} %weights.3) | copy-start | bytes 2949124
  3.2 13.6 %collective-permute-start.3 = (bf16[336,768]{1,0:T(8,128)(2,1)S(1)}, bf16[336,768]{1,0:T(8,128)(2,1)S(1)}, u32[]{:S(2)}, u32[]{:S(2)}) collective-permute-start(bf16[336,768]{1,0:T(8,128)(2,1)S(1)} %pack.1), channel_id=1, source_target_pairs={{0,4},{4,0},{8,12},{12,8},{16,20},{20,16},{24,28},{28,24},{1,5},{5... | collective-permute-start | bytes 1548296 | tf_op jit(solution)/shard_map/ppermute | solution.py:254
  4.8 19.6 %collective-permute-start.1 = (bf16[128,768]{1,0:T(8,128)(2,1)}, bf16[128,768]{1,0:T(8,128)(2,1)S(1)}, u32[]{:S(2)}, u32[]{:S(2)}) collective-permute-start(bf16[128,768]{1,0:T(8,128)(2,1)} %qa.1), channel_id=1, source_target_pairs={{0,24},{4,28},{8,16},{12,20},{16,8},{20,12},{24,0},{28,4},{1,25},{... | collective-permute-start | bytes 589832 | tf_op jit(solution)/shard_map/ppermute | solution.py:251
  6.4 18.1 %collective-permute-start = (bf16[128,768]{1,0:T(8,128)(2,1)}, bf16[128,768]{1,0:T(8,128)(2,1)S(1)}, u32[]{:S(2)}, u32[]{:S(2)}) collective-permute-start(bf16[128,768]{1,0:T(8,128)(2,1)} %qa.1), channel_id=1, source_target_pairs={{0,16},{4,20},{8,24},{12,28},{16,0},{20,4},{24,8},{28,12},{1,17},{... | collective-permute-start | bytes 589832 | tf_op jit(solution)/shard_map/ppermute | solution.py:251
  7.6 14.3 %collective-permute-start.2 = (bf16[128,768]{1,0:T(8,128)(2,1)}, bf16[128,768]{1,0:T(8,128)(2,1)S(1)}, u32[]{:S(2)}, u32[]{:S(2)}) collective-permute-start(bf16[128,768]{1,0:T(8,128)(2,1)} %qa.1), channel_id=1, source_target_pairs={{0,8},{4,12},{8,0},{12,4},{16,24},{20,28},{24,16},{28,20},{1,9},{5... | collective-permute-start | bytes 589832 | tf_op jit(solution)/shard_map/ppermute | solution.py:251
  16.7 5.1 %collective-permute-start.4 = (bf16[336,768]{1,0:T(8,128)(2,1)S(1)}, bf16[336,768]{1,0:T(8,128)(2,1)S(1)}, u32[]{:S(2)}, u32[]{:S(2)}) collective-permute-start(bf16[336,768]{1,0:T(8,128)(2,1)S(1)} %collective-permute-done.3.near_pair), channel_id=1, source_target_pairs={{0,1},{1,0},{2,3},{3,2},{4,5},{5,4},{6,7},{7,6},{8,9},{9,8},{10,11... | collective-permute-start | bytes 1548296 | tf_op jit(solution)/shard_map/ppermute | solution.py:257
  21.9 0.9 %copy-start.1 = (bf16[128,768]{1,0:T(8,128)(2,1)S(1)}, bf16[128,768]{1,0:T(8,128)(2,1)}, u32[]{:S(2)}) copy-start(bf16[128,768]{1,0:T(8,128)(2,1)} %qa.1) | copy-start | bytes 589828
  25.4 3.8 %collective-permute-start.7 = (f32[24,128]{1,0:T(8,128)S(1)}, f32[24,128]{1,0:T(8,128)S(1)}, u32[]{:S(2)}, u32[]{:S(2)}) collective-permute-start(f32[24,128]{1,0:T(8,128)S(1)} %get-tuple-element.26.m0), channel_id=1, source_target_pairs={{0,24},{4,28},{8,16},{12,20},{16,8},{20,12},{24,0},{28,4},{1,25},{... | collective-permute-start | bytes 36872 | tf_op jit(solution)/shard_map/ppermute | solution.py:251
  25.4 5.3 %collective-permute-start.6 = (f32[24,128]{1,0:T(8,128)S(1)}, f32[24,128]{1,0:T(8,128)S(1)}, u32[]{:S(2)}, u32[]{:S(2)}) collective-permute-start(f32[24,128]{1,0:T(8,128)S(1)} %get-tuple-element.26.m0), channel_id=1, source_target_pairs={{0,16},{4,20},{8,24},{12,28},{16,0},{20,4},{24,8},{28,12},{1,17},{... | collective-permute-start | bytes 36872 | tf_op jit(solution)/shard_map/ppermute | solution.py:251
  28.8 3.7 %collective-permute-start.5 = (f32[24,128]{1,0:T(8,128)S(1)}, f32[24,128]{1,0:T(8,128)S(1)}, u32[]{:S(2)}, u32[]{:S(2)}) collective-permute-start(f32[24,128]{1,0:T(8,128)S(1)} %get-tuple-element.26.m0), channel_id=1, source_target_pairs={{0,8},{4,12},{8,0},{12,4},{16,24},{20,28},{24,16},{28,20},{1,9},{5... | collective-permute-start | bytes 36872 | tf_op jit(solution)/shard_map/ppermute | solution.py:251
  37.1 2.6 %collective-permute-start.11 = (bf16[640,768]{1,0:T(8,128)(2,1)S(1)}, bf16[640,768]{1,0:T(8,128)(2,1)S(1)}, u32[]{:S(2)}, u32[]{:S(2)}) collective-permute-start(bf16[640,768]{1,0:T(8,128)(2,1)S(1)} %get-tuple-element.39), channel_id=1, source_target_pairs={{0,1},{1,0},{2,3},{3,2},{4,5},{5,4},{6,7},{7,6},{8,9},{9,8},{10,11... | collective-permute-start | bytes 2949128 | tf_op jit(solution)/shard_map/ppermute | solution.py:257
  37.2 7.8 %collective-permute-start.8 = (bf16[144,768]{1,0:T(8,128)(2,1)S(1)}, bf16[144,768]{1,0:T(8,128)(2,1)S(1)}, u32[]{:S(2)}, u32[]{:S(2)}) collective-permute-start(bf16[144,768]{1,0:T(8,128)(2,1)S(1)} %get-tuple-element.30), channel_id=1, source_target_pairs={{0,8},{4,12},{8,0},{12,4},{16,24},{20,28},{24,16},{28,20},{1,9},{5... | collective-permute-start | bytes 663560 | tf_op jit(solution)/shard_map/ppermute | solution.py:251
  40.1 24.9 %collective-permute-start.14 = (bf16[160,768]{1,0:T(8,128)(2,1)S(1)}, bf16[160,768]{1,0:T(8,128)(2,1)S(1)}, u32[]{:S(2)}, u32[]{:S(2)}) collective-permute-start(bf16[160,768]{1,0:T(8,128)(2,1)S(1)} %get-tuple-element.45), channel_id=1, source_target_pairs={{0,6},{1,7},{2,4},{3,5},{4,2},{5,3},{6,0},{7,1},{8,14},{9,15},{10,... | collective-permute-start | bytes 737288 | tf_op jit(solution)/shard_map/ppermute | solution.py:263
  41.6 23.4 %collective-permute-start.13 = (bf16[160,768]{1,0:T(8,128)(2,1)S(1)}, bf16[160,768]{1,0:T(8,128)(2,1)S(1)}, u32[]{:S(2)}, u32[]{:S(2)}) collective-permute-start(bf16[160,768]{1,0:T(8,128)(2,1)S(1)} %get-tuple-element.46), channel_id=1, source_target_pairs={{0,4},{4,0},{8,12},{12,8},{16,20},{20,16},{24,28},{28,24},{1,5},{5... | collective-permute-start | bytes 737288 | tf_op jit(solution)/shard_map/ppermute | solution.py:254
  43.1 21.9 %collective-permute-start.12 = (bf16[160,768]{1,0:T(8,128)(2,1)S(1)}, bf16[160,768]{1,0:T(8,128)(2,1)S(1)}, u32[]{:S(2)}, u32[]{:S(2)}) collective-permute-start(bf16[160,768]{1,0:T(8,128)(2,1)S(1)} %get-tuple-element.47), channel_id=1, source_target_pairs={{0,2},{1,3},{2,0},{3,1},{4,6},{5,7},{6,4},{7,5},{8,10},{9,11},{10,... | collective-permute-start | bytes 737288 | tf_op jit(solution)/shard_map/ppermute | solution.py:260
  43.7 16.3 %collective-permute-start.9 = (bf16[144,768]{1,0:T(8,128)(2,1)S(1)}, bf16[144,768]{1,0:T(8,128)(2,1)S(1)}, u32[]{:S(2)}, u32[]{:S(2)}) collective-permute-start(bf16[144,768]{1,0:T(8,128)(2,1)S(1)} %get-tuple-element.32), channel_id=1, source_target_pairs={{0,16},{4,20},{8,24},{12,28},{16,0},{20,4},{24,8},{28,12},{1,17},{... | collective-permute-start | bytes 663560 | tf_op jit(solution)/shard_map/ppermute | solution.py:251
  45.1 19.9 %collective-permute-start.10 = (bf16[144,768]{1,0:T(8,128)(2,1)S(1)}, bf16[144,768]{1,0:T(8,128)(2,1)S(1)}, u32[]{:S(2)}, u32[]{:S(2)}) collective-permute-start(bf16[144,768]{1,0:T(8,128)(2,1)S(1)} %get-tuple-element.33), channel_id=1, source_target_pairs={{0,24},{4,28},{8,16},{12,20},{16,8},{20,12},{24,0},{28,4},{1,25},{... | collective-permute-start | bytes 663560 | tf_op jit(solution)/shard_map/ppermute | solution.py:251

commit v4 on v0

--- a/solution.py
+++ b/solution.py
@@ -1,9 +1,14 @@
+import functools
+
 import jax
 import jax.numpy as jnp
 from jax import lax
+from jax.experimental import pallas as pl
+from jax.experimental.pallas import tpu as pltpu
 from jax.sharding import PartitionSpec as P
 
 exact = lax.Precision.HIGHEST
+LOW = -1e30
 
 
 def from_slots(values, picker):
@@ -14,7 +19,7 @@
     return jnp.dot(values, picker, precision=exact)
 
 
-def local(queries, weights, counts, hits, positive_offset, cluster_shard):
+def slot_plan(queries, weights, counts, hits, positive_offset, cluster_shard):
     peer_count = lax.axis_size("label")
     row_count, top_count = hits.shape
     slot_count = 3 * row_count * top_count // 2
@@ -88,7 +93,335 @@
     return (query_loss, query_grad, weight_grad)
 
 
+FAR = 1e30
+NT = (((1,), (1,)), ((), ()))
+TN = (((0,), (0,)), ((), ()))
+ROOM = pltpu.CompilerParams(vmem_limit_bytes=20 * 1024 * 1024)
+
+
+def cost(flops, size, exps=0):
+    return pl.CostEstimate(flops=int(flops), bytes_accessed=int(size), transcendentals=int(exps))
+
+
+def named(bits, shard):
+    return (jnp.right_shift(bits, shard) & 1) == 1
+
+
+def slabs(where, labels):
+    me, lane = where[0], where[1]
+    part = labels // 4
+    for core in range(2):
+        for side in range(2):
+            for x in range(2):
+                first = (me ^ side) * labels + ((2 * x + core) ^ lane) * part
+                yield pl.ds((4 * core + 2 * side + x) * part, part), side, first
+
+
+def pieces(part):
+    unit = 2 * part // 20
+    cuts, start = [], 0
+    for size in CUTS:
+        runs, here, size = [], 0, size * unit
+        while here < size:
+            x, row = divmod(start + here, part)
+            runs.append((x, row, here, min(part - row, size - here)))
+            here += runs[-1][3]
+        cuts.append((size, runs))
+        start += size
+    return cuts
+
+
+def pack(where, weights, counts, *outs):
+    labels = weights.shape[0]
+    part = labels // 4
+    for out, (_, runs) in zip(outs, pieces(part)):
+        for x, row, here, size in runs:
+            base = pl.multiple_of((2 * x + where[1] % 2) * part + row, 16)
+            out[pl.ds(here, size), :] = weights[pl.ds(base, size), :]
+    size = pieces(part)[0][0]
+    row = lax.broadcasted_iota(jnp.int32, (16, labels), 0)
+    count = counts[...]
+    high, low = jnp.right_shift(count, 6), count & 63
+    digits = jnp.where(row == 0, high, jnp.where(row == 1, low, 0)).astype(jnp.float32)
+    outs[0][pl.ds(size, 16), :] = jnp.zeros((16, outs[0].shape[1]), jnp.bfloat16)
+    outs[0][pl.ds(size, 16), pl.ds(0, labels)] = digits.astype(jnp.bfloat16)
+
+
+def score(held, q, logs, s_ref, e_ref):
+    quarter = held.shape[0] // 4
+    peaks = []
+    for c in range(4):
+        rows = pl.ds(c * quarter, quarter)
+        s = lax.dot_general(held[rows, :], q, NT, preferred_element_type=jnp.float32) - logs[rows, :]
+        s_ref[rows, :] = s
+        peaks.append(jnp.max(s, axis=0, keepdims=True))
+    peaks = [jnp.maximum(peaks[0], peaks[2]), jnp.maximum(peaks[1], peaks[3])]
+    totals = []
+    for c in range(4):
+        rows = pl.ds(c * quarter, quarter)
+        e = jnp.exp(s_ref[rows, :] - peaks[c % 2])
+        e_ref[rows, :] = e
+        totals.append(jnp.sum(e, axis=0, keepdims=True))
+    return peaks[0], totals[0] + totals[2], peaks[1], totals[1] + totals[3]
+
+
+def first_scores(cuts, where, qa, qb, weights, counts, *refs):
+    count = len(cuts)
+    near_pair, far_pair = refs[:count], refs[count : 2 * count]
+    held, q, s_ref, e_ref, stats, logs, column = refs[2 * count :]
+    lane = where[1]
+    rows, labels = qa.shape[0], weights.shape[0]
+    part = labels // 4
+    q[pl.ds(0, rows), :] = qa[...]
+    q[pl.ds(rows, rows), :] = qb[...]
+    digits = near_pair[0][pl.ds(cuts[0][0], 16), :].astype(jnp.float32)[:, :labels]
+    lines = (counts[...].astype(jnp.float32), digits[0:1] * 64.0 + digits[1:2])
+    for side, line in enumerate(lines):
+        column[...] = jnp.transpose(jnp.broadcast_to(jnp.log(line), (8, labels)))
+        for core in range(2):
+            for x in range(2):
+                at = pl.ds((4 * core + 2 * side + x) * part, part)
+                base = pl.multiple_of(((2 * x + core) ^ lane) * part, part)
+                logs[at, :] = column[pl.ds(base, part), 0:1]
+                if not side:
+                    held[at, :] = weights[pl.ds(base, part), :]
+    for core, got in enumerate((near_pair, far_pair)):
+        for piece, (_, runs) in zip(got, cuts):
+            for x, row, here, size in runs:
+                first = pl.multiple_of((4 * core + 2 + (x ^ (lane // 2))) * part + row, 16)
+                held[pl.ds(first, size), :] = piece[pl.ds(here, size), :]
+    for i, v in enumerate(score(held, q[...], logs, s_ref, e_ref)):
+        stats[2 * i : 2 * i + 1, :] = v[:, :rows]
+        stats[2 * i + 1 : 2 * i + 2, :] = v[:, rows:]
+
+
+def last_scores(qa, qb, held, logs, stats, meta, q, s_ref, e_ref, message):
+    rows = qa.shape[0]
+    q[pl.ds(0, rows), :] = qa[...]
+    q[pl.ds(rows, rows), :] = qb[...]
+    for i, v in enumerate(score(held, q[...], logs, s_ref, e_ref)):
+        for k in range(2):
+            at, to = 2 * i + k, 4 * i + A[k]
+            message[to : to + 1, :] = stats[at : at + 1, :]
+            to = 4 * i + B[k]
+            message[to : to + 1, :] = v[:, k * rows : (k + 1) * rows]
+    message[16:24, :] = meta[...]
+
+
+def payload(term, lines, dtype):
+    rows, width = term.shape
+    lines = jnp.concatenate(lines + [jnp.zeros((8 - len(lines), rows), jnp.float32)], 0)
+    lines = jnp.concatenate([lines, jnp.zeros((8, width - rows), jnp.float32)], 1)
+    return jnp.concatenate([term, lines], 0).astype(dtype)
+
+
+def block_lines(messages, me, j):
+    bits = messages[j][16:17, :].astype(jnp.int32)
+    pairs = []
+    for k in range(4):
+        for side in range(2):
+            i = 8 * side + (j ^ k)
+            here = named(bits, (me ^ (2 * k)) ^ side)
+            pairs.append((here, messages[k][i : i + 1, :], messages[k][i + 4 : i + 5, :]))
+    peak = functools.reduce(jnp.maximum, [jnp.where(n, m, LOW) for n, m, _ in pairs])
+    total = sum(jnp.where(n, t * jnp.exp(jnp.where(n, m - peak, 0.0)), 0.0) for n, m, t in pairs)
+    normal = peak + jnp.log(total)
+    scales = [jnp.where(n, jnp.exp(jnp.where(n, m - normal, 0.0)), 0.0) for n, m, _ in pairs[:2]]
+    return [normal] + scales + [messages[j][17:18, :].astype(jnp.int32)]
+
+
+def pair_lines(messages, me, blocks):
+    return [jnp.concatenate(v, 1) for v in zip(*(block_lines(messages, me, j) for j in blocks))]
+
+
+def coefficients(blocks, labels, where, m0, m1, m2, m3, s_ref, e_ref, held, coef, last, lines):
+    rows = m0.shape[1]
+    normal, near, pair, target = pair_lines((m0, m1, m2, m3), where[0], blocks)
+    index = lax.broadcasted_iota(jnp.int32, (labels // 4, 2 * rows), 0)
+    positive = jnp.zeros((1, 2 * rows), jnp.float32)
+    for at, side, first in slabs(where, labels):
+        hot = index == target - first
+        p = e_ref[at, :] * (pair if side else near)
+        coef[at, :] = (p - jnp.where(hot, 1.0, 0.0)).astype(jnp.bfloat16)
+        positive += jnp.sum(jnp.where(hot, s_ref[at, :], 0.0), axis=0, keepdims=True)
+    lines[0:1, :] = positive
+    lines[1:2, :] = normal
+    term = lax.dot_general(coef[:, pl.ds(rows, rows)], held[...], TN, preferred_element_type=jnp.float32)
+    last[...] = payload(term, [positive[:, rows:]], last.dtype)
+
+
+def block_terms(coef, held, lines, out):
+    rows = coef.shape[1] // 2
+    term = lax.dot_general(coef[:, pl.ds(0, rows)], held[...], TN, preferred_element_type=jnp.float32)
+    positive = lines[0:1, :rows].astype(jnp.bfloat16).astype(jnp.float32)
+    if out.dtype == jnp.bfloat16:
+        out[...] = payload(term, [positive], out.dtype)
+    else:
+        out[...] = payload(term.astype(jnp.bfloat16).astype(jnp.float32), [positive, lines[1:2, :rows]], out.dtype)
+
+
+def label_terms(half, labels, where, m0, m1, m2, m3, e_a, e_b, qa, qb, out, coef):
+    rows, part = m0.shape[1], labels // 4
+    index = lax.broadcasted_iota(jnp.int32, (part, 2 * rows), 0)
+    total = None
+    for blocks, e_ref, q in ((A, e_a, qa), (B, e_b, qb)):
+        _, near, pair, target = pair_lines((m0, m1, m2, m3), where[0], blocks)
+        for i, (at, side, first) in enumerate(slabs(where, labels)):
+            if i // 4 != half:
+                continue
+            hot = jnp.where(index == target - first, 1.0, 0.0)
+            p = e_ref[at, :] * (pair if side else near)
+            coef[pl.ds((i % 4) * part, part), :] = (p - hot).astype(jnp.bfloat16)
+        term = jnp.dot(coef[...], q[...], preferred_element_type=jnp.float32)
+        total = term if total is None else total + term
+    out[...] = total.astype(out.dtype)
+
+
+A, B = (1, 2), (0, 3)
+CUTS = (7, 5, 4, 4)
+
+
+def join(a, b, out):
+    out[...] = (a[...].astype(jnp.float32) + b[...].astype(jnp.float32)).astype(out.dtype)
+
+
+def add(a, b, out):
+    out[...] = a[...] + b[...].astype(jnp.float32)
+
+
+def finish(t, g, own, s0, s1, s2, loss, query_grad, weight_grad):
+    f32 = jnp.float32
+    rows = query_grad.shape[0]
+    total = t[...] + g[...].astype(f32)
+    query_grad[...] = total[:rows].astype(query_grad.dtype)
+    loss[...] = total[rows + 1 : rows + 2, :rows] - total[rows : rows + 1, :rows]
+    total = own[...] + sum(s[...].astype(f32) for s in (s0, s1, s2))
+    weight_grad[...] = total.astype(weight_grad.dtype)
+
+
+def dense_plan(queries, weights, counts, hits, positive_offset, cluster_shard):
+    n = lax.axis_size("label")
+    dp = lax.axis_size("dp")
+    rows, width = queries.shape
+    labels = weights.shape[0]
+    part = labels // dp
+    me = lax.axis_index("label")
+    lane = lax.axis_index("dp")
+    f32, bf16 = jnp.float32, jnp.bfloat16
+    shape = jax.ShapeDtypeStruct
+
+    def swap(x, k):
+        return lax.ppermute(x, "label", [(i, i ^ (2 * k)) for i in range(n)])
+
+    def pair(x):
+        return lax.ppermute(x, "label", [(i, i ^ 1) for i in range(n)])
+
+    def core(x):
+        return lax.ppermute(x, "dp", [(i, i ^ 1) for i in range(dp)])
+
+    def side(x):
+        return lax.ppermute(x, "dp", [(i, i ^ 2) for i in range(dp)])
+
+    def corner(x):
+        return lax.ppermute(
+            x, ("label", "dp"), [(i * dp + j, (i ^ 1) * dp + (j ^ 2)) for i in range(n) for j in range(dp)]
+        )
+
+    def call(kernel, outs, scalars, arrays, flops, size, scratch=(), name=None):
+        return pl.pallas_call(
+            kernel,
+            out_shape=outs,
+            in_specs=[pl.BlockSpec(memory_space=pltpu.SMEM)] * scalars
+            + [pl.BlockSpec(memory_space=pltpu.VMEM)] * arrays,
+            scratch_shapes=list(scratch),
+            cost_estimate=cost(flops, size),
+            compiler_params=ROOM,
+            name=name,
+        )
+
+    where = jnp.stack([me, lane]).astype(jnp.int32)
+    block_flops = 2 * (2 * labels) * (2 * rows) * width
+    block_bytes = 2 * labels * (width * 2 + rows * 16)
+
+    count_line = counts.reshape(1, labels)
+    cuts = pieces(part)
+    shapes = [shape((size + (0 if i else 16), width), bf16) for i, (size, _) in enumerate(cuts)]
+    packed = call(pack, shapes, 1, 2, 0, labels * width * 2, (), "pack")(where, weights, count_line)
+    near_pair = [pair(p) for p in packed]
+    q2, q1 = swap(queries, 2), swap(queries, 1)
+
+    match = hits[:, :, None] == jnp.arange(cluster_shard.shape[0], dtype=jnp.int32)[None, None, :]
+    owner = jnp.sum(jnp.where(match, cluster_shard[None, None, :], 0), axis=2)
+    bits = jnp.sum(jnp.left_shift(1, owner), axis=1)
+    target = owner[:, 0] * labels + positive_offset
+    meta = jnp.pad(jnp.stack([bits, target]).astype(f32), ((0, 6), (0, 0)))
+
+    q3 = swap(q2, 1)
+    far_pair = [core(p) for p in near_pair]
+
+    scores = shape((2 * labels, 2 * rows), f32)
+    held, qa, sa, ea, stats, logs = call(
+        functools.partial(first_scores, cuts),
+        (shape((2 * labels, width), bf16), shape((2 * rows, width), bf16), scores, scores, shape((8, rows), f32), shape((2 * labels, 1), f32)),
+        1, 4 + 2 * len(cuts), block_flops, block_bytes, [pltpu.VMEM((labels, 8), f32)], "first_scores",
+    )(where, q1, q2, weights, count_line, *near_pair, *far_pair)
+    qb, sb, eb, message = call(
+        last_scores,
+        (shape((2 * rows, width), bf16), scores, scores, shape((24, rows), f32)),
+        0, 6, block_flops, block_bytes, (), "last_scores",
+    )(queries, q3, held, logs, stats, meta)
+
+    m3, m2, m1 = swap(message, 3), swap(message, 2), swap(message, 1)
+    term, line = shape((rows + 8, width), bf16), shape((2, 2 * rows), f32)
+
+    def coefficient(blocks, s, e):
+        return call(
+            functools.partial(coefficients, blocks, labels),
+            (shape((2 * labels, 2 * rows), bf16), term, line),
+            1, 7, block_flops // 2, block_bytes, (), "coefficients",
+        )(where, message, m1, m2, m3, s, e, held)
+
+    def block_part(coef, lines, dtype):
+        return call(block_terms, shape((rows + 8, width), dtype), 0, 3, block_flops // 2, block_bytes // 2, (), "block_terms")(coef, held, lines)
+
+    def label_part(half, dtype):
+        return call(
+            functools.partial(label_terms, half, labels),
+            shape((labels, width), dtype),
+            1, 8, block_flops, block_bytes, [pltpu.VMEM((labels, 2 * rows), bf16)], "label_terms",
+        )(where, message, m1, m2, m3, ea, eb, qa, qb)
+
+    sent, kept = label_part(1, bf16), label_part(0, f32)
+    arrived = core(sent)
+    coef_b, t3, lines_b = coefficient(B, sb, eb)
+    g3 = swap(t3, 1)
+    coef_a, t2, lines_a = coefficient(A, sa, ea)
+    t1 = block_part(coef_a, lines_a, bf16)
+    t0 = block_part(coef_b, lines_b, f32)
+    joined = call(join, term, 0, 2, 0, rows * width * 6, (), "join")(t2, g3)
+    joined, t1 = lax.optimization_barrier((joined, t1))
+    g1, g2 = swap(t1, 1), swap(joined, 2)
+    summed = kept + arrived.astype(f32)
+    sent = summed[part:].astype(bf16)
+    s0, s1, s2 = side(sent[:part]), pair(sent[part : 2 * part]), corner(sent[2 * part :])
+    both = call(add, shape((rows + 8, width), f32), 0, 2, 0, rows * width * 10, (), "add")(t0, g2)
+    loss, query_grad, weight_grad = call(
+        finish,
+        (shape((1, rows), f32), shape((rows, width), bf16), shape((part, width), bf16)),
+        0, 6, 0, 10 * (rows + part) * width, (), "finish",
+    )(both, g1, summed[:part], s0, s1, s2)
+    return loss[0], query_grad, weight_grad
+
+
 def solution(mesh):
+    n, dp = mesh.shape["label"], mesh.shape["dp"]
+
+    def local(queries, weights, counts, hits, positive_offset, cluster_shard):
+        rows, top = hits.shape
+        args = (queries, weights, counts, hits, positive_offset, cluster_shard)
+        dense = n == 8 and dp == 4 and weights.shape[0] % 640 == 0 and (n // 2) * rows <= 3 * rows * top // 2
+        return dense_plan(*args) if dense else slot_plan(*args)
+
     return jax.shard_map(
         local,
         mesh=mesh,

time: 158 us -> 57.4 us (0.36)
  blocking collectives: 34 us -> 0 us
  waiting for transfers between devices: 52.6 us -> 18.6 us
  matrix products: 17 us -> 0 us
  between operations: 14.2 us -> 0.8 us
  Pallas kernels: 0 us -> 10.5 us
  other arithmetic: 8.83 us -> 1.87 us
  local copies, waits for them, and re-layouts: 6.29 us -> 1.98 us
    all_to_all x6 -> x0, waiting for transfers between devices: 52.2 us -> none  [the longest x1 28.1 us: local(): lax.all_to_all(outgoing, 'label', split_axis=0, concat_axis=0, tiled=True)]
    all_to_all x2 -> x0, blocking collectives: 34 us -> none  [the longest x1 25.2 us: local(): lax.all_to_all(slot_grad, 'label', split_axis=0, concat_axis=0, tiled=True)]
    all_to_all x6 -> x0, starting transfers between devices: 24.5 us -> none  [the longest x1 7.28 us: local(): lax.all_to_all(outgoing, 'label', split_axis=0, concat_axis=0, tiled=True)]
    ppermute x0 -> x21, starting transfers between devices: none -> 23.5 us  [the longest x9 14.1 us: swap(): return lax.ppermute(x, 'label', [(i, i ^ 2 * k) for i in range(n)])]
    ppermute x0 -> x21, waiting for transfers between devices: none -> 18.6 us  [the longest x9 11.7 us: swap(): return lax.ppermute(x, 'label', [(i, i ^ 2 * k) for i in range(n)])]
    dot_general x11 -> x0, matrix products: 17 us -> none  [the longest x3 3.95 us: to_slots(): return jnp.dot(values, picker, precision=exact)]
    pallas_call x0 -> x12, Pallas kernels: none -> 10.5 us  [the longest x2 2.8 us: coefficient(): call(functools.partial(coefficients, blocks, labels), (shape((2 * labels,...]
    all_to_all x6 -> x0, other arithmetic: 3.55 us -> none  [the longest x1 0.7 us: local(): lax.all_to_all(target_slots, 'label', split_axis=0, concat_axis=0, tiled=...]
  transfers between devices with their start and end apart: 7 -> 21, of which waited for: 7 -> 9; matrix products, arithmetic and copies ran while one was open for 6% -> 5% of each run, Pallas kernels for 0% -> 13%
where the time goes in v4:
time: 57.4 us; the launch traced here: 57.2 us
  starting transfers between devices  23.5 us (41%)
  waiting for transfers between devices  18.6 us (32%)
  Pallas kernels  10.5 us (18%)
  local copies, waits for them, and re-layouts  1.98 us (3%)
  other arithmetic  1.87 us (3%)
  between operations  0.8 us (1%)
    ppermute x9, starting transfers between devices, swap(): return lax.ppermute(x, 'label', [(i, i ^ 2 * k) for i in range(n)])  14.1 us
    ppermute x9, waiting for transfers between devices, swap(): return lax.ppermute(x, 'label', [(i, i ^ 2 * k) for i in range(n)])  11.7 us
    ppermute x5, waiting for transfers between devices, pair(): return lax.ppermute(x, 'label', [(i, i ^ 1) for i in range(n)])  5.98 us
    ppermute x5, starting transfers between devices, pair(): return lax.ppermute(x, 'label', [(i, i ^ 1) for i in range(n)])  5.97 us
    pallas_call x2, Pallas kernels, coefficient(): call(functools.partial(coefficients, blocks, labels), (shape((2 * labels,...  2.8 us
    pallas_call x2, Pallas kernels, label_part(): call(functools.partial(label_terms, half, labels), shape((labels, width),...  2.55 us
    ppermute x1, starting transfers between devices, corner(): lax.ppermute(x, ('label', 'dp'), [(i * dp + j, (i ^ 1) * dp + (j ^ 2)) fo...  2.32 us
    pallas_call x1, Pallas kernels, dense_plan(): call(functools.partial(first_scores, cuts), (shape((2 * labels, width), b...  1.7 us
  transfers between devices with their start and end apart: 21, of which 9 were waited for; matrix products, arithmetic and copies ran while one was open for 5% of the time, Pallas kernels for 13%

profile of v4, /device:TPU:0, one launch (start us, length us, event | category | flops | bytes accessed | tf_op | source)
XLA Modules:
  0.0 57.2 jit_solution(1414759797151257233)
XLA Ops:
  0.6 4.1 %collective-permute-start = (bf16[128,768]{1,0:T(8,128)(2,1)}, bf16[128,768]{1,0:T(8,128)(2,1)S(1)}, u32[]{:S(2)}, u32[]{:S(2)}) collective-permute-start(bf16[128,768]{1,0:T(8,128)(2,1)} %qa.1), channel_id=1, source_target_pairs={{0,16},{4,20},{8,24},{12,28},{16,0},{20,4},{24,8},{28,12},{1,17},{... | collective-permute-start | bytes 589832 | tf_op jit(solution)/shard_map/ppermute | solution.py:314
  4.7 1.6 %collective-permute-start.2 = (bf16[128,768]{1,0:T(8,128)(2,1)}, bf16[128,768]{1,0:T(8,128)(2,1)S(1)}, u32[]{:S(2)}, u32[]{:S(2)}) collective-permute-start(bf16[128,768]{1,0:T(8,128)(2,1)} %qa.1), channel_id=1, source_target_pairs={{0,8},{4,12},{8,0},{12,4},{16,24},{20,28},{24,16},{28,20},{1,9},{5... | collective-permute-start | bytes 589832 | tf_op jit(solution)/shard_map/ppermute | solution.py:314
  6.3 0.7 %reshape.13.counts = s32[1,640]{1,0:T(1,128)S(1)} reshape(s32[640]{0:T(1024)} %param.8) | data formatting | bytes 5120 | tf_op jit(solution)/shard_map/reshape | solution.py:346
  7.1 1.2 %copy-done = bf16[640,768]{1,0:T(8,128)(2,1)S(1)} copy-done((bf16[640,768]{1,0:T(8,128)(2,1)S(1)}, bf16[640,768]{1,0:T(8,128)(2,1)}, u32[]{:S(2)}) %copy-start) | copy-done | bytes 983064
  8.3 0.6 %pack.1 = (bf16[128,768]{1,0:T(8,128)(2,1)S(1)}, bf16[80,768]{1,0:T(8,128)(2,1)S(1)}, bf16[64,768]{1,0:T(8,128)(2,1)S(1)}, bf16[64,768]{1,0:T(8,128)(2,1)S(1)}) custom-call(s32[2]{0:T(128)S(1)} %pad_add_fusion.where, bf16[640,768]{1,0:T(8,128)(2,1)S(1)} %copy-done, s32[1,640]{1,0:T(1,128)S(1)} %reshape.13.counts), custom_call_target="tpu_custom_call" | custom-call | bytes 983040 | tf_op jit(solution)/shard_map/pack/pallas_call | solution.py:349
  8.9 1.6 %collective-permute-start.5 = (bf16[64,768]{1,0:T(8,128)(2,1)S(1)}, bf16[64,768]{1,0:T(8,128)(2,1)S(1)}, u32[]{:S(2)}, u32[]{:S(2)}) collective-permute-start(bf16[64,768]{1,0:T(8,128)(2,1)S(1)} %get-tuple-element.30), channel_id=1, source_target_pairs={{0,4},{4,0},{8,12},{12,8},{16,20},{20,16},{24,28},{28,24},{1,5},{5... | collective-permute-start | bytes 294920 | tf_op jit(solution)/shard_map/ppermute | solution.py:317
  11.0 1.5 %collective-permute-start.3 = (bf16[128,768]{1,0:T(8,128)(2,1)S(1)}, bf16[128,768]{1,0:T(8,128)(2,1)S(1)}, u32[]{:S(2)}, u32[]{:S(2)}) collective-permute-start(bf16[128,768]{1,0:T(8,128)(2,1)S(1)} %get-tuple-element.28), channel_id=1, source_target_pairs={{0,4},{4,0},{8,12},{12,8},{16,20},{20,16},{24,28},{28,24},{1,5},{5... | collective-permute-start | bytes 589832 | tf_op jit(solution)/shard_map/ppermute | solution.py:317
  12.5 0.8 %select_reduce_fusion = s32[128,4]{0,1:T(4,128)S(1)} fusion(s32[8]{0:T(128)} %param.11, s32[128,4]{0,1:T(4,128)} %param.9), kind=kLoop, calls=%fused_computation.1 | loop fusion | flops 11776 | bytes 4128 | tf_op jit(solution)/shard_map/reduce_sum | solution.py:354
  13.3 0.7 %fusion = s32[1,128]{1,0:T(1,128)S(1)} fusion(s32[128]{0:T(128)} %param.10, s32[128,4]{0,1:T(4,128)S(1)} %select_reduce_fusion), kind=kLoop, calls=%fused_computation.7 | loop fusion | flops 256 | bytes 1536 | tf_op jit(solution)/shard_map/stack | solution.py:357
  13.9 0.6 %collective-permute-done.5.refs_2_ = bf16[64,768]{1,0:T(8,128)(2,1)S(1)} collective-permute-done((bf16[64,768]{1,0:T(8,128)(2,1)S(1)}, bf16[64,768]{1,0:T(8,128)(2,1)S(1)}, u32[]{:S(2)}, u32[]{:S(2)}) %collective-permute-start.5) | collective-permute-done | bytes 98336 | tf_op jit(solution)/shard_map/ppermute | solution.py:317
  14.5 1.7 %collective-permute-start.6 = (bf16[64,768]{1,0:T(8,128)(2,1)S(1)}, bf16[64,768]{1,0:T(8,128)(2,1)S(1)}, u32[]{:S(2)}, u32[]{:S(2)}) collective-permute-start(bf16[64,768]{1,0:T(8,128)(2,1)S(1)} %get-tuple-element.31), channel_id=1, source_target_pairs={{0,4},{4,0},{8,12},{12,8},{16,20},{20,16},{24,28},{28,24},{1,5},{5... | collective-permute-start | bytes 294920 | tf_op jit(solution)/shard_map/ppermute | solution.py:317
  16.2 1.0 %collective-permute-done.4.refs_1_ = bf16[80,768]{1,0:T(8,128)(2,1)S(1)} collective-permute-done((bf16[80,768]{1,0:T(8,128)(2,1)S(1)}, bf16[80,768]{1,0:T(8,128)(2,1)S(1)}, u32[]{:S(2)}, u32[]{:S(2)}) %collective-permute-start.4) | collective-permute-done | bytes 122912 | tf_op jit(solution)/shard_map/ppermute | solution.py:317
  17.6 3.4 %collective-permute-done.3.refs_0_ = bf16[128,768]{1,0:T(8,128)(2,1)S(1)} collective-permute-done((bf16[128,768]{1,0:T(8,128)(2,1)S(1)}, bf16[128,768]{1,0:T(8,128)(2,1)S(1)}, u32[]{:S(2)}, u32[]{:S(2)}) %collective-permute-start.3) | collective-permute-done | bytes 196640 | tf_op jit(solution)/shard_map/ppermute | solution.py:317
  21.0 1.0 %collective-permute-done.6.refs_3_ = bf16[64,768]{1,0:T(8,128)(2,1)S(1)} collective-permute-done((bf16[64,768]{1,0:T(8,128)(2,1)S(1)}, bf16[64,768]{1,0:T(8,128)(2,1)S(1)}, u32[]{:S(2)}, u32[]{:S(2)}) %collective-permute-start.6) | collective-permute-done | bytes 98336 | tf_op jit(solution)/shard_map/ppermute | solution.py:317
  22.6 0.8 %collective-permute-done.9.refs_6_ = bf16[64,768]{1,0:T(8,128)(2,1)S(1)} collective-permute-done((bf16[64,768]{1,0:T(8,128)(2,1)S(1)}, bf16[64,768]{1,0:T(8,128)(2,1)S(1)}, u32[]{:S(2)}, u32[]{:S(2)}) %collective-permute-start.9) | collective-permute-done | bytes 98336 | tf_op jit(solution)/shard_map/ppermute | solution.py:320
  23.5 1.7 %first_scores.1 = (bf16[1280,768]{1,0:T(8,128)(2,1)S(1)}, bf16[256,768]{1,0:T(8,128)(2,1)S(1)}, f32[1280,256]{1,0:T(8,128)S(1)}, f32[1280,256]{1,0:T(8,128)S(1)}...) custom-call(s32[2]{0:T(128)S(1)} %pad_add_fusion.where, bf16[128,768]{1,0:T(8,128)(2,1)S(1)} %collective-permute-done.2.qa, ...), custom_call_target="tpu_custom_call" | custom-call | flops 503316480 | bytes 4587520 | tf_op jit(solution)/shard_map/first_scores/pallas_call | solution.py:363
  25.2 1.0 %last_scores.1 = (bf16[256,768]{1,0:T(8,128)(2,1)S(1)}, f32[1280,256]{1,0:T(8,128)S(1)}, f32[1280,256]{1,0:T(8,128)S(1)}, f32[24,128]{1,0:T(8,128)S(1)}) custom-call(bf16[128,768]{1,0:T(8,128)(2,1)S(1)} %copy-done.1, bf16[128,768]{1,0:T(8,128)(2,1)S(1)} %collective-permute-done.1.qb, bf16[1280,768]{1,0:T(8,128)(2,1)S(1)} %get-tuple-element.32.held, ...), custom_call_target="tpu_custom_call" | custom-call | flops 503316480 | bytes 4587520 | tf_op jit(solution)/shard_map/last_scores/pallas_call | solution.py:368
  26.5 1.7 %collective-permute-start.12 = (f32[24,128]{1,0:T(8,128)S(1)}, f32[24,128]{1,0:T(8,128)S(1)}, u32[]{:S(2)}, u32[]{:S(2)}) collective-permute-start(f32[24,128]{1,0:T(8,128)S(1)} %get-tuple-element.35.m0), channel_id=1, source_target_pairs={{0,16},{4,20},{8,24},{12,28},{16,0},{20,4},{24,8},{28,12},{1,17},{... | collective-permute-start | bytes 36872 | tf_op jit(solution)/shard_map/ppermute | solution.py:314
  28.2 2.5 %collective-permute-start.11 = (f32[24,128]{1,0:T(8,128)S(1)}, f32[24,128]{1,0:T(8,128)S(1)}, u32[]{:S(2)}, u32[]{:S(2)}) collective-permute-start(f32[24,128]{1,0:T(8,128)S(1)} %get-tuple-element.35.m0), channel_id=1, source_target_pairs={{0,8},{4,12},{8,0},{12,4},{16,24},{20,28},{24,16},{28,20},{1,9},{5... | collective-permute-start | bytes 36872 | tf_op jit(solution)/shard_map/ppermute | solution.py:314
  30.7 1.1 %collective-permute-done.13.m3 = f32[24,128]{1,0:T(8,128)S(1)} collective-permute-done((f32[24,128]{1,0:T(8,128)S(1)}, f32[24,128]{1,0:T(8,128)S(1)}, u32[]{:S(2)}, u32[]{:S(2)}) %collective-permute-start.13) | collective-permute-done | bytes 12320 | tf_op jit(solution)/shard_map/ppermute | solution.py:314
  31.8 0.6 collective-permute-done.11.m1
  32.3 1.3 %label_terms.3 = bf16[640,768]{1,0:T(8,128)(2,1)S(1)} custom-call(s32[2]{0:T(128)S(1)} %pad_add_fusion.where, f32[24,128]{1,0:T(8,128)S(1)} %get-tuple-element.35.m0, f32[24,128]{1,0:T(8,128)S(1)} %collective-permute-done.11.m1, f32[24,128]{1,0:T(8,128)S(1)} %collective-permute-done.12.m2, f32[24,128]{1,0:T(8,128)S(1)} %collective-permute-done.13.m3, ...), custom_call_target="tpu_custom_call" | custom-call | flops 503316480 | bytes 4587520 | tf_op jit(solution)/shard_map/label_terms/pallas_call | solution.py:388
  33.7 1.4 %coefficients.2 = (bf16[1280,256]{1,0:T(8,128)(2,1)S(1)}, bf16[136,768]{1,0:T(8,128)(2,1)S(1)}, f32[2,256]{1,0:T(2,128)S(1)}) custom-call(s32[2]{0:T(128)S(1)} %pad_add_fusion.where, f32[24,128]{1,0:T(8,128)S(1)} %get-tuple-element.35.m0, f32[24,128]{1,0:T(8,128)S(1)} %collective-permute-done.11.m1, f32[24,128]{1,0:T(8,128)S(1)} %collective-permute-done.12.m2, ...), custom_call_target="tpu_custom_call" | custom-call | flops 251658240 | bytes 4587520 | tf_op jit(solution)/shard_map/coefficients/pallas_call | solution.py:378
  35.1 2.1 %collective-permute-start.14 = (bf16[136,768]{1,0:T(8,128)(2,1)S(1)}, bf16[136,768]{1,0:T(8,128)(2,1)S(1)}, u32[]{:S(2)}, u32[]{:S(2)}) collective-permute-start(bf16[136,768]{1,0:T(8,128)(2,1)S(1)} %get-tuple-element.43), channel_id=1, source_target_pairs={{0,8},{4,12},{8,0},{12,4},{16,24},{20,28},{24,16},{28,20},{1,9},{5... | collective-permute-start | bytes 626696 | tf_op jit(solution)/shard_map/ppermute | solution.py:314
  37.2 1.3 %label_terms.2 = f32[640,768]{1,0:T(8,128)S(1)} custom-call(s32[2]{0:T(128)S(1)} %pad_add_fusion.where, f32[24,128]{1,0:T(8,128)S(1)} %get-tuple-element.35.m0, f32[24,128]{1,0:T(8,128)S(1)} %collective-permute-done.11.m1, f32[24,128]{1,0:T(8,128)S(1)} %collective-permute-done.12.m2, f32[24,128]{1,0:T(8,128)S(1)} %collective-permute-done.13.m3, ...), custom_call_target="tpu_custom_call" | custom-call | flops 503316480 | bytes 4587520 | tf_op jit(solution)/shard_map/label_terms/pallas_call | solution.py:388
  38.9 2.3 %collective-permute-start.20 = (bf16[160,768]{1,0:T(8,128)(2,1)S(1)}, bf16[160,768]{1,0:T(8,128)(2,1)S(1)}, u32[]{:S(2)}, u32[]{:S(2)}) collective-permute-start(bf16[160,768]{1,0:T(8,128)(2,1)S(1)} %get-tuple-element.55), channel_id=1, source_target_pairs={{0,6},{1,7},{2,4},{3,5},{4,2},{5,3},{6,0},{7,1},{8,14},{9,15},{10,... | collective-permute-start | bytes 737288 | tf_op jit(solution)/shard_map/ppermute | solution.py:326
  41.2 0.7 %collective-permute-start.19 = (bf16[160,768]{1,0:T(8,128)(2,1)S(1)}, bf16[160,768]{1,0:T(8,128)(2,1)S(1)}, u32[]{:S(2)}, u32[]{:S(2)}) collective-permute-start(bf16[160,768]{1,0:T(8,128)(2,1)S(1)} %get-tuple-element.56), channel_id=1, source_target_pairs={{0,4},{4,0},{8,12},{12,8},{16,20},{20,16},{24,28},{28,24},{1,5},{5... | collective-permute-start | bytes 737288 | tf_op jit(solution)/shard_map/ppermute | solution.py:317
  41.9 0.5 collective-permute-start.18
  42.4 1.4 %coefficients.3 = (bf16[1280,256]{1,0:T(8,128)(2,1)S(1)}, bf16[136,768]{1,0:T(8,128)(2,1)S(1)}, f32[2,256]{1,0:T(2,128)S(1)}) custom-call(s32[2]{0:T(128)S(1)} %pad_add_fusion.where, f32[24,128]{1,0:T(8,128)S(1)} %get-tuple-element.35.m0, f32[24,128]{1,0:T(8,128)S(1)} %collective-permute-done.11.m1, f32[24,128]{1,0:T(8,128)S(1)} %collective-permute-done.12.m2, ...), custom_call_target="tpu_custom_call" | custom-call | flops 251658240 | bytes 4587520 | tf_op jit(solution)/shard_map/coefficients/pallas_call | solution.py:378
  44.4 1.0 %collective-permute-start.15 = (bf16[136,768]{1,0:T(8,128)(2,1)S(1)}, bf16[136,768]{1,0:T(8,128)(2,1)S(1)}, u32[]{:S(2)}, u32[]{:S(2)}) collective-permute-start(bf16[136,768]{1,0:T(8,128)(2,1)S(1)} %join.1), channel_id=1, source_target_pairs={{0,16},{4,20},{8,24},{12,28},{16,0},{20,4},{24,8},{28,12},{1,17},{... | collective-permute-start | bytes 626696 | tf_op jit(solution)/shard_map/ppermute | solution.py:314
  46.2 10.0 %collective-permute-done.15.b = bf16[136,768]{1,0:T(8,128)(2,1)S(1)} collective-permute-done((bf16[136,768]{1,0:T(8,128)(2,1)S(1)}, bf16[136,768]{1,0:T(8,128)(2,1)S(1)}, u32[]{:S(2)}, u32[]{:S(2)}) %collective-permute-start.15) | collective-permute-done | bytes 208928 | tf_op jit(solution)/shard_map/ppermute | solution.py:314
  56.4 0.8 %finish.1 = (f32[1,128]{1,0:T(1,128)}, bf16[128,768]{1,0:T(8,128)(2,1)}, bf16[160,768]{1,0:T(8,128)(2,1)}) custom-call(f32[136,768]{1,0:T(8,128)S(1)} %add.20.t, bf16[136,768]{1,0:T(8,128)(2,1)S(1)} %collective-permute-done.16.g, f32[160,768]{1,0:T(8,128)S(1)} %slice.25.own, bf16[160,768]{1,0:T(8,128)(2,1)S(1)} %collective-permute-done.18.s0, ...), custom_call_target="tpu_custom_call" | custom-call | bytes 2211840 | tf_op jit(solution)/shard_map/finish/pallas_call | solution.py:408
  (36 shorter events, 4.0 us)
Async XLA Ops:
  0.6 16.5 %collective-permute-start = (bf16[128,768]{1,0:T(8,128)(2,1)}, bf16[128,768]{1,0:T(8,128)(2,1)S(1)}, u32[]{:S(2)}, u32[]{:S(2)}) collective-permute-start(bf16[128,768]{1,0:T(8,128)(2,1)} %qa.1), channel_id=1, source_target_pairs={{0,16},{4,20},{8,24},{12,28},{16,0},{20,4},{24,8},{28,12},{1,17},{... | collective-permute-start | bytes 589832 | tf_op jit(solution)/shard_map/ppermute | solution.py:314
  4.7 17.3 %collective-permute-start.2 = (bf16[128,768]{1,0:T(8,128)(2,1)}, bf16[128,768]{1,0:T(8,128)(2,1)S(1)}, u32[]{:S(2)}, u32[]{:S(2)}) collective-permute-start(bf16[128,768]{1,0:T(8,128)(2,1)} %qa.1), channel_id=1, source_target_pairs={{0,8},{4,12},{8,0},{12,4},{16,24},{20,28},{24,16},{28,20},{1,9},{5... | collective-permute-start | bytes 589832 | tf_op jit(solution)/shard_map/ppermute | solution.py:314
  7.1 1.2 %copy-start = (bf16[640,768]{1,0:T(8,128)(2,1)S(1)}, bf16[640,768]{1,0:T(8,128)(2,1)}, u32[]{:S(2)}) copy-start(bf16[640,768]{1,0:T(8,128)(2,1)} %weights.3) | copy-start | bytes 2949124
  8.3 17.0 %copy-start.1 = (bf16[128,768]{1,0:T(8,128)(2,1)S(1)}, bf16[128,768]{1,0:T(8,128)(2,1)}, u32[]{:S(2)}) copy-start(bf16[128,768]{1,0:T(8,128)(2,1)} %qa.1) | copy-start | bytes 589828
  8.9 5.7 %collective-permute-start.5 = (bf16[64,768]{1,0:T(8,128)(2,1)S(1)}, bf16[64,768]{1,0:T(8,128)(2,1)S(1)}, u32[]{:S(2)}, u32[]{:S(2)}) collective-permute-start(bf16[64,768]{1,0:T(8,128)(2,1)S(1)} %get-tuple-element.30), channel_id=1, source_target_pairs={{0,4},{4,0},{8,12},{12,8},{16,20},{20,16},{24,28},{28,24},{1,5},{5... | collective-permute-start | bytes 294920 | tf_op jit(solution)/shard_map/ppermute | solution.py:317
  10.5 6.7 %collective-permute-start.4 = (bf16[80,768]{1,0:T(8,128)(2,1)S(1)}, bf16[80,768]{1,0:T(8,128)(2,1)S(1)}, u32[]{:S(2)}, u32[]{:S(2)}) collective-permute-start(bf16[80,768]{1,0:T(8,128)(2,1)S(1)} %get-tuple-element.29), channel_id=1, source_target_pairs={{0,4},{4,0},{8,12},{12,8},{16,20},{20,16},{24,28},{28,24},{1,5},{5... | collective-permute-start | bytes 368648 | tf_op jit(solution)/shard_map/ppermute | solution.py:317
  11.0 10.0 %collective-permute-start.3 = (bf16[128,768]{1,0:T(8,128)(2,1)S(1)}, bf16[128,768]{1,0:T(8,128)(2,1)S(1)}, u32[]{:S(2)}, u32[]{:S(2)}) collective-permute-start(bf16[128,768]{1,0:T(8,128)(2,1)S(1)} %get-tuple-element.28), channel_id=1, source_target_pairs={{0,4},{4,0},{8,12},{12,8},{16,20},{20,16},{24,28},{28,24},{1,5},{5... | collective-permute-start | bytes 589832 | tf_op jit(solution)/shard_map/ppermute | solution.py:317
  14.5 7.5 %collective-permute-start.6 = (bf16[64,768]{1,0:T(8,128)(2,1)S(1)}, bf16[64,768]{1,0:T(8,128)(2,1)S(1)}, u32[]{:S(2)}, u32[]{:S(2)}) collective-permute-start(bf16[64,768]{1,0:T(8,128)(2,1)S(1)} %get-tuple-element.31), channel_id=1, source_target_pairs={{0,4},{4,0},{8,12},{12,8},{16,20},{20,16},{24,28},{28,24},{1,5},{5... | collective-permute-start | bytes 294920 | tf_op jit(solution)/shard_map/ppermute | solution.py:317
  17.2 6.4 %collective-permute-start.8 = (bf16[80,768]{1,0:T(8,128)(2,1)S(1)}, bf16[80,768]{1,0:T(8,128)(2,1)S(1)}, u32[]{:S(2)}, u32[]{:S(2)}) collective-permute-start(bf16[80,768]{1,0:T(8,128)(2,1)S(1)} %collective-permute-done.4.refs_1_), channel_id=1, source_target_pairs={{0,1},{1,0},{2,3},{3,2},{4,5},{5,4},{6,7},{7,6},{8,9},{9,8},{10,11... | collective-permute-start | bytes 368648 | tf_op jit(solution)/shard_map/ppermute | solution.py:320
  17.2 8.1 %collective-permute-start.1 = (bf16[128,768]{1,0:T(8,128)(2,1)S(1)}, bf16[128,768]{1,0:T(8,128)(2,1)S(1)}, u32[]{:S(2)}, u32[]{:S(2)}) collective-permute-start(bf16[128,768]{1,0:T(8,128)(2,1)S(1)} %collective-permute-done.qb), channel_id=1, source_target_pairs={{0,8},{4,12},{8,0},{12,4},{16,24},{20,28},{24,16},{28,20},{1,9},{5... | collective-permute-start | bytes 589832 | tf_op jit(solution)/shard_map/ppermute | solution.py:314
  21.0 2.5 %collective-permute-start.7 = (bf16[128,768]{1,0:T(8,128)(2,1)S(1)}, bf16[128,768]{1,0:T(8,128)(2,1)S(1)}, u32[]{:S(2)}, u32[]{:S(2)}) collective-permute-start(bf16[128,768]{1,0:T(8,128)(2,1)S(1)} %collective-permute-done.3.refs_0_), channel_id=1, source_target_pairs={{0,1},{1,0},{2,3},{3,2},{4,5},{5,4},{6,7},{7,6},{8,9},{9,8},{10,11... | collective-permute-start | bytes 589832 | tf_op jit(solution)/shard_map/ppermute | solution.py:320
  22.0 1.3 %collective-permute-start.9 = (bf16[64,768]{1,0:T(8,128)(2,1)S(1)}, bf16[64,768]{1,0:T(8,128)(2,1)S(1)}, u32[]{:S(2)}, u32[]{:S(2)}) collective-permute-start(bf16[64,768]{1,0:T(8,128)(2,1)S(1)} %collective-permute-done.5.refs_2_), channel_id=1, source_target_pairs={{0,1},{1,0},{2,3},{3,2},{4,5},{5,4},{6,7},{7,6},{8,9},{9,8},{10,11... | collective-permute-start | bytes 294920 | tf_op jit(solution)/shard_map/ppermute | solution.py:320
  22.1 1.5 %collective-permute-start.10 = (bf16[64,768]{1,0:T(8,128)(2,1)S(1)}, bf16[64,768]{1,0:T(8,128)(2,1)S(1)}, u32[]{:S(2)}, u32[]{:S(2)}) collective-permute-start(bf16[64,768]{1,0:T(8,128)(2,1)S(1)} %collective-permute-done.6.refs_3_), channel_id=1, source_target_pairs={{0,1},{1,0},{2,3},{3,2},{4,5},{5,4},{6,7},{7,6},{8,9},{9,8},{10,11... | collective-permute-start | bytes 294920 | tf_op jit(solution)/shard_map/ppermute | solution.py:320
  26.2 5.6 %collective-permute-start.13 = (f32[24,128]{1,0:T(8,128)S(1)}, f32[24,128]{1,0:T(8,128)S(1)}, u32[]{:S(2)}, u32[]{:S(2)}) collective-permute-start(f32[24,128]{1,0:T(8,128)S(1)} %get-tuple-element.35.m0), channel_id=1, source_target_pairs={{0,24},{4,28},{8,16},{12,20},{16,8},{20,12},{24,0},{28,4},{1,25},{... | collective-permute-start | bytes 36872 | tf_op jit(solution)/shard_map/ppermute | solution.py:314
  26.5 5.3 %collective-permute-start.12 = (f32[24,128]{1,0:T(8,128)S(1)}, f32[24,128]{1,0:T(8,128)S(1)}, u32[]{:S(2)}, u32[]{:S(2)}) collective-permute-start(f32[24,128]{1,0:T(8,128)S(1)} %get-tuple-element.35.m0), channel_id=1, source_target_pairs={{0,16},{4,20},{8,24},{12,28},{16,0},{20,4},{24,8},{28,12},{1,17},{... | collective-permute-start | bytes 36872 | tf_op jit(solution)/shard_map/ppermute | solution.py:314
  28.2 4.2 %collective-permute-start.11 = (f32[24,128]{1,0:T(8,128)S(1)}, f32[24,128]{1,0:T(8,128)S(1)}, u32[]{:S(2)}, u32[]{:S(2)}) collective-permute-start(f32[24,128]{1,0:T(8,128)S(1)} %get-tuple-element.35.m0), channel_id=1, source_target_pairs={{0,8},{4,12},{8,0},{12,4},{16,24},{20,28},{24,16},{28,20},{1,9},{5... | collective-permute-start | bytes 36872 | tf_op jit(solution)/shard_map/ppermute | solution.py:314
  33.6 4.9 %collective-permute-start.17 = (bf16[640,768]{1,0:T(8,128)(2,1)S(1)}, bf16[640,768]{1,0:T(8,128)(2,1)S(1)}, u32[]{:S(2)}, u32[]{:S(2)}) collective-permute-start(bf16[640,768]{1,0:T(8,128)(2,1)S(1)} %label_terms.3), channel_id=1, source_target_pairs={{0,1},{1,0},{2,3},{3,2},{4,5},{5,4},{6,7},{7,6},{8,9},{9,8},{10,11... | collective-permute-start | bytes 2949128 | tf_op jit(solution)/shard_map/ppermute | solution.py:320
  35.1 9.2 %collective-permute-start.14 = (bf16[136,768]{1,0:T(8,128)(2,1)S(1)}, bf16[136,768]{1,0:T(8,128)(2,1)S(1)}, u32[]{:S(2)}, u32[]{:S(2)}) collective-permute-start(bf16[136,768]{1,0:T(8,128)(2,1)S(1)} %get-tuple-element.43), channel_id=1, source_target_pairs={{0,8},{4,12},{8,0},{12,4},{16,24},{20,28},{24,16},{28,20},{1,9},{5... | collective-permute-start | bytes 626696 | tf_op jit(solution)/shard_map/ppermute | solution.py:314
  38.9 17.5 %collective-permute-start.20 = (bf16[160,768]{1,0:T(8,128)(2,1)S(1)}, bf16[160,768]{1,0:T(8,128)(2,1)S(1)}, u32[]{:S(2)}, u32[]{:S(2)}) collective-permute-start(bf16[160,768]{1,0:T(8,128)(2,1)S(1)} %get-tuple-element.55), channel_id=1, source_target_pairs={{0,6},{1,7},{2,4},{3,5},{4,2},{5,3},{6,0},{7,1},{8,14},{9,15},{10,... | collective-permute-start | bytes 737288 | tf_op jit(solution)/shard_map/ppermute | solution.py:326
  41.2 15.2 %collective-permute-start.19 = (bf16[160,768]{1,0:T(8,128)(2,1)S(1)}, bf16[160,768]{1,0:T(8,128)(2,1)S(1)}, u32[]{:S(2)}, u32[]{:S(2)}) collective-permute-start(bf16[160,768]{1,0:T(8,128)(2,1)S(1)} %get-tuple-element.56), channel_id=1, source_target_pairs={{0,4},{4,0},{8,12},{12,8},{16,20},{20,16},{24,28},{28,24},{1,5},{5... | collective-permute-start | bytes 737288 | tf_op jit(solution)/shard_map/ppermute | solution.py:317
  41.9 14.5 %collective-permute-start.18 = (bf16[160,768]{1,0:T(8,128)(2,1)S(1)}, bf16[160,768]{1,0:T(8,128)(2,1)S(1)}, u32[]{:S(2)}, u32[]{:S(2)}) collective-permute-start(bf16[160,768]{1,0:T(8,128)(2,1)S(1)} %get-tuple-element.57), channel_id=1, source_target_pairs={{0,2},{1,3},{2,0},{3,1},{4,6},{5,7},{6,4},{7,5},{8,10},{9,11},{10,... | collective-permute-start | bytes 737288 | tf_op jit(solution)/shard_map/ppermute | solution.py:323
  44.4 11.9 %collective-permute-start.15 = (bf16[136,768]{1,0:T(8,128)(2,1)S(1)}, bf16[136,768]{1,0:T(8,128)(2,1)S(1)}, u32[]{:S(2)}, u32[]{:S(2)}) collective-permute-start(bf16[136,768]{1,0:T(8,128)(2,1)S(1)} %join.1), channel_id=1, source_target_pairs={{0,16},{4,20},{8,24},{12,28},{16,0},{20,4},{24,8},{28,12},{1,17},{... | collective-permute-start | bytes 626696 | tf_op jit(solution)/shard_map/ppermute | solution.py:314
  45.3 11.0 %collective-permute-start.16 = (bf16[136,768]{1,0:T(8,128)(2,1)S(1)}, bf16[136,768]{1,0:T(8,128)(2,1)S(1)}, u32[]{:S(2)}, u32[]{:S(2)}) collective-permute-start(bf16[136,768]{1,0:T(8,128)(2,1)S(1)} %block_terms.3), channel_id=1, source_target_pairs={{0,8},{4,12},{8,0},{12,4},{16,24},{20,28},{24,16},{28,20},{1,9},{5... | collective-permute-start | bytes 626696 | tf_op jit(solution)/shard_map/ppermute | solution.py:314

commit v5 on v4

--- a/solution.py
+++ b/solution.py
@@ -278,7 +278,7 @@
 
 
 A, B = (1, 2), (0, 3)
-CUTS = (7, 5, 4, 4)
+CUTS = (8, 6, 6)
 
 
 def join(a, b, out):
@@ -348,7 +348,8 @@
     shapes = [shape((size + (0 if i else 16), width), bf16) for i, (size, _) in enumerate(cuts)]
     packed = call(pack, shapes, 1, 2, 0, labels * width * 2, (), "pack")(where, weights, count_line)
     near_pair = [pair(p) for p in packed]
-    q2, q1 = swap(queries, 2), swap(queries, 1)
+    q2 = swap(queries, 2)
+    q1 = swap(lax.optimization_barrier((queries, near_pair[1]))[0], 1)
 
     match = hits[:, :, None] == jnp.arange(cluster_shard.shape[0], dtype=jnp.int32)[None, None, :]
     owner = jnp.sum(jnp.where(match, cluster_shard[None, None, :], 0), axis=2)

time: 57.4 us -> 56.8 us (0.990)
  starting transfers between devices: 23.5 us -> 22.4 us
    ppermute x5 -> x4, starting transfers between devices: 5.97 us -> 4.12 us  [pair(): return lax.ppermute(x, 'label', [(i, i ^ 1) for i in range(n)])]
    ppermute x9, starting transfers between devices: 14.1 us -> 15.2 us  [swap(): return lax.ppermute(x, 'label', [(i, i ^ 2 * k) for i in range(n)])]
    ppermute x5 -> x4, waiting for transfers between devices: 5.98 us -> 5.06 us  [pair(): return lax.ppermute(x, 'label', [(i, i ^ 1) for i in range(n)])]
    ppermute x9, waiting for transfers between devices: 11.7 us -> 12.6 us  [swap(): return lax.ppermute(x, 'label', [(i, i ^ 2 * k) for i in range(n)])]
    ppermute x5 -> x4, waiting for transfers between devices: 0.93 us -> 1.41 us  [core(): return lax.ppermute(x, 'dp', [(i, i ^ 1) for i in range(dp)])]
  transfers between devices with their start and end apart: 21 -> 19, of which waited for: 9 -> 9; matrix products, arithmetic and copies ran while one was open for 5% -> 5% of each run, Pallas kernels for 13% -> 13%
where the time goes in v5:
time: 56.8 us; the launch traced here: 56.6 us
  starting transfers between devices  22.4 us (39%)
  waiting for transfers between devices  19.1 us (34%)
  Pallas kernels  10.4 us (18%)
  local copies, waits for them, and re-layouts  1.98 us (3%)
  other arithmetic  1.87 us (3%)
  between operations  0.81 us (1%)
    ppermute x9, starting transfers between devices, swap(): return lax.ppermute(x, 'label', [(i, i ^ 2 * k) for i in range(n)])  15.2 us
    ppermute x9, waiting for transfers between devices, swap(): return lax.ppermute(x, 'label', [(i, i ^ 2 * k) for i in range(n)])  12.6 us
    ppermute x4, waiting for transfers between devices, pair(): return lax.ppermute(x, 'label', [(i, i ^ 1) for i in range(n)])  5.06 us
    ppermute x4, starting transfers between devices, pair(): return lax.ppermute(x, 'label', [(i, i ^ 1) for i in range(n)])  4.12 us
    pallas_call x2, Pallas kernels, coefficient(): call(functools.partial(coefficients, blocks, labels), (shape((2 * labels,...  2.8 us
    pallas_call x2, Pallas kernels, label_part(): call(functools.partial(label_terms, half, labels), shape((labels, width),...  2.55 us
    ppermute x1, starting transfers between devices, corner(): lax.ppermute(x, ('label', 'dp'), [(i * dp + j, (i ^ 1) * dp + (j ^ 2)) fo...  2.52 us
    pallas_call x1, Pallas kernels, dense_plan(): call(functools.partial(first_scores, cuts), (shape((2 * labels, width), b...  1.69 us
  transfers between devices with their start and end apart: 19, of which 9 were waited for; matrix products, arithmetic and copies ran while one was open for 5% of the time, Pallas kernels for 13%

profile of v5, /device:TPU:0, one launch (start us, length us, event | category | flops | bytes accessed | tf_op | source)
XLA Modules:
  0.0 56.6 jit_solution(13764063914894993545)
XLA Ops:
  0.6 4.1 %collective-permute-start = (bf16[128,768]{1,0:T(8,128)(2,1)}, bf16[128,768]{1,0:T(8,128)(2,1)S(1)}, u32[]{:S(2)}, u32[]{:S(2)}) collective-permute-start(bf16[128,768]{1,0:T(8,128)(2,1)} %qa.1), channel_id=1, source_target_pairs={{0,16},{4,20},{8,24},{12,28},{16,0},{20,4},{24,8},{28,12},{1,17},{... | collective-permute-start | bytes 589832 | tf_op jit(solution)/shard_map/ppermute | solution.py:314
  4.7 0.7 %reshape.13.counts = s32[1,640]{1,0:T(1,128)S(1)} reshape(s32[640]{0:T(1024)} %param.8) | data formatting | bytes 5120 | tf_op jit(solution)/shard_map/reshape | solution.py:346
  5.5 1.2 %copy-done = bf16[640,768]{1,0:T(8,128)(2,1)S(1)} copy-done((bf16[640,768]{1,0:T(8,128)(2,1)S(1)}, bf16[640,768]{1,0:T(8,128)(2,1)}, u32[]{:S(2)}) %copy-start) | copy-done | bytes 983064
  6.7 0.6 %pack.1 = (bf16[144,768]{1,0:T(8,128)(2,1)S(1)}, bf16[96,768]{1,0:T(8,128)(2,1)S(1)}, bf16[96,768]{1,0:T(8,128)(2,1)S(1)}) custom-call(s32[2]{0:T(128)S(1)} %pad_add_fusion.where, bf16[640,768]{1,0:T(8,128)(2,1)S(1)} %copy-done, s32[1,640]{1,0:T(1,128)S(1)} %reshape.13.counts), custom_call_target="tpu_custom_call" | custom-call | bytes 983040 | tf_op jit(solution)/shard_map/pack/pallas_call | solution.py:349
  7.3 1.6 %collective-permute-start.2 = (bf16[96,768]{1,0:T(8,128)(2,1)S(1)}, bf16[96,768]{1,0:T(8,128)(2,1)S(1)}, u32[]{:S(2)}, u32[]{:S(2)}) collective-permute-start(bf16[96,768]{1,0:T(8,128)(2,1)S(1)} %get-tuple-element.28), channel_id=1, source_target_pairs={{0,4},{4,0},{8,12},{12,8},{16,20},{20,16},{24,28},{28,24},{1,5},{5... | collective-permute-start | bytes 442376 | tf_op jit(solution)/shard_map/ppermute | solution.py:317
  9.4 1.5 %collective-permute-start.4 = (bf16[144,768]{1,0:T(8,128)(2,1)S(1)}, bf16[144,768]{1,0:T(8,128)(2,1)S(1)}, u32[]{:S(2)}, u32[]{:S(2)}) collective-permute-start(bf16[144,768]{1,0:T(8,128)(2,1)S(1)} %get-tuple-element.30), channel_id=1, source_target_pairs={{0,4},{4,0},{8,12},{12,8},{16,20},{20,16},{24,28},{28,24},{1,5},{5... | collective-permute-start | bytes 663560 | tf_op jit(solution)/shard_map/ppermute | solution.py:317
  10.9 0.8 %select_reduce_fusion = s32[128,4]{0,1:T(4,128)S(1)} fusion(s32[8]{0:T(128)} %param.11, s32[128,4]{0,1:T(4,128)} %param.9), kind=kLoop, calls=%fused_computation.1 | loop fusion | flops 11776 | bytes 4128 | tf_op jit(solution)/shard_map/reduce_sum | solution.py:355
  11.7 0.7 %fusion = s32[1,128]{1,0:T(1,128)S(1)} fusion(s32[128]{0:T(128)} %param.10, s32[128,4]{0,1:T(4,128)S(1)} %select_reduce_fusion), kind=kLoop, calls=%fused_computation.7 | loop fusion | flops 256 | bytes 1536 | tf_op jit(solution)/shard_map/stack | solution.py:358
  12.3 1.8 %collective-permute-done.2.refs_1_ = bf16[96,768]{1,0:T(8,128)(2,1)S(1)} collective-permute-done((bf16[96,768]{1,0:T(8,128)(2,1)S(1)}, bf16[96,768]{1,0:T(8,128)(2,1)S(1)}, u32[]{:S(2)}, u32[]{:S(2)}) %collective-permute-start.2) | collective-permute-done | bytes 147488 | tf_op jit(solution)/shard_map/ppermute | solution.py:317
  14.1 1.6 %collective-permute-start.3 = (bf16[128,768]{1,0:T(8,128)(2,1)}, bf16[128,768]{1,0:T(8,128)(2,1)S(1)}, u32[]{:S(2)}, u32[]{:S(2)}) collective-permute-start(bf16[128,768]{1,0:T(8,128)(2,1)} %qa.1), channel_id=1, source_target_pairs={{0,8},{4,12},{8,0},{12,4},{16,24},{20,28},{24,16},{28,20},{1,9},{5... | collective-permute-start | bytes 589832 | tf_op jit(solution)/shard_map/ppermute | solution.py:314
  15.7 1.6 %collective-permute-done.5.refs_2_ = bf16[96,768]{1,0:T(8,128)(2,1)S(1)} collective-permute-done((bf16[96,768]{1,0:T(8,128)(2,1)S(1)}, bf16[96,768]{1,0:T(8,128)(2,1)S(1)}, u32[]{:S(2)}, u32[]{:S(2)}) %collective-permute-start.5) | collective-permute-done | bytes 147488 | tf_op jit(solution)/shard_map/ppermute | solution.py:317
  17.3 1.6 %collective-permute-start.1 = (bf16[128,768]{1,0:T(8,128)(2,1)S(1)}, bf16[128,768]{1,0:T(8,128)(2,1)S(1)}, u32[]{:S(2)}, u32[]{:S(2)}) collective-permute-start(bf16[128,768]{1,0:T(8,128)(2,1)S(1)} %collective-permute-done.qb), channel_id=1, source_target_pairs={{0,8},{4,12},{8,0},{12,4},{16,24},{20,28},{24,16},{28,20},{1,9},{5... | collective-permute-start | bytes 589832 | tf_op jit(solution)/shard_map/ppermute | solution.py:314
  18.9 1.7 %collective-permute-done.4.refs_0_ = bf16[144,768]{1,0:T(8,128)(2,1)S(1)} collective-permute-done((bf16[144,768]{1,0:T(8,128)(2,1)S(1)}, bf16[144,768]{1,0:T(8,128)(2,1)S(1)}, u32[]{:S(2)}, u32[]{:S(2)}) %collective-permute-start.4) | collective-permute-done | bytes 221216 | tf_op jit(solution)/shard_map/ppermute | solution.py:317
  20.6 1.4 %collective-permute-done.6.refs_3_ = bf16[144,768]{1,0:T(8,128)(2,1)S(1)} collective-permute-done((bf16[144,768]{1,0:T(8,128)(2,1)S(1)}, bf16[144,768]{1,0:T(8,128)(2,1)S(1)}, u32[]{:S(2)}, u32[]{:S(2)}) %collective-permute-start.6) | collective-permute-done | bytes 221216 | tf_op jit(solution)/shard_map/ppermute | solution.py:320
  22.0 1.7 %first_scores.1 = (bf16[1280,768]{1,0:T(8,128)(2,1)S(1)}, bf16[256,768]{1,0:T(8,128)(2,1)S(1)}, f32[1280,256]{1,0:T(8,128)S(1)}, f32[1280,256]{1,0:T(8,128)S(1)}...) custom-call(s32[2]{0:T(128)S(1)} %pad_add_fusion.where, bf16[128,768]{1,0:T(8,128)(2,1)S(1)} %collective-permute-done.3.qa, ...), custom_call_target="tpu_custom_call" | custom-call | flops 503316480 | bytes 4587520 | tf_op jit(solution)/shard_map/first_scores/pallas_call | solution.py:364
  23.7 0.9 %collective-permute-done.1.qb = bf16[128,768]{1,0:T(8,128)(2,1)S(1)} collective-permute-done((bf16[128,768]{1,0:T(8,128)(2,1)S(1)}, bf16[128,768]{1,0:T(8,128)(2,1)S(1)}, u32[]{:S(2)}, u32[]{:S(2)}) %collective-permute-start.1) | collective-permute-done | bytes 196640 | tf_op jit(solution)/shard_map/ppermute | solution.py:314
  24.6 1.0 %last_scores.1 = (bf16[256,768]{1,0:T(8,128)(2,1)S(1)}, f32[1280,256]{1,0:T(8,128)S(1)}, f32[1280,256]{1,0:T(8,128)S(1)}, f32[24,128]{1,0:T(8,128)S(1)}) custom-call(bf16[128,768]{1,0:T(8,128)(2,1)S(1)} %copy-done.1, bf16[128,768]{1,0:T(8,128)(2,1)S(1)} %collective-permute-done.1.qb, bf16[1280,768]{1,0:T(8,128)(2,1)S(1)} %get-tuple-element.32.held, ...), custom_call_target="tpu_custom_call" | custom-call | flops 503316480 | bytes 4587520 | tf_op jit(solution)/shard_map/last_scores/pallas_call | solution.py:369
  25.6 1.5 %collective-permute-start.11 = (f32[24,128]{1,0:T(8,128)S(1)}, f32[24,128]{1,0:T(8,128)S(1)}, u32[]{:S(2)}, u32[]{:S(2)}) collective-permute-start(f32[24,128]{1,0:T(8,128)S(1)} %get-tuple-element.35.m0), channel_id=1, source_target_pairs={{0,24},{4,28},{8,16},{12,20},{16,8},{20,12},{24,0},{28,4},{1,25},{... | collective-permute-start | bytes 36872 | tf_op jit(solution)/shard_map/ppermute | solution.py:314
  27.1 1.6 %collective-permute-start.10 = (f32[24,128]{1,0:T(8,128)S(1)}, f32[24,128]{1,0:T(8,128)S(1)}, u32[]{:S(2)}, u32[]{:S(2)}) collective-permute-start(f32[24,128]{1,0:T(8,128)S(1)} %get-tuple-element.35.m0), channel_id=1, source_target_pairs={{0,16},{4,20},{8,24},{12,28},{16,0},{20,4},{24,8},{28,12},{1,17},{... | collective-permute-start | bytes 36872 | tf_op jit(solution)/shard_map/ppermute | solution.py:314
  28.7 1.3 %collective-permute-start.9 = (f32[24,128]{1,0:T(8,128)S(1)}, f32[24,128]{1,0:T(8,128)S(1)}, u32[]{:S(2)}, u32[]{:S(2)}) collective-permute-start(f32[24,128]{1,0:T(8,128)S(1)} %get-tuple-element.35.m0), channel_id=1, source_target_pairs={{0,8},{4,12},{8,0},{12,4},{16,24},{20,28},{24,16},{28,20},{1,9},{5... | collective-permute-start | bytes 36872 | tf_op jit(solution)/shard_map/ppermute | solution.py:314
  30.0 1.1 %collective-permute-done.11.m3 = f32[24,128]{1,0:T(8,128)S(1)} collective-permute-done((f32[24,128]{1,0:T(8,128)S(1)}, f32[24,128]{1,0:T(8,128)S(1)}, u32[]{:S(2)}, u32[]{:S(2)}) %collective-permute-start.11) | collective-permute-done | bytes 12320 | tf_op jit(solution)/shard_map/ppermute | solution.py:314
  31.7 0.7 %collective-permute-done.9.m1 = f32[24,128]{1,0:T(8,128)S(1)} collective-permute-done((f32[24,128]{1,0:T(8,128)S(1)}, f32[24,128]{1,0:T(8,128)S(1)}, u32[]{:S(2)}, u32[]{:S(2)}) %collective-permute-start.9) | collective-permute-done | bytes 12320 | tf_op jit(solution)/shard_map/ppermute | solution.py:314
  32.4 1.3 %label_terms.3 = bf16[640,768]{1,0:T(8,128)(2,1)S(1)} custom-call(s32[2]{0:T(128)S(1)} %pad_add_fusion.where, f32[24,128]{1,0:T(8,128)S(1)} %get-tuple-element.35.m0, f32[24,128]{1,0:T(8,128)S(1)} %collective-permute-done.9.m1, f32[24,128]{1,0:T(8,128)S(1)} %collective-permute-done.10.m2, f32[24,128]{1,0:T(8,128)S(1)} %collective-permute-done.11.m3, ...), custom_call_target="tpu_custom_call" | custom-call | flops 503316480 | bytes 4587520 | tf_op jit(solution)/shard_map/label_terms/pallas_call | solution.py:389
  33.7 1.4 %coefficients.2 = (bf16[1280,256]{1,0:T(8,128)(2,1)S(1)}, bf16[136,768]{1,0:T(8,128)(2,1)S(1)}, f32[2,256]{1,0:T(2,128)S(1)}) custom-call(s32[2]{0:T(128)S(1)} %pad_add_fusion.where, f32[24,128]{1,0:T(8,128)S(1)} %get-tuple-element.35.m0, f32[24,128]{1,0:T(8,128)S(1)} %collective-permute-done.9.m1, f32[24,128]{1,0:T(8,128)S(1)} %collective-permute-done.10.m2, ...), custom_call_target="tpu_custom_call" | custom-call | flops 251658240 | bytes 4587520 | tf_op jit(solution)/shard_map/coefficients/pallas_call | solution.py:379
  35.1 1.4 %collective-permute-start.12 = (bf16[136,768]{1,0:T(8,128)(2,1)S(1)}, bf16[136,768]{1,0:T(8,128)(2,1)S(1)}, u32[]{:S(2)}, u32[]{:S(2)}) collective-permute-start(bf16[136,768]{1,0:T(8,128)(2,1)S(1)} %get-tuple-element.43), channel_id=1, source_target_pairs={{0,8},{4,12},{8,0},{12,4},{16,24},{20,28},{24,16},{28,20},{1,9},{5... | collective-permute-start | bytes 626696 | tf_op jit(solution)/shard_map/ppermute | solution.py:314
  36.6 1.3 %label_terms.2 = f32[640,768]{1,0:T(8,128)S(1)} custom-call(s32[2]{0:T(128)S(1)} %pad_add_fusion.where, f32[24,128]{1,0:T(8,128)S(1)} %get-tuple-element.35.m0, f32[24,128]{1,0:T(8,128)S(1)} %collective-permute-done.9.m1, f32[24,128]{1,0:T(8,128)S(1)} %collective-permute-done.10.m2, f32[24,128]{1,0:T(8,128)S(1)} %collective-permute-done.11.m3, ...), custom_call_target="tpu_custom_call" | custom-call | flops 503316480 | bytes 4587520 | tf_op jit(solution)/shard_map/label_terms/pallas_call | solution.py:389
  38.2 2.5 %collective-permute-start.18 = (bf16[160,768]{1,0:T(8,128)(2,1)S(1)}, bf16[160,768]{1,0:T(8,128)(2,1)S(1)}, u32[]{:S(2)}, u32[]{:S(2)}) collective-permute-start(bf16[160,768]{1,0:T(8,128)(2,1)S(1)} %get-tuple-element.55), channel_id=1, source_target_pairs={{0,6},{1,7},{2,4},{3,5},{4,2},{5,3},{6,0},{7,1},{8,14},{9,15},{10,... | collective-permute-start | bytes 737288 | tf_op jit(solution)/shard_map/ppermute | solution.py:326
  41.8 1.4 %coefficients.3 = (bf16[1280,256]{1,0:T(8,128)(2,1)S(1)}, bf16[136,768]{1,0:T(8,128)(2,1)S(1)}, f32[2,256]{1,0:T(2,128)S(1)}) custom-call(s32[2]{0:T(128)S(1)} %pad_add_fusion.where, f32[24,128]{1,0:T(8,128)S(1)} %get-tuple-element.35.m0, f32[24,128]{1,0:T(8,128)S(1)} %collective-permute-done.9.m1, f32[24,128]{1,0:T(8,128)S(1)} %collective-permute-done.10.m2, ...), custom_call_target="tpu_custom_call" | custom-call | flops 251658240 | bytes 4587520 | tf_op jit(solution)/shard_map/coefficients/pallas_call | solution.py:379
  43.7 1.0 %collective-permute-start.13 = (bf16[136,768]{1,0:T(8,128)(2,1)S(1)}, bf16[136,768]{1,0:T(8,128)(2,1)S(1)}, u32[]{:S(2)}, u32[]{:S(2)}) collective-permute-start(bf16[136,768]{1,0:T(8,128)(2,1)S(1)} %join.1), channel_id=1, source_target_pairs={{0,16},{4,20},{8,24},{12,28},{16,0},{20,4},{24,8},{28,12},{1,17},{... | collective-permute-start | bytes 626696 | tf_op jit(solution)/shard_map/ppermute | solution.py:314
  44.7 1.1 %collective-permute-start.14 = (bf16[136,768]{1,0:T(8,128)(2,1)S(1)}, bf16[136,768]{1,0:T(8,128)(2,1)S(1)}, u32[]{:S(2)}, u32[]{:S(2)}) collective-permute-start(bf16[136,768]{1,0:T(8,128)(2,1)S(1)} %block_terms.3), channel_id=1, source_target_pairs={{0,8},{4,12},{8,0},{12,4},{16,24},{20,28},{24,16},{28,20},{1,9},{5... | collective-permute-start | bytes 626696 | tf_op jit(solution)/shard_map/ppermute | solution.py:314
  46.2 9.4 %collective-permute-done.13.b = bf16[136,768]{1,0:T(8,128)(2,1)S(1)} collective-permute-done((bf16[136,768]{1,0:T(8,128)(2,1)S(1)}, bf16[136,768]{1,0:T(8,128)(2,1)S(1)}, u32[]{:S(2)}, u32[]{:S(2)}) %collective-permute-start.13) | collective-permute-done | bytes 208928 | tf_op jit(solution)/shard_map/ppermute | solution.py:314
  55.7 0.8 %finish.1 = (f32[1,128]{1,0:T(1,128)}, bf16[128,768]{1,0:T(8,128)(2,1)}, bf16[160,768]{1,0:T(8,128)(2,1)}) custom-call(f32[136,768]{1,0:T(8,128)S(1)} %add.20.t, bf16[136,768]{1,0:T(8,128)(2,1)S(1)} %collective-permute-done.14.g, f32[160,768]{1,0:T(8,128)S(1)} %slice.25.own, bf16[160,768]{1,0:T(8,128)(2,1)S(1)} %collective-permute-done.16.s0, ...), custom_call_target="tpu_custom_call" | custom-call | bytes 2211840 | tf_op jit(solution)/shard_map/finish/pallas_call | solution.py:409
  (32 shorter events, 3.7 us)
Async XLA Ops:
  0.6 16.7 %collective-permute-start = (bf16[128,768]{1,0:T(8,128)(2,1)}, bf16[128,768]{1,0:T(8,128)(2,1)S(1)}, u32[]{:S(2)}, u32[]{:S(2)}) collective-permute-start(bf16[128,768]{1,0:T(8,128)(2,1)} %qa.1), channel_id=1, source_target_pairs={{0,16},{4,20},{8,24},{12,28},{16,0},{20,4},{24,8},{28,12},{1,17},{... | collective-permute-start | bytes 589832 | tf_op jit(solution)/shard_map/ppermute | solution.py:314
  5.5 1.2 %copy-start = (bf16[640,768]{1,0:T(8,128)(2,1)S(1)}, bf16[640,768]{1,0:T(8,128)(2,1)}, u32[]{:S(2)}) copy-start(bf16[640,768]{1,0:T(8,128)(2,1)} %weights.3) | copy-start | bytes 2949124
  6.7 17.9 %copy-start.1 = (bf16[128,768]{1,0:T(8,128)(2,1)S(1)}, bf16[128,768]{1,0:T(8,128)(2,1)}, u32[]{:S(2)}) copy-start(bf16[128,768]{1,0:T(8,128)(2,1)} %qa.1) | copy-start | bytes 589828
  7.3 6.8 %collective-permute-start.2 = (bf16[96,768]{1,0:T(8,128)(2,1)S(1)}, bf16[96,768]{1,0:T(8,128)(2,1)S(1)}, u32[]{:S(2)}, u32[]{:S(2)}) collective-permute-start(bf16[96,768]{1,0:T(8,128)(2,1)S(1)} %get-tuple-element.28), channel_id=1, source_target_pairs={{0,4},{4,0},{8,12},{12,8},{16,20},{20,16},{24,28},{28,24},{1,5},{5... | collective-permute-start | bytes 442376 | tf_op jit(solution)/shard_map/ppermute | solution.py:317
  8.9 8.4 %collective-permute-start.5 = (bf16[96,768]{1,0:T(8,128)(2,1)S(1)}, bf16[96,768]{1,0:T(8,128)(2,1)S(1)}, u32[]{:S(2)}, u32[]{:S(2)}) collective-permute-start(bf16[96,768]{1,0:T(8,128)(2,1)S(1)} %get-tuple-element.31), channel_id=1, source_target_pairs={{0,4},{4,0},{8,12},{12,8},{16,20},{20,16},{24,28},{28,24},{1,5},{5... | collective-permute-start | bytes 442376 | tf_op jit(solution)/shard_map/ppermute | solution.py:317
  9.4 11.2 %collective-permute-start.4 = (bf16[144,768]{1,0:T(8,128)(2,1)S(1)}, bf16[144,768]{1,0:T(8,128)(2,1)S(1)}, u32[]{:S(2)}, u32[]{:S(2)}) collective-permute-start(bf16[144,768]{1,0:T(8,128)(2,1)S(1)} %get-tuple-element.30), channel_id=1, source_target_pairs={{0,4},{4,0},{8,12},{12,8},{16,20},{20,16},{24,28},{28,24},{1,5},{5... | collective-permute-start | bytes 663560 | tf_op jit(solution)/shard_map/ppermute | solution.py:317
  14.1 6.5 %collective-permute-start.3 = (bf16[128,768]{1,0:T(8,128)(2,1)}, bf16[128,768]{1,0:T(8,128)(2,1)S(1)}, u32[]{:S(2)}, u32[]{:S(2)}) collective-permute-start(bf16[128,768]{1,0:T(8,128)(2,1)} %qa.1), channel_id=1, source_target_pairs={{0,8},{4,12},{8,0},{12,4},{16,24},{20,28},{24,16},{28,20},{1,9},{5... | collective-permute-start | bytes 589832 | tf_op jit(solution)/shard_map/ppermute | solution.py:314
  15.7 4.9 %collective-permute-start.7 = (bf16[96,768]{1,0:T(8,128)(2,1)S(1)}, bf16[96,768]{1,0:T(8,128)(2,1)S(1)}, u32[]{:S(2)}, u32[]{:S(2)}) collective-permute-start(bf16[96,768]{1,0:T(8,128)(2,1)S(1)} %collective-permute-done.2.refs_1_), channel_id=1, source_target_pairs={{0,1},{1,0},{2,3},{3,2},{4,5},{5,4},{6,7},{7,6},{8,9},{9,8},{10,11... | collective-permute-start | bytes 442376 | tf_op jit(solution)/shard_map/ppermute | solution.py:320
  17.3 3.3 %collective-permute-start.8 = (bf16[96,768]{1,0:T(8,128)(2,1)S(1)}, bf16[96,768]{1,0:T(8,128)(2,1)S(1)}, u32[]{:S(2)}, u32[]{:S(2)}) collective-permute-start(bf16[96,768]{1,0:T(8,128)(2,1)S(1)} %collective-permute-done.5.refs_2_), channel_id=1, source_target_pairs={{0,1},{1,0},{2,3},{3,2},{4,5},{5,4},{6,7},{7,6},{8,9},{9,8},{10,11... | collective-permute-start | bytes 442376 | tf_op jit(solution)/shard_map/ppermute | solution.py:320
  17.3 7.3 %collective-permute-start.1 = (bf16[128,768]{1,0:T(8,128)(2,1)S(1)}, bf16[128,768]{1,0:T(8,128)(2,1)S(1)}, u32[]{:S(2)}, u32[]{:S(2)}) collective-permute-start(bf16[128,768]{1,0:T(8,128)(2,1)S(1)} %collective-permute-done.qb), channel_id=1, source_target_pairs={{0,8},{4,12},{8,0},{12,4},{16,24},{20,28},{24,16},{28,20},{1,9},{5... | collective-permute-start | bytes 589832 | tf_op jit(solution)/shard_map/ppermute | solution.py:314
  20.6 1.5 %collective-permute-start.6 = (bf16[144,768]{1,0:T(8,128)(2,1)S(1)}, bf16[144,768]{1,0:T(8,128)(2,1)S(1)}, u32[]{:S(2)}, u32[]{:S(2)}) collective-permute-start(bf16[144,768]{1,0:T(8,128)(2,1)S(1)} %collective-permute-done.4.refs_0_), channel_id=1, source_target_pairs={{0,1},{1,0},{2,3},{3,2},{4,5},{5,4},{6,7},{7,6},{8,9},{9,8},{10,11... | collective-permute-start | bytes 663560 | tf_op jit(solution)/shard_map/ppermute | solution.py:320
  25.6 5.6 %collective-permute-start.11 = (f32[24,128]{1,0:T(8,128)S(1)}, f32[24,128]{1,0:T(8,128)S(1)}, u32[]{:S(2)}, u32[]{:S(2)}) collective-permute-start(f32[24,128]{1,0:T(8,128)S(1)} %get-tuple-element.35.m0), channel_id=1, source_target_pairs={{0,24},{4,28},{8,16},{12,20},{16,8},{20,12},{24,0},{28,4},{1,25},{... | collective-permute-start | bytes 36872 | tf_op jit(solution)/shard_map/ppermute | solution.py:314
  27.1 4.6 %collective-permute-start.10 = (f32[24,128]{1,0:T(8,128)S(1)}, f32[24,128]{1,0:T(8,128)S(1)}, u32[]{:S(2)}, u32[]{:S(2)}) collective-permute-start(f32[24,128]{1,0:T(8,128)S(1)} %get-tuple-element.35.m0), channel_id=1, source_target_pairs={{0,16},{4,20},{8,24},{12,28},{16,0},{20,4},{24,8},{28,12},{1,17},{... | collective-permute-start | bytes 36872 | tf_op jit(solution)/shard_map/ppermute | solution.py:314
  28.7 3.7 %collective-permute-start.9 = (f32[24,128]{1,0:T(8,128)S(1)}, f32[24,128]{1,0:T(8,128)S(1)}, u32[]{:S(2)}, u32[]{:S(2)}) collective-permute-start(f32[24,128]{1,0:T(8,128)S(1)} %get-tuple-element.35.m0), channel_id=1, source_target_pairs={{0,8},{4,12},{8,0},{12,4},{16,24},{20,28},{24,16},{28,20},{1,9},{5... | collective-permute-start | bytes 36872 | tf_op jit(solution)/shard_map/ppermute | solution.py:314
  33.6 4.2 %collective-permute-start.15 = (bf16[640,768]{1,0:T(8,128)(2,1)S(1)}, bf16[640,768]{1,0:T(8,128)(2,1)S(1)}, u32[]{:S(2)}, u32[]{:S(2)}) collective-permute-start(bf16[640,768]{1,0:T(8,128)(2,1)S(1)} %label_terms.3), channel_id=1, source_target_pairs={{0,1},{1,0},{2,3},{3,2},{4,5},{5,4},{6,7},{7,6},{8,9},{9,8},{10,11... | collective-permute-start | bytes 2949128 | tf_op jit(solution)/shard_map/ppermute | solution.py:320
  35.1 8.5 %collective-permute-start.12 = (bf16[136,768]{1,0:T(8,128)(2,1)S(1)}, bf16[136,768]{1,0:T(8,128)(2,1)S(1)}, u32[]{:S(2)}, u32[]{:S(2)}) collective-permute-start(bf16[136,768]{1,0:T(8,128)(2,1)S(1)} %get-tuple-element.43), channel_id=1, source_target_pairs={{0,8},{4,12},{8,0},{12,4},{16,24},{20,28},{24,16},{28,20},{1,9},{5... | collective-permute-start | bytes 626696 | tf_op jit(solution)/shard_map/ppermute | solution.py:314
  38.2 17.5 %collective-permute-start.18 = (bf16[160,768]{1,0:T(8,128)(2,1)S(1)}, bf16[160,768]{1,0:T(8,128)(2,1)S(1)}, u32[]{:S(2)}, u32[]{:S(2)}) collective-permute-start(bf16[160,768]{1,0:T(8,128)(2,1)S(1)} %get-tuple-element.55), channel_id=1, source_target_pairs={{0,6},{1,7},{2,4},{3,5},{4,2},{5,3},{6,0},{7,1},{8,14},{9,15},{10,... | collective-permute-start | bytes 737288 | tf_op jit(solution)/shard_map/ppermute | solution.py:326
  40.8 15.0 %collective-permute-start.17 = (bf16[160,768]{1,0:T(8,128)(2,1)S(1)}, bf16[160,768]{1,0:T(8,128)(2,1)S(1)}, u32[]{:S(2)}, u32[]{:S(2)}) collective-permute-start(bf16[160,768]{1,0:T(8,128)(2,1)S(1)} %get-tuple-element.56), channel_id=1, source_target_pairs={{0,4},{4,0},{8,12},{12,8},{16,20},{20,16},{24,28},{28,24},{1,5},{5... | collective-permute-start | bytes 737288 | tf_op jit(solution)/shard_map/ppermute | solution.py:317
  41.3 14.5 %collective-permute-start.16 = (bf16[160,768]{1,0:T(8,128)(2,1)S(1)}, bf16[160,768]{1,0:T(8,128)(2,1)S(1)}, u32[]{:S(2)}, u32[]{:S(2)}) collective-permute-start(bf16[160,768]{1,0:T(8,128)(2,1)S(1)} %get-tuple-element.57), channel_id=1, source_target_pairs={{0,2},{1,3},{2,0},{3,1},{4,6},{5,7},{6,4},{7,5},{8,10},{9,11},{10,... | collective-permute-start | bytes 737288 | tf_op jit(solution)/shard_map/ppermute | solution.py:323
  43.7 11.9 %collective-permute-start.13 = (bf16[136,768]{1,0:T(8,128)(2,1)S(1)}, bf16[136,768]{1,0:T(8,128)(2,1)S(1)}, u32[]{:S(2)}, u32[]{:S(2)}) collective-permute-start(bf16[136,768]{1,0:T(8,128)(2,1)S(1)} %join.1), channel_id=1, source_target_pairs={{0,16},{4,20},{8,24},{12,28},{16,0},{20,4},{24,8},{28,12},{1,17},{... | collective-permute-start | bytes 626696 | tf_op jit(solution)/shard_map/ppermute | solution.py:314
  44.7 11.0 %collective-permute-start.14 = (bf16[136,768]{1,0:T(8,128)(2,1)S(1)}, bf16[136,768]{1,0:T(8,128)(2,1)S(1)}, u32[]{:S(2)}, u32[]{:S(2)}) collective-permute-start(bf16[136,768]{1,0:T(8,128)(2,1)S(1)} %block_terms.3), channel_id=1, source_target_pairs={{0,8},{4,12},{8,0},{12,4},{16,24},{20,28},{24,16},{28,20},{1,9},{5... | collective-permute-start | bytes 626696 | tf_op jit(solution)/shard_map/ppermute | solution.py:314

commit v6 on v5

--- a/solution.py
+++ b/solution.py
@@ -94,6 +94,8 @@
 
 
 FAR = 1e30
+A, B = (1, 2), (0, 3)
+CUTS = (8, 6, 6)
 NT = (((1,), (1,)), ((), ()))
 TN = (((0,), (0,)), ((), ()))
 ROOM = pltpu.CompilerParams(vmem_limit_bytes=20 * 1024 * 1024)
@@ -234,51 +236,72 @@
     return [jnp.concatenate(v, 1) for v in zip(*(block_lines(messages, me, j) for j in blocks))]
 
 
-def coefficients(blocks, labels, where, m0, m1, m2, m3, s_ref, e_ref, held, coef, last, lines):
+def coef_dot(coefs, held, rows):
+    half = held.shape[0] // 2
+    return sum(
+        lax.dot_general(c[:, rows], held[pl.ds(i * half, half), :], TN, preferred_element_type=jnp.float32)
+        for i, c in enumerate(coefs)
+    )
+
+
+def slab_coefs(half, labels, where, lines, e_ref, coef, s_ref=None):
+    _, near, pair, target = lines
+    part, positive = labels // 4, jnp.zeros_like(near)
+    index = lax.broadcasted_iota(jnp.int32, (part, target.shape[1]), 0)
+    for i, (at, side, first) in enumerate(slabs(where, labels)):
+        if i // 4 == half or s_ref is not None:
+            hot = index == target - first
+        if s_ref is not None:
+            positive += jnp.sum(jnp.where(hot, s_ref[at, :], 0.0), axis=0, keepdims=True)
+        if i // 4 == half:
+            p = e_ref[at, :] * (pair if side else near)
+            coef[pl.ds((i % 4) * part, part), :] = (p - jnp.where(hot, 1.0, 0.0)).astype(jnp.bfloat16)
+    return positive
+
+
+def send_terms(labels, where, m0, m1, m2, m3, e_a, e_b, qa, qb, out, far_a, far_b):
+    messages = (m0, m1, m2, m3)
+    slab_coefs(1, labels, where, pair_lines(messages, where[0], A), e_a, far_a)
+    slab_coefs(1, labels, where, pair_lines(messages, where[0], B), e_b, far_b)
+    total = jnp.dot(far_a[...], qa[...], preferred_element_type=jnp.float32)
+    total += jnp.dot(far_b[...], qb[...], preferred_element_type=jnp.float32)
+    out[...] = total.astype(out.dtype)
+
+
+def keep_terms(labels, where, m0, m1, m2, m3, e_a, near_b, qa, qb, out, near_a):
+    slab_coefs(0, labels, where, pair_lines((m0, m1, m2, m3), where[0], A), e_a, near_a)
+    total = jnp.dot(near_a[...], qa[...], preferred_element_type=jnp.float32)
+    out[...] = total + jnp.dot(near_b[...], qb[...], preferred_element_type=jnp.float32)
+
+
+def far_block(labels, where, m0, m1, m2, m3, s_ref, e_ref, far, held, last, lines, near):
     rows = m0.shape[1]
-    normal, near, pair, target = pair_lines((m0, m1, m2, m3), where[0], blocks)
-    index = lax.broadcasted_iota(jnp.int32, (labels // 4, 2 * rows), 0)
-    positive = jnp.zeros((1, 2 * rows), jnp.float32)
-    for at, side, first in slabs(where, labels):
-        hot = index == target - first
-        p = e_ref[at, :] * (pair if side else near)
-        coef[at, :] = (p - jnp.where(hot, 1.0, 0.0)).astype(jnp.bfloat16)
-        positive += jnp.sum(jnp.where(hot, s_ref[at, :], 0.0), axis=0, keepdims=True)
+    found = pair_lines((m0, m1, m2, m3), where[0], B)
+    positive = slab_coefs(0, labels, where, found, e_ref, near, s_ref)
     lines[0:1, :] = positive
-    lines[1:2, :] = normal
-    term = lax.dot_general(coef[:, pl.ds(rows, rows)], held[...], TN, preferred_element_type=jnp.float32)
+    lines[1:2, :] = found[0]
+    term = coef_dot((near, far), held, pl.ds(rows, rows))
     last[...] = payload(term, [positive[:, rows:]], last.dtype)
 
 
-def block_terms(coef, held, lines, out):
-    rows = coef.shape[1] // 2
-    term = lax.dot_general(coef[:, pl.ds(0, rows)], held[...], TN, preferred_element_type=jnp.float32)
+def next_block(labels, where, m0, m1, m2, m3, s_ref, near, far, held, last, lines):
+    rows = m0.shape[1]
+    found = pair_lines((m0, m1, m2, m3), where[0], A)
+    positive = slab_coefs(2, labels, where, found, None, None, s_ref)
+    lines[0:1, :] = positive
+    lines[1:2, :] = found[0]
+    term = coef_dot((near, far), held, pl.ds(rows, rows))
+    last[...] = payload(term, [positive[:, rows:]], last.dtype)
+
+
+def first_terms(coef_near, coef_far, held, lines, out):
+    rows = coef_near.shape[1] // 2
+    term = coef_dot((coef_near, coef_far), held, pl.ds(0, rows))
     positive = lines[0:1, :rows].astype(jnp.bfloat16).astype(jnp.float32)
     if out.dtype == jnp.bfloat16:
         out[...] = payload(term, [positive], out.dtype)
     else:
         out[...] = payload(term.astype(jnp.bfloat16).astype(jnp.float32), [positive, lines[1:2, :rows]], out.dtype)
-
-
-def label_terms(half, labels, where, m0, m1, m2, m3, e_a, e_b, qa, qb, out, coef):
-    rows, part = m0.shape[1], labels // 4
-    index = lax.broadcasted_iota(jnp.int32, (part, 2 * rows), 0)
-    total = None
-    for blocks, e_ref, q in ((A, e_a, qa), (B, e_b, qb)):
-        _, near, pair, target = pair_lines((m0, m1, m2, m3), where[0], blocks)
-        for i, (at, side, first) in enumerate(slabs(where, labels)):
-            if i // 4 != half:
-                continue
-            hot = jnp.where(index == target - first, 1.0, 0.0)
-            p = e_ref[at, :] * (pair if side else near)
-            coef[pl.ds((i % 4) * part, part), :] = (p - hot).astype(jnp.bfloat16)
-        term = jnp.dot(coef[...], q[...], preferred_element_type=jnp.float32)
-        total = term if total is None else total + term
-    out[...] = total.astype(out.dtype)
-
-
-A, B = (1, 2), (0, 3)
-CUTS = (8, 6, 6)
 
 
 def join(a, b, out):
@@ -375,32 +398,36 @@
     m3, m2, m1 = swap(message, 3), swap(message, 2), swap(message, 1)
     term, line = shape((rows + 8, width), bf16), shape((2, 2 * rows), f32)
 
-    def coefficient(blocks, s, e):
+    coefs = shape((labels, 2 * rows), bf16)
+    stated = (where, message, m1, m2, m3)
+
+    def first_part(near, far, lines, dtype):
         return call(
-            functools.partial(coefficients, blocks, labels),
-            (shape((2 * labels, 2 * rows), bf16), term, line),
-            1, 7, block_flops // 2, block_bytes, (), "coefficients",
-        )(where, message, m1, m2, m3, s, e, held)
-
-    def block_part(coef, lines, dtype):
-        return call(block_terms, shape((rows + 8, width), dtype), 0, 3, block_flops // 2, block_bytes // 2, (), "block_terms")(coef, held, lines)
-
-    def label_part(half, dtype):
-        return call(
-            functools.partial(label_terms, half, labels),
-            shape((labels, width), dtype),
-            1, 8, block_flops, block_bytes, [pltpu.VMEM((labels, 2 * rows), bf16)], "label_terms",
-        )(where, message, m1, m2, m3, ea, eb, qa, qb)
-
-    sent, kept = label_part(1, bf16), label_part(0, f32)
+            first_terms, shape((rows + 8, width), dtype), 0, 4, block_flops // 2, block_bytes // 2, (), "first_terms"
+        )(near, far, held, lines)
+
+    sent, far_a, far_b = call(
+        functools.partial(send_terms, labels),
+        (shape((labels, width), bf16), coefs, coefs),
+        1, 8, block_flops, block_bytes, (), "send_terms",
+    )(*stated, ea, eb, qa, qb)
     arrived = core(sent)
-    coef_b, t3, lines_b = coefficient(B, sb, eb)
+    t3, lines_b, near_b = call(
+        functools.partial(far_block, labels), (term, line, coefs), 1, 8, block_flops // 2, block_bytes, (), "far_block"
+    )(*stated, sb, eb, far_b, held)
     g3 = swap(t3, 1)
-    coef_a, t2, lines_a = coefficient(A, sa, ea)
-    t1 = block_part(coef_a, lines_a, bf16)
-    t0 = block_part(coef_b, lines_b, f32)
+    kept, near_a = call(
+        functools.partial(keep_terms, labels),
+        (shape((labels, width), f32), coefs),
+        1, 8, block_flops, block_bytes, (), "keep_terms",
+    )(*stated, ea, near_b, qa, qb)
+    t2, lines_a = call(
+        functools.partial(next_block, labels), (term, line), 1, 8, block_flops // 2, block_bytes, (), "next_block"
+    )(*stated, sa, near_a, far_a, held)
+    t0 = first_part(near_b, far_b, lines_b, f32)
     joined = call(join, term, 0, 2, 0, rows * width * 6, (), "join")(t2, g3)
-    joined, t1 = lax.optimization_barrier((joined, t1))
+    joined, lines_a = lax.optimization_barrier((joined, lines_a))
+    t1 = first_part(near_a, far_a, lines_a, bf16)
     g1, g2 = swap(t1, 1), swap(joined, 2)
     summed = kept + arrived.astype(f32)
     sent = summed[part:].astype(bf16)

time: 56.8 us -> 56.1 us (0.988)
  waiting for transfers between devices: 19.1 us -> 18.5 us
    ppermute x9, waiting for transfers between devices: 12.6 us -> 12 us  [swap(): return lax.ppermute(x, 'label', [(i, i ^ 2 * k) for i in range(n)])]
where the time goes in v6:
time: 56.1 us; the launch traced here: 55.9 us
  starting transfers between devices  22.7 us (40%)
  waiting for transfers between devices  18.5 us (33%)
  Pallas kernels  10.1 us (18%)
  local copies, waits for them, and re-layouts  1.98 us (4%)
  other arithmetic  1.83 us (3%)
  between operations  0.81 us (1%)
    ppermute x9, starting transfers between devices, swap(): return lax.ppermute(x, 'label', [(i, i ^ 2 * k) for i in range(n)])  15.4 us
    ppermute x9, waiting for transfers between devices, swap(): return lax.ppermute(x, 'label', [(i, i ^ 2 * k) for i in range(n)])  12 us
    ppermute x4, waiting for transfers between devices, pair(): return lax.ppermute(x, 'label', [(i, i ^ 1) for i in range(n)])  5.06 us
    ppermute x4, starting transfers between devices, pair(): return lax.ppermute(x, 'label', [(i, i ^ 1) for i in range(n)])  4.11 us
    ppermute x1, starting transfers between devices, corner(): lax.ppermute(x, ('label', 'dp'), [(i * dp + j, (i ^ 1) * dp + (j ^ 2)) fo...  2.52 us
    pallas_call x1, Pallas kernels, dense_plan(): call(functools.partial(first_scores, cuts), (shape((2 * labels, width), b...  1.69 us
    ppermute x4, waiting for transfers between devices, core(): return lax.ppermute(x, 'dp', [(i, i ^ 1) for i in range(dp)])  1.41 us
    pallas_call x1, Pallas kernels, dense_plan(): call(functools.partial(send_terms, labels), (shape((labels, width), bf16)...  1.3 us
  transfers between devices with their start and end apart: 19, of which 9 were waited for; matrix products, arithmetic and copies ran while one was open for 5% of the time, Pallas kernels for 13%

profile of v6, /device:TPU:0, one launch (start us, length us, event | category | flops | bytes accessed | tf_op | source)
XLA Modules:
  0.0 55.9 jit_solution(13805434259030976228)
XLA Ops:
  0.6 4.1 %collective-permute-start = (bf16[128,768]{1,0:T(8,128)(2,1)}, bf16[128,768]{1,0:T(8,128)(2,1)S(1)}, u32[]{:S(2)}, u32[]{:S(2)}) collective-permute-start(bf16[128,768]{1,0:T(8,128)(2,1)} %qa.1), channel_id=1, source_target_pairs={{0,16},{4,20},{8,24},{12,28},{16,0},{20,4},{24,8},{28,12},{1,17},{... | collective-permute-start | bytes 589832 | tf_op jit(solution)/shard_map/ppermute | solution.py:337
  4.7 0.7 %reshape.13.counts = s32[1,640]{1,0:T(1,128)S(1)} reshape(s32[640]{0:T(1024)} %param.8) | data formatting | bytes 5120 | tf_op jit(solution)/shard_map/reshape | solution.py:369
  5.5 1.2 %copy-done = bf16[640,768]{1,0:T(8,128)(2,1)S(1)} copy-done((bf16[640,768]{1,0:T(8,128)(2,1)S(1)}, bf16[640,768]{1,0:T(8,128)(2,1)}, u32[]{:S(2)}) %copy-start) | copy-done | bytes 983064
  6.7 0.6 %pack.1 = (bf16[144,768]{1,0:T(8,128)(2,1)S(1)}, bf16[96,768]{1,0:T(8,128)(2,1)S(1)}, bf16[96,768]{1,0:T(8,128)(2,1)S(1)}) custom-call(s32[2]{0:T(128)S(1)} %pad_add_fusion.where, bf16[640,768]{1,0:T(8,128)(2,1)S(1)} %copy-done, s32[1,640]{1,0:T(1,128)S(1)} %reshape.13.counts), custom_call_target="tpu_custom_call" | custom-call | bytes 983040 | tf_op jit(solution)/shard_map/pack/pallas_call | solution.py:372
  7.3 1.6 %collective-permute-start.2 = (bf16[96,768]{1,0:T(8,128)(2,1)S(1)}, bf16[96,768]{1,0:T(8,128)(2,1)S(1)}, u32[]{:S(2)}, u32[]{:S(2)}) collective-permute-start(bf16[96,768]{1,0:T(8,128)(2,1)S(1)} %get-tuple-element.32), channel_id=1, source_target_pairs={{0,4},{4,0},{8,12},{12,8},{16,20},{20,16},{24,28},{28,24},{1,5},{5... | collective-permute-start | bytes 442376 | tf_op jit(solution)/shard_map/ppermute | solution.py:340
  9.4 1.5 %collective-permute-start.4 = (bf16[144,768]{1,0:T(8,128)(2,1)S(1)}, bf16[144,768]{1,0:T(8,128)(2,1)S(1)}, u32[]{:S(2)}, u32[]{:S(2)}) collective-permute-start(bf16[144,768]{1,0:T(8,128)(2,1)S(1)} %get-tuple-element.34), channel_id=1, source_target_pairs={{0,4},{4,0},{8,12},{12,8},{16,20},{20,16},{24,28},{28,24},{1,5},{5... | collective-permute-start | bytes 663560 | tf_op jit(solution)/shard_map/ppermute | solution.py:340
  10.9 0.8 %select_reduce_fusion = s32[128,4]{0,1:T(4,128)S(1)} fusion(s32[8]{0:T(128)} %param.11, s32[128,4]{0,1:T(4,128)} %param.9), kind=kLoop, calls=%fused_computation.1 | loop fusion | flops 11776 | bytes 4128 | tf_op jit(solution)/shard_map/reduce_sum | solution.py:378
  11.7 0.7 %fusion = s32[1,128]{1,0:T(1,128)S(1)} fusion(s32[128]{0:T(128)} %param.10, s32[128,4]{0,1:T(4,128)S(1)} %select_reduce_fusion), kind=kLoop, calls=%fused_computation.7 | loop fusion | flops 256 | bytes 1536 | tf_op jit(solution)/shard_map/stack | solution.py:381
  12.3 1.8 %collective-permute-done.2.refs_1_ = bf16[96,768]{1,0:T(8,128)(2,1)S(1)} collective-permute-done((bf16[96,768]{1,0:T(8,128)(2,1)S(1)}, bf16[96,768]{1,0:T(8,128)(2,1)S(1)}, u32[]{:S(2)}, u32[]{:S(2)}) %collective-permute-start.2) | collective-permute-done | bytes 147488 | tf_op jit(solution)/shard_map/ppermute | solution.py:340
  14.1 1.6 %collective-permute-start.3 = (bf16[128,768]{1,0:T(8,128)(2,1)}, bf16[128,768]{1,0:T(8,128)(2,1)S(1)}, u32[]{:S(2)}, u32[]{:S(2)}) collective-permute-start(bf16[128,768]{1,0:T(8,128)(2,1)} %qa.1), channel_id=1, source_target_pairs={{0,8},{4,12},{8,0},{12,4},{16,24},{20,28},{24,16},{28,20},{1,9},{5... | collective-permute-start | bytes 589832 | tf_op jit(solution)/shard_map/ppermute | solution.py:337
  15.7 1.6 %collective-permute-done.5.refs_2_ = bf16[96,768]{1,0:T(8,128)(2,1)S(1)} collective-permute-done((bf16[96,768]{1,0:T(8,128)(2,1)S(1)}, bf16[96,768]{1,0:T(8,128)(2,1)S(1)}, u32[]{:S(2)}, u32[]{:S(2)}) %collective-permute-start.5) | collective-permute-done | bytes 147488 | tf_op jit(solution)/shard_map/ppermute | solution.py:340
  17.3 1.6 %collective-permute-start.1 = (bf16[128,768]{1,0:T(8,128)(2,1)S(1)}, bf16[128,768]{1,0:T(8,128)(2,1)S(1)}, u32[]{:S(2)}, u32[]{:S(2)}) collective-permute-start(bf16[128,768]{1,0:T(8,128)(2,1)S(1)} %collective-permute-done.qb), channel_id=1, source_target_pairs={{0,8},{4,12},{8,0},{12,4},{16,24},{20,28},{24,16},{28,20},{1,9},{5... | collective-permute-start | bytes 589832 | tf_op jit(solution)/shard_map/ppermute | solution.py:337
  18.9 1.7 %collective-permute-done.4.refs_0_ = bf16[144,768]{1,0:T(8,128)(2,1)S(1)} collective-permute-done((bf16[144,768]{1,0:T(8,128)(2,1)S(1)}, bf16[144,768]{1,0:T(8,128)(2,1)S(1)}, u32[]{:S(2)}, u32[]{:S(2)}) %collective-permute-start.4) | collective-permute-done | bytes 221216 | tf_op jit(solution)/shard_map/ppermute | solution.py:340
  20.6 1.4 %collective-permute-done.6.refs_3_ = bf16[144,768]{1,0:T(8,128)(2,1)S(1)} collective-permute-done((bf16[144,768]{1,0:T(8,128)(2,1)S(1)}, bf16[144,768]{1,0:T(8,128)(2,1)S(1)}, u32[]{:S(2)}, u32[]{:S(2)}) %collective-permute-start.6) | collective-permute-done | bytes 221216 | tf_op jit(solution)/shard_map/ppermute | solution.py:343
  22.0 1.7 %first_scores.1 = (bf16[1280,768]{1,0:T(8,128)(2,1)S(1)}, bf16[256,768]{1,0:T(8,128)(2,1)S(1)}, f32[1280,256]{1,0:T(8,128)S(1)}, f32[1280,256]{1,0:T(8,128)S(1)}...) custom-call(s32[2]{0:T(128)S(1)} %pad_add_fusion.where, bf16[128,768]{1,0:T(8,128)(2,1)S(1)} %collective-permute-done.3.qa, ...), custom_call_target="tpu_custom_call" | custom-call | flops 503316480 | bytes 4587520 | tf_op jit(solution)/shard_map/first_scores/pallas_call | solution.py:387
  23.7 0.9 %collective-permute-done.1.qb = bf16[128,768]{1,0:T(8,128)(2,1)S(1)} collective-permute-done((bf16[128,768]{1,0:T(8,128)(2,1)S(1)}, bf16[128,768]{1,0:T(8,128)(2,1)S(1)}, u32[]{:S(2)}, u32[]{:S(2)}) %collective-permute-start.1) | collective-permute-done | bytes 196640 | tf_op jit(solution)/shard_map/ppermute | solution.py:337
  24.6 1.0 %last_scores.1 = (bf16[256,768]{1,0:T(8,128)(2,1)S(1)}, f32[1280,256]{1,0:T(8,128)S(1)}, f32[1280,256]{1,0:T(8,128)S(1)}, f32[24,128]{1,0:T(8,128)S(1)}) custom-call(bf16[128,768]{1,0:T(8,128)(2,1)S(1)} %copy-done.1, bf16[128,768]{1,0:T(8,128)(2,1)S(1)} %collective-permute-done.1.qb, bf16[1280,768]{1,0:T(8,128)(2,1)S(1)} %get-tuple-element.36.held, ...), custom_call_target="tpu_custom_call" | custom-call | flops 503316480 | bytes 4587520 | tf_op jit(solution)/shard_map/last_scores/pallas_call | solution.py:392
  25.6 1.5 %collective-permute-start.11 = (f32[24,128]{1,0:T(8,128)S(1)}, f32[24,128]{1,0:T(8,128)S(1)}, u32[]{:S(2)}, u32[]{:S(2)}) collective-permute-start(f32[24,128]{1,0:T(8,128)S(1)} %get-tuple-element.39.m0), channel_id=1, source_target_pairs={{0,24},{4,28},{8,16},{12,20},{16,8},{20,12},{24,0},{28,4},{1,25},{... | collective-permute-start | bytes 36872 | tf_op jit(solution)/shard_map/ppermute | solution.py:337
  27.1 1.6 %collective-permute-start.10 = (f32[24,128]{1,0:T(8,128)S(1)}, f32[24,128]{1,0:T(8,128)S(1)}, u32[]{:S(2)}, u32[]{:S(2)}) collective-permute-start(f32[24,128]{1,0:T(8,128)S(1)} %get-tuple-element.39.m0), channel_id=1, source_target_pairs={{0,16},{4,20},{8,24},{12,28},{16,0},{20,4},{24,8},{28,12},{1,17},{... | collective-permute-start | bytes 36872 | tf_op jit(solution)/shard_map/ppermute | solution.py:337
  28.7 1.3 %collective-permute-start.9 = (f32[24,128]{1,0:T(8,128)S(1)}, f32[24,128]{1,0:T(8,128)S(1)}, u32[]{:S(2)}, u32[]{:S(2)}) collective-permute-start(f32[24,128]{1,0:T(8,128)S(1)} %get-tuple-element.39.m0), channel_id=1, source_target_pairs={{0,8},{4,12},{8,0},{12,4},{16,24},{20,28},{24,16},{28,20},{1,9},{5... | collective-permute-start | bytes 36872 | tf_op jit(solution)/shard_map/ppermute | solution.py:337
  30.0 1.1 %collective-permute-done.11.m3 = f32[24,128]{1,0:T(8,128)S(1)} collective-permute-done((f32[24,128]{1,0:T(8,128)S(1)}, f32[24,128]{1,0:T(8,128)S(1)}, u32[]{:S(2)}, u32[]{:S(2)}) %collective-permute-start.11) | collective-permute-done | bytes 12320 | tf_op jit(solution)/shard_map/ppermute | solution.py:337
  31.7 0.7 %collective-permute-done.9.m1 = f32[24,128]{1,0:T(8,128)S(1)} collective-permute-done((f32[24,128]{1,0:T(8,128)S(1)}, f32[24,128]{1,0:T(8,128)S(1)}, u32[]{:S(2)}, u32[]{:S(2)}) %collective-permute-start.9) | collective-permute-done | bytes 12320 | tf_op jit(solution)/shard_map/ppermute | solution.py:337
  32.4 1.3 %send_terms.1 = (bf16[640,768]{1,0:T(8,128)(2,1)S(1)}, bf16[640,256]{1,0:T(8,128)(2,1)S(1)}, bf16[640,256]{1,0:T(8,128)(2,1)S(1)}) custom-call(s32[2]{0:T(128)S(1)} %pad_add_fusion.where, f32[24,128]{1,0:T(8,128)S(1)} %get-tuple-element.39.m0, f32[24,128]{1,0:T(8,128)S(1)} %collective-permute-done.9.m1, f32[24,128]{1,0:T(8,128)S(1)} %collective-permute-done.10.m2, ...), custom_call_target="tpu_custom_call" | custom-call | flops 503316480 | bytes 4587520 | tf_op jit(solution)/shard_map/send_terms/pallas_call | solution.py:409
  33.8 1.3 %far_block.1 = (bf16[136,768]{1,0:T(8,128)(2,1)S(1)}, f32[2,256]{1,0:T(2,128)S(1)}, bf16[640,256]{1,0:T(8,128)(2,1)S(1)}) custom-call(s32[2]{0:T(128)S(1)} %pad_add_fusion.where, f32[24,128]{1,0:T(8,128)S(1)} %get-tuple-element.39.m0, f32[24,128]{1,0:T(8,128)S(1)} %collective-permute-done.9.m1, f32[24,128]{1,0:T(8,128)S(1)} %collective-permute-done.10.m2, ...), custom_call_target="tpu_custom_call" | custom-call | flops 251658240 | bytes 4587520 | tf_op jit(solution)/shard_map/far_block/pallas_call | solution.py:415
  35.0 1.4 %collective-permute-start.12 = (bf16[136,768]{1,0:T(8,128)(2,1)S(1)}, bf16[136,768]{1,0:T(8,128)(2,1)S(1)}, u32[]{:S(2)}, u32[]{:S(2)}) collective-permute-start(bf16[136,768]{1,0:T(8,128)(2,1)S(1)} %get-tuple-element.52), channel_id=1, source_target_pairs={{0,8},{4,12},{8,0},{12,4},{16,24},{20,28},{24,16},{28,20},{1,9},{5... | collective-permute-start | bytes 626696 | tf_op jit(solution)/shard_map/ppermute | solution.py:337
  36.5 1.2 %keep_terms.1 = (f32[640,768]{1,0:T(8,128)S(1)}, bf16[640,256]{1,0:T(8,128)(2,1)S(1)}) custom-call(s32[2]{0:T(128)S(1)} %pad_add_fusion.where, f32[24,128]{1,0:T(8,128)S(1)} %get-tuple-element.39.m0, f32[24,128]{1,0:T(8,128)S(1)} %collective-permute-done.9.m1, f32[24,128]{1,0:T(8,128)S(1)} %collective-permute-done.10.m2, ...), custom_call_target="tpu_custom_call" | custom-call | flops 503316480 | bytes 4587520 | tf_op jit(solution)/shard_map/keep_terms/pallas_call | solution.py:419
  38.1 2.5 %collective-permute-start.18 = (bf16[160,768]{1,0:T(8,128)(2,1)S(1)}, bf16[160,768]{1,0:T(8,128)(2,1)S(1)}, u32[]{:S(2)}, u32[]{:S(2)}) collective-permute-start(bf16[160,768]{1,0:T(8,128)(2,1)S(1)} %get-tuple-element.63), channel_id=1, source_target_pairs={{0,6},{1,7},{2,4},{3,5},{4,2},{5,3},{6,0},{7,1},{8,14},{9,15},{10,... | collective-permute-start | bytes 737288 | tf_op jit(solution)/shard_map/ppermute | solution.py:349
  41.6 1.1 %next_block.1 = (bf16[136,768]{1,0:T(8,128)(2,1)S(1)}, f32[2,256]{1,0:T(2,128)S(1)}) custom-call(s32[2]{0:T(128)S(1)} %pad_add_fusion.where, f32[24,128]{1,0:T(8,128)S(1)} %get-tuple-element.39.m0, f32[24,128]{1,0:T(8,128)S(1)} %collective-permute-done.9.m1, f32[24,128]{1,0:T(8,128)S(1)} %collective-permute-done.10.m2, ...), custom_call_target="tpu_custom_call" | custom-call | flops 251658240 | bytes 4587520 | tf_op jit(solution)/shard_map/next_block/pallas_call | solution.py:424
  42.8 1.3 %collective-permute-start.13 = (bf16[136,768]{1,0:T(8,128)(2,1)S(1)}, bf16[136,768]{1,0:T(8,128)(2,1)S(1)}, u32[]{:S(2)}, u32[]{:S(2)}) collective-permute-start(bf16[136,768]{1,0:T(8,128)(2,1)S(1)} %join.1), channel_id=1, source_target_pairs={{0,16},{4,20},{8,24},{12,28},{16,0},{20,4},{24,8},{28,12},{1,17},{... | collective-permute-start | bytes 626696 | tf_op jit(solution)/shard_map/ppermute | solution.py:337
  44.6 1.0 %collective-permute-start.14 = (bf16[136,768]{1,0:T(8,128)(2,1)S(1)}, bf16[136,768]{1,0:T(8,128)(2,1)S(1)}, u32[]{:S(2)}, u32[]{:S(2)}) collective-permute-start(bf16[136,768]{1,0:T(8,128)(2,1)S(1)} %first_terms.3), channel_id=1, source_target_pairs={{0,8},{4,12},{8,0},{12,4},{16,24},{20,28},{24,16},{28,20},{1,9},{5... | collective-permute-start | bytes 626696 | tf_op jit(solution)/shard_map/ppermute | solution.py:337
  46.1 8.8 %collective-permute-done.13.b = bf16[136,768]{1,0:T(8,128)(2,1)S(1)} collective-permute-done((bf16[136,768]{1,0:T(8,128)(2,1)S(1)}, bf16[136,768]{1,0:T(8,128)(2,1)S(1)}, u32[]{:S(2)}, u32[]{:S(2)}) %collective-permute-start.13) | collective-permute-done | bytes 208928 | tf_op jit(solution)/shard_map/ppermute | solution.py:337
  55.1 0.8 %finish.1 = (f32[1,128]{1,0:T(1,128)}, bf16[128,768]{1,0:T(8,128)(2,1)}, bf16[160,768]{1,0:T(8,128)(2,1)}) custom-call(f32[136,768]{1,0:T(8,128)S(1)} %add.20.t, bf16[136,768]{1,0:T(8,128)(2,1)S(1)} %collective-permute-done.14.g, f32[160,768]{1,0:T(8,128)S(1)} %slice.25.own, bf16[160,768]{1,0:T(8,128)(2,1)S(1)} %collective-permute-done.16.s0, ...), custom_call_target="tpu_custom_call" | custom-call | bytes 2211840 | tf_op jit(solution)/shard_map/finish/pallas_call | solution.py:436
  (32 shorter events, 3.8 us)
Async XLA Ops:
  0.6 16.7 %collective-permute-start = (bf16[128,768]{1,0:T(8,128)(2,1)}, bf16[128,768]{1,0:T(8,128)(2,1)S(1)}, u32[]{:S(2)}, u32[]{:S(2)}) collective-permute-start(bf16[128,768]{1,0:T(8,128)(2,1)} %qa.1), channel_id=1, source_target_pairs={{0,16},{4,20},{8,24},{12,28},{16,0},{20,4},{24,8},{28,12},{1,17},{... | collective-permute-start | bytes 589832 | tf_op jit(solution)/shard_map/ppermute | solution.py:337
  5.5 1.2 %copy-start = (bf16[640,768]{1,0:T(8,128)(2,1)S(1)}, bf16[640,768]{1,0:T(8,128)(2,1)}, u32[]{:S(2)}) copy-start(bf16[640,768]{1,0:T(8,128)(2,1)} %weights.3) | copy-start | bytes 2949124
  6.7 17.9 %copy-start.1 = (bf16[128,768]{1,0:T(8,128)(2,1)S(1)}, bf16[128,768]{1,0:T(8,128)(2,1)}, u32[]{:S(2)}) copy-start(bf16[128,768]{1,0:T(8,128)(2,1)} %qa.1) | copy-start | bytes 589828
  7.3 6.8 %collective-permute-start.2 = (bf16[96,768]{1,0:T(8,128)(2,1)S(1)}, bf16[96,768]{1,0:T(8,128)(2,1)S(1)}, u32[]{:S(2)}, u32[]{:S(2)}) collective-permute-start(bf16[96,768]{1,0:T(8,128)(2,1)S(1)} %get-tuple-element.32), channel_id=1, source_target_pairs={{0,4},{4,0},{8,12},{12,8},{16,20},{20,16},{24,28},{28,24},{1,5},{5... | collective-permute-start | bytes 442376 | tf_op jit(solution)/shard_map/ppermute | solution.py:340
  8.9 8.4 %collective-permute-start.5 = (bf16[96,768]{1,0:T(8,128)(2,1)S(1)}, bf16[96,768]{1,0:T(8,128)(2,1)S(1)}, u32[]{:S(2)}, u32[]{:S(2)}) collective-permute-start(bf16[96,768]{1,0:T(8,128)(2,1)S(1)} %get-tuple-element.35), channel_id=1, source_target_pairs={{0,4},{4,0},{8,12},{12,8},{16,20},{20,16},{24,28},{28,24},{1,5},{5... | collective-permute-start | bytes 442376 | tf_op jit(solution)/shard_map/ppermute | solution.py:340
  9.4 11.2 %collective-permute-start.4 = (bf16[144,768]{1,0:T(8,128)(2,1)S(1)}, bf16[144,768]{1,0:T(8,128)(2,1)S(1)}, u32[]{:S(2)}, u32[]{:S(2)}) collective-permute-start(bf16[144,768]{1,0:T(8,128)(2,1)S(1)} %get-tuple-element.34), channel_id=1, source_target_pairs={{0,4},{4,0},{8,12},{12,8},{16,20},{20,16},{24,28},{28,24},{1,5},{5... | collective-permute-start | bytes 663560 | tf_op jit(solution)/shard_map/ppermute | solution.py:340
  14.1 6.5 %collective-permute-start.3 = (bf16[128,768]{1,0:T(8,128)(2,1)}, bf16[128,768]{1,0:T(8,128)(2,1)S(1)}, u32[]{:S(2)}, u32[]{:S(2)}) collective-permute-start(bf16[128,768]{1,0:T(8,128)(2,1)} %qa.1), channel_id=1, source_target_pairs={{0,8},{4,12},{8,0},{12,4},{16,24},{20,28},{24,16},{28,20},{1,9},{5... | collective-permute-start | bytes 589832 | tf_op jit(solution)/shard_map/ppermute | solution.py:337
  15.7 4.9 %collective-permute-start.7 = (bf16[96,768]{1,0:T(8,128)(2,1)S(1)}, bf16[96,768]{1,0:T(8,128)(2,1)S(1)}, u32[]{:S(2)}, u32[]{:S(2)}) collective-permute-start(bf16[96,768]{1,0:T(8,128)(2,1)S(1)} %collective-permute-done.2.refs_1_), channel_id=1, source_target_pairs={{0,1},{1,0},{2,3},{3,2},{4,5},{5,4},{6,7},{7,6},{8,9},{9,8},{10,11... | collective-permute-start | bytes 442376 | tf_op jit(solution)/shard_map/ppermute | solution.py:343
  17.3 3.3 %collective-permute-start.8 = (bf16[96,768]{1,0:T(8,128)(2,1)S(1)}, bf16[96,768]{1,0:T(8,128)(2,1)S(1)}, u32[]{:S(2)}, u32[]{:S(2)}) collective-permute-start(bf16[96,768]{1,0:T(8,128)(2,1)S(1)} %collective-permute-done.5.refs_2_), channel_id=1, source_target_pairs={{0,1},{1,0},{2,3},{3,2},{4,5},{5,4},{6,7},{7,6},{8,9},{9,8},{10,11... | collective-permute-start | bytes 442376 | tf_op jit(solution)/shard_map/ppermute | solution.py:343
  17.3 7.3 %collective-permute-start.1 = (bf16[128,768]{1,0:T(8,128)(2,1)S(1)}, bf16[128,768]{1,0:T(8,128)(2,1)S(1)}, u32[]{:S(2)}, u32[]{:S(2)}) collective-permute-start(bf16[128,768]{1,0:T(8,128)(2,1)S(1)} %collective-permute-done.qb), channel_id=1, source_target_pairs={{0,8},{4,12},{8,0},{12,4},{16,24},{20,28},{24,16},{28,20},{1,9},{5... | collective-permute-start | bytes 589832 | tf_op jit(solution)/shard_map/ppermute | solution.py:337
  20.6 1.5 %collective-permute-start.6 = (bf16[144,768]{1,0:T(8,128)(2,1)S(1)}, bf16[144,768]{1,0:T(8,128)(2,1)S(1)}, u32[]{:S(2)}, u32[]{:S(2)}) collective-permute-start(bf16[144,768]{1,0:T(8,128)(2,1)S(1)} %collective-permute-done.4.refs_0_), channel_id=1, source_target_pairs={{0,1},{1,0},{2,3},{3,2},{4,5},{5,4},{6,7},{7,6},{8,9},{9,8},{10,11... | collective-permute-start | bytes 663560 | tf_op jit(solution)/shard_map/ppermute | solution.py:343
  25.6 5.6 %collective-permute-start.11 = (f32[24,128]{1,0:T(8,128)S(1)}, f32[24,128]{1,0:T(8,128)S(1)}, u32[]{:S(2)}, u32[]{:S(2)}) collective-permute-start(f32[24,128]{1,0:T(8,128)S(1)} %get-tuple-element.39.m0), channel_id=1, source_target_pairs={{0,24},{4,28},{8,16},{12,20},{16,8},{20,12},{24,0},{28,4},{1,25},{... | collective-permute-start | bytes 36872 | tf_op jit(solution)/shard_map/ppermute | solution.py:337
  27.1 4.6 %collective-permute-start.10 = (f32[24,128]{1,0:T(8,128)S(1)}, f32[24,128]{1,0:T(8,128)S(1)}, u32[]{:S(2)}, u32[]{:S(2)}) collective-permute-start(f32[24,128]{1,0:T(8,128)S(1)} %get-tuple-element.39.m0), channel_id=1, source_target_pairs={{0,16},{4,20},{8,24},{12,28},{16,0},{20,4},{24,8},{28,12},{1,17},{... | collective-permute-start | bytes 36872 | tf_op jit(solution)/shard_map/ppermute | solution.py:337
  28.7 3.7 %collective-permute-start.9 = (f32[24,128]{1,0:T(8,128)S(1)}, f32[24,128]{1,0:T(8,128)S(1)}, u32[]{:S(2)}, u32[]{:S(2)}) collective-permute-start(f32[24,128]{1,0:T(8,128)S(1)} %get-tuple-element.39.m0), channel_id=1, source_target_pairs={{0,8},{4,12},{8,0},{12,4},{16,24},{20,28},{24,16},{28,20},{1,9},{5... | collective-permute-start | bytes 36872 | tf_op jit(solution)/shard_map/ppermute | solution.py:337
  33.7 4.0 %collective-permute-start.15 = (bf16[640,768]{1,0:T(8,128)(2,1)S(1)}, bf16[640,768]{1,0:T(8,128)(2,1)S(1)}, u32[]{:S(2)}, u32[]{:S(2)}) collective-permute-start(bf16[640,768]{1,0:T(8,128)(2,1)S(1)} %get-tuple-element.57), channel_id=1, source_target_pairs={{0,1},{1,0},{2,3},{3,2},{4,5},{5,4},{6,7},{7,6},{8,9},{9,8},{10,11... | collective-permute-start | bytes 2949128 | tf_op jit(solution)/shard_map/ppermute | solution.py:343
  35.0 7.7 %collective-permute-start.12 = (bf16[136,768]{1,0:T(8,128)(2,1)S(1)}, bf16[136,768]{1,0:T(8,128)(2,1)S(1)}, u32[]{:S(2)}, u32[]{:S(2)}) collective-permute-start(bf16[136,768]{1,0:T(8,128)(2,1)S(1)} %get-tuple-element.52), channel_id=1, source_target_pairs={{0,8},{4,12},{8,0},{12,4},{16,24},{20,28},{24,16},{28,20},{1,9},{5... | collective-permute-start | bytes 626696 | tf_op jit(solution)/shard_map/ppermute | solution.py:337
  38.1 17.0 %collective-permute-start.18 = (bf16[160,768]{1,0:T(8,128)(2,1)S(1)}, bf16[160,768]{1,0:T(8,128)(2,1)S(1)}, u32[]{:S(2)}, u32[]{:S(2)}) collective-permute-start(bf16[160,768]{1,0:T(8,128)(2,1)S(1)} %get-tuple-element.63), channel_id=1, source_target_pairs={{0,6},{1,7},{2,4},{3,5},{4,2},{5,3},{6,0},{7,1},{8,14},{9,15},{10,... | collective-permute-start | bytes 737288 | tf_op jit(solution)/shard_map/ppermute | solution.py:349
  40.6 14.5 %collective-permute-start.17 = (bf16[160,768]{1,0:T(8,128)(2,1)S(1)}, bf16[160,768]{1,0:T(8,128)(2,1)S(1)}, u32[]{:S(2)}, u32[]{:S(2)}) collective-permute-start(bf16[160,768]{1,0:T(8,128)(2,1)S(1)} %get-tuple-element.64), channel_id=1, source_target_pairs={{0,4},{4,0},{8,12},{12,8},{16,20},{20,16},{24,28},{28,24},{1,5},{5... | collective-permute-start | bytes 737288 | tf_op jit(solution)/shard_map/ppermute | solution.py:340
  41.1 14.0 %collective-permute-start.16 = (bf16[160,768]{1,0:T(8,128)(2,1)S(1)}, bf16[160,768]{1,0:T(8,128)(2,1)S(1)}, u32[]{:S(2)}, u32[]{:S(2)}) collective-permute-start(bf16[160,768]{1,0:T(8,128)(2,1)S(1)} %get-tuple-element.65), channel_id=1, source_target_pairs={{0,2},{1,3},{2,0},{3,1},{4,6},{5,7},{6,4},{7,5},{8,10},{9,11},{10,... | collective-permute-start | bytes 737288 | tf_op jit(solution)/shard_map/ppermute | solution.py:346
  42.8 12.1 %collective-permute-start.13 = (bf16[136,768]{1,0:T(8,128)(2,1)S(1)}, bf16[136,768]{1,0:T(8,128)(2,1)S(1)}, u32[]{:S(2)}, u32[]{:S(2)}) collective-permute-start(bf16[136,768]{1,0:T(8,128)(2,1)S(1)} %join.1), channel_id=1, source_target_pairs={{0,16},{4,20},{8,24},{12,28},{16,0},{20,4},{24,8},{28,12},{1,17},{... | collective-permute-start | bytes 626696 | tf_op jit(solution)/shard_map/ppermute | solution.py:337
  44.6 10.4 %collective-permute-start.14 = (bf16[136,768]{1,0:T(8,128)(2,1)S(1)}, bf16[136,768]{1,0:T(8,128)(2,1)S(1)}, u32[]{:S(2)}, u32[]{:S(2)}) collective-permute-start(bf16[136,768]{1,0:T(8,128)(2,1)S(1)} %first_terms.3), channel_id=1, source_target_pairs={{0,8},{4,12},{8,0},{12,4},{16,24},{20,28},{24,16},{28,20},{1,9},{5... | collective-permute-start | bytes 626696 | tf_op jit(solution)/shard_map/ppermute | solution.py:337

commit v7 on v6

--- a/solution.py
+++ b/solution.py
@@ -268,10 +268,14 @@
     out[...] = total.astype(out.dtype)
 
 
-def keep_terms(labels, where, m0, m1, m2, m3, e_a, near_b, qa, qb, out, near_a):
+def keep_terms(labels, where, m0, m1, m2, m3, e_a, near_b, qa, qb, arrived, own, side, pair, corner, near_a):
     slab_coefs(0, labels, where, pair_lines((m0, m1, m2, m3), where[0], A), e_a, near_a)
     total = jnp.dot(near_a[...], qa[...], preferred_element_type=jnp.float32)
-    out[...] = total + jnp.dot(near_b[...], qb[...], preferred_element_type=jnp.float32)
+    total += jnp.dot(near_b[...], qb[...], preferred_element_type=jnp.float32)
+    total += arrived[...].astype(jnp.float32)
+    part = own.shape[0]
+    for i, out in enumerate((own, side, pair, corner)):
+        out[...] = total[i * part : (i + 1) * part].astype(out.dtype)
 
 
 def far_block(labels, where, m0, m1, m2, m3, s_ref, e_ref, far, held, last, lines, near):
@@ -416,11 +420,12 @@
         functools.partial(far_block, labels), (term, line, coefs), 1, 8, block_flops // 2, block_bytes, (), "far_block"
     )(*stated, sb, eb, far_b, held)
     g3 = swap(t3, 1)
-    kept, near_a = call(
+    portion = shape((part, width), bf16)
+    own, to_side, to_pair, to_corner, near_a = call(
         functools.partial(keep_terms, labels),
-        (shape((labels, width), f32), coefs),
-        1, 8, block_flops, block_bytes, (), "keep_terms",
-    )(*stated, ea, near_b, qa, qb)
+        (shape((part, width), f32), portion, portion, portion, coefs),
+        1, 9, block_flops, block_bytes, (), "keep_terms",
+    )(*stated, ea, near_b, qa, qb, arrived)
     t2, lines_a = call(
         functools.partial(next_block, labels), (term, line), 1, 8, block_flops // 2, block_bytes, (), "next_block"
     )(*stated, sa, near_a, far_a, held)
@@ -429,15 +434,13 @@
     joined, lines_a = lax.optimization_barrier((joined, lines_a))
     t1 = first_part(near_a, far_a, lines_a, bf16)
     g1, g2 = swap(t1, 1), swap(joined, 2)
-    summed = kept + arrived.astype(f32)
-    sent = summed[part:].astype(bf16)
-    s0, s1, s2 = side(sent[:part]), pair(sent[part : 2 * part]), corner(sent[2 * part :])
+    s0, s1, s2 = side(to_side), pair(to_pair), corner(to_corner)
     both = call(add, shape((rows + 8, width), f32), 0, 2, 0, rows * width * 10, (), "add")(t0, g2)
     loss, query_grad, weight_grad = call(
         finish,
         (shape((1, rows), f32), shape((rows, width), bf16), shape((part, width), bf16)),
         0, 6, 0, 10 * (rows + part) * width, (), "finish",
-    )(both, g1, summed[:part], s0, s1, s2)
+    )(both, g1, own, s0, s1, s2)
     return loss[0], query_grad, weight_grad
 
 

time: 56.1 us -> 56.1 us (level)
    ppermute x1, starting transfers between devices: 2.52 us -> 0.47 us  [corner(): lax.ppermute(x, ('label', 'dp'), [(i * dp + j, (i ^ 1) * dp + (j ^ 2)) fo...]
    ppermute x4, starting transfers between devices: 4.11 us -> 5.13 us  [pair(): return lax.ppermute(x, 'label', [(i, i ^ 1) for i in range(n)])]
    ppermute x1, starting transfers between devices: 0.54 us -> 1.56 us  [side(): return lax.ppermute(x, 'dp', [(i, i ^ 2) for i in range(dp)])]
  transfers between devices with their start and end apart: 19 -> 19, of which waited for: 9 -> 10; matrix products, arithmetic and copies ran while one was open for 5% -> 4% of each run, Pallas kernels for 13% -> 13%
where the time goes in v7:
time: 56.1 us; the launch traced here: 55.9 us
  starting transfers between devices  22.8 us (41%)
  waiting for transfers between devices  18.8 us (34%)
  Pallas kernels  10.1 us (18%)
  local copies, waits for them, and re-layouts  1.9 us (3%)
  other arithmetic  1.54 us (3%)
  between operations  0.78 us (1%)
    ppermute x9, starting transfers between devices, swap(): return lax.ppermute(x, 'label', [(i, i ^ 2 * k) for i in range(n)])  15.5 us
    ppermute x9, waiting for transfers between devices, swap(): return lax.ppermute(x, 'label', [(i, i ^ 2 * k) for i in range(n)])  12.3 us
    ppermute x4, starting transfers between devices, pair(): return lax.ppermute(x, 'label', [(i, i ^ 1) for i in range(n)])  5.13 us
    ppermute x4, waiting for transfers between devices, pair(): return lax.ppermute(x, 'label', [(i, i ^ 1) for i in range(n)])  5.06 us
    pallas_call x1, Pallas kernels, dense_plan(): call(functools.partial(first_scores, cuts), (shape((2 * labels, width), b...  1.7 us
    ppermute x1, starting transfers between devices, side(): return lax.ppermute(x, 'dp', [(i, i ^ 2) for i in range(dp)])  1.56 us
    ppermute x4, waiting for transfers between devices, core(): return lax.ppermute(x, 'dp', [(i, i ^ 1) for i in range(dp)])  1.41 us
    pallas_call x1, Pallas kernels, dense_plan(): call(functools.partial(send_terms, labels), (shape((labels, width), bf16)...  1.3 us
  transfers between devices with their start and end apart: 19, of which 10 were waited for; matrix products, arithmetic and copies ran while one was open for 4% of the time, Pallas kernels for 13%

profile of v7, /device:TPU:0, one launch (start us, length us, event | category | flops | bytes accessed | tf_op | source)
XLA Modules:
  0.0 55.9 jit_solution(17856062963742695920)
XLA Ops:
  0.6 4.1 %collective-permute-start = (bf16[128,768]{1,0:T(8,128)(2,1)}, bf16[128,768]{1,0:T(8,128)(2,1)S(1)}, u32[]{:S(2)}, u32[]{:S(2)}) collective-permute-start(bf16[128,768]{1,0:T(8,128)(2,1)} %qa.1), channel_id=1, source_target_pairs={{0,16},{4,20},{8,24},{12,28},{16,0},{20,4},{24,8},{28,12},{1,17},{... | collective-permute-start | bytes 589832 | tf_op jit(solution)/shard_map/ppermute | solution.py:341
  4.7 0.7 %reshape.13.counts = s32[1,640]{1,0:T(1,128)S(1)} reshape(s32[640]{0:T(1024)} %param.8) | data formatting | bytes 5120 | tf_op jit(solution)/shard_map/reshape | solution.py:373
  5.5 1.2 %copy-done = bf16[640,768]{1,0:T(8,128)(2,1)S(1)} copy-done((bf16[640,768]{1,0:T(8,128)(2,1)S(1)}, bf16[640,768]{1,0:T(8,128)(2,1)}, u32[]{:S(2)}) %copy-start) | copy-done | bytes 983064
  7.3 1.6 %collective-permute-start.2 = (bf16[96,768]{1,0:T(8,128)(2,1)S(1)}, bf16[96,768]{1,0:T(8,128)(2,1)S(1)}, u32[]{:S(2)}, u32[]{:S(2)}) collective-permute-start(bf16[96,768]{1,0:T(8,128)(2,1)S(1)} %get-tuple-element.35), channel_id=1, source_target_pairs={{0,4},{4,0},{8,12},{12,8},{16,20},{20,16},{24,28},{28,24},{1,5},{5... | collective-permute-start | bytes 442376 | tf_op jit(solution)/shard_map/ppermute | solution.py:344
  9.4 1.5 %collective-permute-start.4 = (bf16[144,768]{1,0:T(8,128)(2,1)S(1)}, bf16[144,768]{1,0:T(8,128)(2,1)S(1)}, u32[]{:S(2)}, u32[]{:S(2)}) collective-permute-start(bf16[144,768]{1,0:T(8,128)(2,1)S(1)} %get-tuple-element.37), channel_id=1, source_target_pairs={{0,4},{4,0},{8,12},{12,8},{16,20},{20,16},{24,28},{28,24},{1,5},{5... | collective-permute-start | bytes 663560 | tf_op jit(solution)/shard_map/ppermute | solution.py:344
  10.9 0.8 %select_reduce_fusion = s32[128,4]{0,1:T(4,128)S(1)} fusion(s32[8]{0:T(128)} %param.11, s32[128,4]{0,1:T(4,128)} %param.9), kind=kLoop, calls=%fused_computation | loop fusion | flops 11776 | bytes 4128 | tf_op jit(solution)/shard_map/reduce_sum | solution.py:382
  11.7 0.7 %fusion = s32[1,128]{1,0:T(1,128)S(1)} fusion(s32[128]{0:T(128)} %param.10, s32[128,4]{0,1:T(4,128)S(1)} %select_reduce_fusion), kind=kLoop, calls=%fused_computation.6 | loop fusion | flops 256 | bytes 1536 | tf_op jit(solution)/shard_map/stack | solution.py:385
  12.4 1.8 %collective-permute-done.2.refs_1_ = bf16[96,768]{1,0:T(8,128)(2,1)S(1)} collective-permute-done((bf16[96,768]{1,0:T(8,128)(2,1)S(1)}, bf16[96,768]{1,0:T(8,128)(2,1)S(1)}, u32[]{:S(2)}, u32[]{:S(2)}) %collective-permute-start.2) | collective-permute-done | bytes 147488 | tf_op jit(solution)/shard_map/ppermute | solution.py:344
  14.1 1.6 %collective-permute-start.3 = (bf16[128,768]{1,0:T(8,128)(2,1)}, bf16[128,768]{1,0:T(8,128)(2,1)S(1)}, u32[]{:S(2)}, u32[]{:S(2)}) collective-permute-start(bf16[128,768]{1,0:T(8,128)(2,1)} %qa.1), channel_id=1, source_target_pairs={{0,8},{4,12},{8,0},{12,4},{16,24},{20,28},{24,16},{28,20},{1,9},{5... | collective-permute-start | bytes 589832 | tf_op jit(solution)/shard_map/ppermute | solution.py:341
  15.7 1.6 %collective-permute-done.5.refs_2_ = bf16[96,768]{1,0:T(8,128)(2,1)S(1)} collective-permute-done((bf16[96,768]{1,0:T(8,128)(2,1)S(1)}, bf16[96,768]{1,0:T(8,128)(2,1)S(1)}, u32[]{:S(2)}, u32[]{:S(2)}) %collective-permute-start.5) | collective-permute-done | bytes 147488 | tf_op jit(solution)/shard_map/ppermute | solution.py:344
  17.3 1.6 %collective-permute-start.1 = (bf16[128,768]{1,0:T(8,128)(2,1)S(1)}, bf16[128,768]{1,0:T(8,128)(2,1)S(1)}, u32[]{:S(2)}, u32[]{:S(2)}) collective-permute-start(bf16[128,768]{1,0:T(8,128)(2,1)S(1)} %collective-permute-done.qb), channel_id=1, source_target_pairs={{0,8},{4,12},{8,0},{12,4},{16,24},{20,28},{24,16},{28,20},{1,9},{5... | collective-permute-start | bytes 589832 | tf_op jit(solution)/shard_map/ppermute | solution.py:341
  18.9 1.7 %collective-permute-done.4.refs_0_ = bf16[144,768]{1,0:T(8,128)(2,1)S(1)} collective-permute-done((bf16[144,768]{1,0:T(8,128)(2,1)S(1)}, bf16[144,768]{1,0:T(8,128)(2,1)S(1)}, u32[]{:S(2)}, u32[]{:S(2)}) %collective-permute-start.4) | collective-permute-done | bytes 221216 | tf_op jit(solution)/shard_map/ppermute | solution.py:344
  20.6 1.4 %collective-permute-done.6.refs_3_ = bf16[144,768]{1,0:T(8,128)(2,1)S(1)} collective-permute-done((bf16[144,768]{1,0:T(8,128)(2,1)S(1)}, bf16[144,768]{1,0:T(8,128)(2,1)S(1)}, u32[]{:S(2)}, u32[]{:S(2)}) %collective-permute-start.6) | collective-permute-done | bytes 221216 | tf_op jit(solution)/shard_map/ppermute | solution.py:347
  22.1 1.7 %first_scores.1 = (bf16[1280,768]{1,0:T(8,128)(2,1)S(1)}, bf16[256,768]{1,0:T(8,128)(2,1)S(1)}, f32[1280,256]{1,0:T(8,128)S(1)}, f32[1280,256]{1,0:T(8,128)S(1)}...) custom-call(s32[2]{0:T(128)S(1)} %pad_add_fusion.where, bf16[128,768]{1,0:T(8,128)(2,1)S(1)} %collective-permute-done.3.qa, ...), custom_call_target="tpu_custom_call" | custom-call | flops 503316480 | bytes 4587520 | tf_op jit(solution)/shard_map/first_scores/pallas_call | solution.py:391
  23.8 0.9 %collective-permute-done.1.qb = bf16[128,768]{1,0:T(8,128)(2,1)S(1)} collective-permute-done((bf16[128,768]{1,0:T(8,128)(2,1)S(1)}, bf16[128,768]{1,0:T(8,128)(2,1)S(1)}, u32[]{:S(2)}, u32[]{:S(2)}) %collective-permute-start.1) | collective-permute-done | bytes 196640 | tf_op jit(solution)/shard_map/ppermute | solution.py:341
  24.6 1.0 %last_scores.1 = (bf16[256,768]{1,0:T(8,128)(2,1)S(1)}, f32[1280,256]{1,0:T(8,128)S(1)}, f32[1280,256]{1,0:T(8,128)S(1)}, f32[24,128]{1,0:T(8,128)S(1)}) custom-call(bf16[128,768]{1,0:T(8,128)(2,1)S(1)} %copy-done.1, bf16[128,768]{1,0:T(8,128)(2,1)S(1)} %collective-permute-done.1.qb, bf16[1280,768]{1,0:T(8,128)(2,1)S(1)} %get-tuple-element.39.held, ...), custom_call_target="tpu_custom_call" | custom-call | flops 503316480 | bytes 4587520 | tf_op jit(solution)/shard_map/last_scores/pallas_call | solution.py:396
  25.6 1.5 %collective-permute-start.11 = (f32[24,128]{1,0:T(8,128)S(1)}, f32[24,128]{1,0:T(8,128)S(1)}, u32[]{:S(2)}, u32[]{:S(2)}) collective-permute-start(f32[24,128]{1,0:T(8,128)S(1)} %get-tuple-element.42.m0), channel_id=1, source_target_pairs={{0,24},{4,28},{8,16},{12,20},{16,8},{20,12},{24,0},{28,4},{1,25},{... | collective-permute-start | bytes 36872 | tf_op jit(solution)/shard_map/ppermute | solution.py:341
  27.1 1.6 %collective-permute-start.10 = (f32[24,128]{1,0:T(8,128)S(1)}, f32[24,128]{1,0:T(8,128)S(1)}, u32[]{:S(2)}, u32[]{:S(2)}) collective-permute-start(f32[24,128]{1,0:T(8,128)S(1)} %get-tuple-element.42.m0), channel_id=1, source_target_pairs={{0,16},{4,20},{8,24},{12,28},{16,0},{20,4},{24,8},{28,12},{1,17},{... | collective-permute-start | bytes 36872 | tf_op jit(solution)/shard_map/ppermute | solution.py:341
  28.7 1.3 %collective-permute-start.9 = (f32[24,128]{1,0:T(8,128)S(1)}, f32[24,128]{1,0:T(8,128)S(1)}, u32[]{:S(2)}, u32[]{:S(2)}) collective-permute-start(f32[24,128]{1,0:T(8,128)S(1)} %get-tuple-element.42.m0), channel_id=1, source_target_pairs={{0,8},{4,12},{8,0},{12,4},{16,24},{20,28},{24,16},{28,20},{1,9},{5... | collective-permute-start | bytes 36872 | tf_op jit(solution)/shard_map/ppermute | solution.py:341
  30.0 1.1 %collective-permute-done.11.m3 = f32[24,128]{1,0:T(8,128)S(1)} collective-permute-done((f32[24,128]{1,0:T(8,128)S(1)}, f32[24,128]{1,0:T(8,128)S(1)}, u32[]{:S(2)}, u32[]{:S(2)}) %collective-permute-start.11) | collective-permute-done | bytes 12320 | tf_op jit(solution)/shard_map/ppermute | solution.py:341
  31.7 0.7 %collective-permute-done.9.m1 = f32[24,128]{1,0:T(8,128)S(1)} collective-permute-done((f32[24,128]{1,0:T(8,128)S(1)}, f32[24,128]{1,0:T(8,128)S(1)}, u32[]{:S(2)}, u32[]{:S(2)}) %collective-permute-start.9) | collective-permute-done | bytes 12320 | tf_op jit(solution)/shard_map/ppermute | solution.py:341
  32.4 1.3 %send_terms.1 = (bf16[640,768]{1,0:T(8,128)(2,1)S(1)}, bf16[640,256]{1,0:T(8,128)(2,1)S(1)}, bf16[640,256]{1,0:T(8,128)(2,1)S(1)}) custom-call(s32[2]{0:T(128)S(1)} %pad_add_fusion.where, f32[24,128]{1,0:T(8,128)S(1)} %get-tuple-element.42.m0, f32[24,128]{1,0:T(8,128)S(1)} %collective-permute-done.9.m1, f32[24,128]{1,0:T(8,128)S(1)} %collective-permute-done.10.m2, ...), custom_call_target="tpu_custom_call" | custom-call | flops 503316480 | bytes 4587520 | tf_op jit(solution)/shard_map/send_terms/pallas_call | solution.py:413
  33.8 1.3 %far_block.1 = (bf16[136,768]{1,0:T(8,128)(2,1)S(1)}, f32[2,256]{1,0:T(2,128)S(1)}, bf16[640,256]{1,0:T(8,128)(2,1)S(1)}) custom-call(s32[2]{0:T(128)S(1)} %pad_add_fusion.where, f32[24,128]{1,0:T(8,128)S(1)} %get-tuple-element.42.m0, f32[24,128]{1,0:T(8,128)S(1)} %collective-permute-done.9.m1, f32[24,128]{1,0:T(8,128)S(1)} %collective-permute-done.10.m2, ...), custom_call_target="tpu_custom_call" | custom-call | flops 251658240 | bytes 4587520 | tf_op jit(solution)/shard_map/far_block/pallas_call | solution.py:419
  35.0 1.4 %collective-permute-start.13 = (bf16[136,768]{1,0:T(8,128)(2,1)S(1)}, bf16[136,768]{1,0:T(8,128)(2,1)S(1)}, u32[]{:S(2)}, u32[]{:S(2)}) collective-permute-start(bf16[136,768]{1,0:T(8,128)(2,1)S(1)} %get-tuple-element.56), channel_id=1, source_target_pairs={{0,8},{4,12},{8,0},{12,4},{16,24},{20,28},{24,16},{28,20},{1,9},{5... | collective-permute-start | bytes 626696 | tf_op jit(solution)/shard_map/ppermute | solution.py:341
  36.5 1.2 %keep_terms.1 = (f32[160,768]{1,0:T(8,128)S(1)}, bf16[160,768]{1,0:T(8,128)(2,1)S(1)}, bf16[160,768]{1,0:T(8,128)(2,1)S(1)}, bf16[160,768]{1,0:T(8,128)(2,1)S(1)}, bf16[640,256]{1,0:T(8,128)(2,1)S(1)}) custom-call(s32[2]{0:T(128)S(1)} %pad_add_fusion.where, f32[24,128]{1,0:T(8,128)S(1)} %get-tuple-element.42.m0, f32[24,128]{1,0:T(8,128)S(1)} %collective-permute-done.9.m1, ...), custom_call_target="tpu_custom_call" | custom-call | flops 503316480 | bytes 4587520 | tf_op jit(solution)/shard_map/keep_terms/pallas_call | solution.py:424
  37.7 1.6 %collective-permute-start.16 = (bf16[160,768]{1,0:T(8,128)(2,1)S(1)}, bf16[160,768]{1,0:T(8,128)(2,1)S(1)}, u32[]{:S(2)}, u32[]{:S(2)}) collective-permute-start(bf16[160,768]{1,0:T(8,128)(2,1)S(1)} %get-tuple-element.61), channel_id=1, source_target_pairs={{0,2},{1,3},{2,0},{3,1},{4,6},{5,7},{6,4},{7,5},{8,10},{9,11},{10,... | collective-permute-start | bytes 737288 | tf_op jit(solution)/shard_map/ppermute | solution.py:350
  39.3 1.5 %collective-permute-start.17 = (bf16[160,768]{1,0:T(8,128)(2,1)S(1)}, bf16[160,768]{1,0:T(8,128)(2,1)S(1)}, u32[]{:S(2)}, u32[]{:S(2)}) collective-permute-start(bf16[160,768]{1,0:T(8,128)(2,1)S(1)} %get-tuple-element.62), channel_id=1, source_target_pairs={{0,4},{4,0},{8,12},{12,8},{16,20},{20,16},{24,28},{28,24},{1,5},{5... | collective-permute-start | bytes 737288 | tf_op jit(solution)/shard_map/ppermute | solution.py:344
  41.3 1.1 %next_block.1 = (bf16[136,768]{1,0:T(8,128)(2,1)S(1)}, f32[2,256]{1,0:T(2,128)S(1)}) custom-call(s32[2]{0:T(128)S(1)} %pad_add_fusion.where, f32[24,128]{1,0:T(8,128)S(1)} %get-tuple-element.42.m0, f32[24,128]{1,0:T(8,128)S(1)} %collective-permute-done.9.m1, f32[24,128]{1,0:T(8,128)S(1)} %collective-permute-done.10.m2, ...), custom_call_target="tpu_custom_call" | custom-call | flops 251658240 | bytes 4587520 | tf_op jit(solution)/shard_map/next_block/pallas_call | solution.py:429
  42.7 1.4 %collective-permute-start.14 = (bf16[136,768]{1,0:T(8,128)(2,1)S(1)}, bf16[136,768]{1,0:T(8,128)(2,1)S(1)}, u32[]{:S(2)}, u32[]{:S(2)}) collective-permute-start(bf16[136,768]{1,0:T(8,128)(2,1)S(1)} %join.1), channel_id=1, source_target_pairs={{0,16},{4,20},{8,24},{12,28},{16,0},{20,4},{24,8},{28,12},{1,17},{... | collective-permute-start | bytes 626696 | tf_op jit(solution)/shard_map/ppermute | solution.py:341
  44.6 1.0 %collective-permute-start.15 = (bf16[136,768]{1,0:T(8,128)(2,1)S(1)}, bf16[136,768]{1,0:T(8,128)(2,1)S(1)}, u32[]{:S(2)}, u32[]{:S(2)}) collective-permute-start(bf16[136,768]{1,0:T(8,128)(2,1)S(1)} %first_terms.3), channel_id=1, source_target_pairs={{0,8},{4,12},{8,0},{12,4},{16,24},{20,28},{24,16},{28,20},{1,9},{5... | collective-permute-start | bytes 626696 | tf_op jit(solution)/shard_map/ppermute | solution.py:341
  46.2 8.8 %collective-permute-done.14.b = bf16[136,768]{1,0:T(8,128)(2,1)S(1)} collective-permute-done((bf16[136,768]{1,0:T(8,128)(2,1)S(1)}, bf16[136,768]{1,0:T(8,128)(2,1)S(1)}, u32[]{:S(2)}, u32[]{:S(2)}) %collective-permute-start.14) | collective-permute-done | bytes 208928 | tf_op jit(solution)/shard_map/ppermute | solution.py:341
  55.0 0.8 %finish.1 = (f32[1,128]{1,0:T(1,128)}, bf16[128,768]{1,0:T(8,128)(2,1)}, bf16[160,768]{1,0:T(8,128)(2,1)}) custom-call(f32[136,768]{1,0:T(8,128)S(1)} %add.14.t, bf16[136,768]{1,0:T(8,128)(2,1)S(1)} %collective-permute-done.15.g, f32[160,768]{1,0:T(8,128)S(1)} %get-tuple-element.60.own, bf16[160,768]{1,0:T(8,128)(2,1)S(1)} %collective-permute-done.16.s0, ...), custom_call_target="tpu_custom_call" | custom-call | bytes 2211840 | tf_op jit(solution)/shard_map/finish/pallas_call | solution.py:439
  (29 shorter events, 3.7 us)
Async XLA Ops:
  0.6 16.7 %collective-permute-start = (bf16[128,768]{1,0:T(8,128)(2,1)}, bf16[128,768]{1,0:T(8,128)(2,1)S(1)}, u32[]{:S(2)}, u32[]{:S(2)}) collective-permute-start(bf16[128,768]{1,0:T(8,128)(2,1)} %qa.1), channel_id=1, source_target_pairs={{0,16},{4,20},{8,24},{12,28},{16,0},{20,4},{24,8},{28,12},{1,17},{... | collective-permute-start | bytes 589832 | tf_op jit(solution)/shard_map/ppermute | solution.py:341
  5.5 1.2 %copy-start = (bf16[640,768]{1,0:T(8,128)(2,1)S(1)}, bf16[640,768]{1,0:T(8,128)(2,1)}, u32[]{:S(2)}) copy-start(bf16[640,768]{1,0:T(8,128)(2,1)} %weights.3) | copy-start | bytes 2949124
  7.3 17.3 %copy-start.1 = (bf16[128,768]{1,0:T(8,128)(2,1)S(1)}, bf16[128,768]{1,0:T(8,128)(2,1)}, u32[]{:S(2)}) copy-start(bf16[128,768]{1,0:T(8,128)(2,1)} %qa.1) | copy-start | bytes 589828
  7.3 6.8 %collective-permute-start.2 = (bf16[96,768]{1,0:T(8,128)(2,1)S(1)}, bf16[96,768]{1,0:T(8,128)(2,1)S(1)}, u32[]{:S(2)}, u32[]{:S(2)}) collective-permute-start(bf16[96,768]{1,0:T(8,128)(2,1)S(1)} %get-tuple-element.35), channel_id=1, source_target_pairs={{0,4},{4,0},{8,12},{12,8},{16,20},{20,16},{24,28},{28,24},{1,5},{5... | collective-permute-start | bytes 442376 | tf_op jit(solution)/shard_map/ppermute | solution.py:344
  8.9 8.4 %collective-permute-start.5 = (bf16[96,768]{1,0:T(8,128)(2,1)S(1)}, bf16[96,768]{1,0:T(8,128)(2,1)S(1)}, u32[]{:S(2)}, u32[]{:S(2)}) collective-permute-start(bf16[96,768]{1,0:T(8,128)(2,1)S(1)} %get-tuple-element.38), channel_id=1, source_target_pairs={{0,4},{4,0},{8,12},{12,8},{16,20},{20,16},{24,28},{28,24},{1,5},{5... | collective-permute-start | bytes 442376 | tf_op jit(solution)/shard_map/ppermute | solution.py:344
  9.4 11.2 %collective-permute-start.4 = (bf16[144,768]{1,0:T(8,128)(2,1)S(1)}, bf16[144,768]{1,0:T(8,128)(2,1)S(1)}, u32[]{:S(2)}, u32[]{:S(2)}) collective-permute-start(bf16[144,768]{1,0:T(8,128)(2,1)S(1)} %get-tuple-element.37), channel_id=1, source_target_pairs={{0,4},{4,0},{8,12},{12,8},{16,20},{20,16},{24,28},{28,24},{1,5},{5... | collective-permute-start | bytes 663560 | tf_op jit(solution)/shard_map/ppermute | solution.py:344
  14.1 6.5 %collective-permute-start.3 = (bf16[128,768]{1,0:T(8,128)(2,1)}, bf16[128,768]{1,0:T(8,128)(2,1)S(1)}, u32[]{:S(2)}, u32[]{:S(2)}) collective-permute-start(bf16[128,768]{1,0:T(8,128)(2,1)} %qa.1), channel_id=1, source_target_pairs={{0,8},{4,12},{8,0},{12,4},{16,24},{20,28},{24,16},{28,20},{1,9},{5... | collective-permute-start | bytes 589832 | tf_op jit(solution)/shard_map/ppermute | solution.py:341
  15.7 4.9 %collective-permute-start.7 = (bf16[96,768]{1,0:T(8,128)(2,1)S(1)}, bf16[96,768]{1,0:T(8,128)(2,1)S(1)}, u32[]{:S(2)}, u32[]{:S(2)}) collective-permute-start(bf16[96,768]{1,0:T(8,128)(2,1)S(1)} %collective-permute-done.2.refs_1_), channel_id=1, source_target_pairs={{0,1},{1,0},{2,3},{3,2},{4,5},{5,4},{6,7},{7,6},{8,9},{9,8},{10,11... | collective-permute-start | bytes 442376 | tf_op jit(solution)/shard_map/ppermute | solution.py:347
  17.3 3.3 %collective-permute-start.8 = (bf16[96,768]{1,0:T(8,128)(2,1)S(1)}, bf16[96,768]{1,0:T(8,128)(2,1)S(1)}, u32[]{:S(2)}, u32[]{:S(2)}) collective-permute-start(bf16[96,768]{1,0:T(8,128)(2,1)S(1)} %collective-permute-done.5.refs_2_), channel_id=1, source_target_pairs={{0,1},{1,0},{2,3},{3,2},{4,5},{5,4},{6,7},{7,6},{8,9},{9,8},{10,11... | collective-permute-start | bytes 442376 | tf_op jit(solution)/shard_map/ppermute | solution.py:347
  17.3 7.3 %collective-permute-start.1 = (bf16[128,768]{1,0:T(8,128)(2,1)S(1)}, bf16[128,768]{1,0:T(8,128)(2,1)S(1)}, u32[]{:S(2)}, u32[]{:S(2)}) collective-permute-start(bf16[128,768]{1,0:T(8,128)(2,1)S(1)} %collective-permute-done.qb), channel_id=1, source_target_pairs={{0,8},{4,12},{8,0},{12,4},{16,24},{20,28},{24,16},{28,20},{1,9},{5... | collective-permute-start | bytes 589832 | tf_op jit(solution)/shard_map/ppermute | solution.py:341
  20.6 1.5 %collective-permute-start.6 = (bf16[144,768]{1,0:T(8,128)(2,1)S(1)}, bf16[144,768]{1,0:T(8,128)(2,1)S(1)}, u32[]{:S(2)}, u32[]{:S(2)}) collective-permute-start(bf16[144,768]{1,0:T(8,128)(2,1)S(1)} %collective-permute-done.4.refs_0_), channel_id=1, source_target_pairs={{0,1},{1,0},{2,3},{3,2},{4,5},{5,4},{6,7},{7,6},{8,9},{9,8},{10,11... | collective-permute-start | bytes 663560 | tf_op jit(solution)/shard_map/ppermute | solution.py:347
  25.6 5.6 %collective-permute-start.11 = (f32[24,128]{1,0:T(8,128)S(1)}, f32[24,128]{1,0:T(8,128)S(1)}, u32[]{:S(2)}, u32[]{:S(2)}) collective-permute-start(f32[24,128]{1,0:T(8,128)S(1)} %get-tuple-element.42.m0), channel_id=1, source_target_pairs={{0,24},{4,28},{8,16},{12,20},{16,8},{20,12},{24,0},{28,4},{1,25},{... | collective-permute-start | bytes 36872 | tf_op jit(solution)/shard_map/ppermute | solution.py:341
  27.1 4.6 %collective-permute-start.10 = (f32[24,128]{1,0:T(8,128)S(1)}, f32[24,128]{1,0:T(8,128)S(1)}, u32[]{:S(2)}, u32[]{:S(2)}) collective-permute-start(f32[24,128]{1,0:T(8,128)S(1)} %get-tuple-element.42.m0), channel_id=1, source_target_pairs={{0,16},{4,20},{8,24},{12,28},{16,0},{20,4},{24,8},{28,12},{1,17},{... | collective-permute-start | bytes 36872 | tf_op jit(solution)/shard_map/ppermute | solution.py:341
  28.7 3.7 %collective-permute-start.9 = (f32[24,128]{1,0:T(8,128)S(1)}, f32[24,128]{1,0:T(8,128)S(1)}, u32[]{:S(2)}, u32[]{:S(2)}) collective-permute-start(f32[24,128]{1,0:T(8,128)S(1)} %get-tuple-element.42.m0), channel_id=1, source_target_pairs={{0,8},{4,12},{8,0},{12,4},{16,24},{20,28},{24,16},{28,20},{1,9},{5... | collective-permute-start | bytes 36872 | tf_op jit(solution)/shard_map/ppermute | solution.py:341
  33.7 2.8 %collective-permute-start.12 = (bf16[640,768]{1,0:T(8,128)(2,1)S(1)}, bf16[640,768]{1,0:T(8,128)(2,1)S(1)}, u32[]{:S(2)}, u32[]{:S(2)}) collective-permute-start(bf16[640,768]{1,0:T(8,128)(2,1)S(1)} %get-tuple-element.52), channel_id=1, source_target_pairs={{0,1},{1,0},{2,3},{3,2},{4,5},{5,4},{6,7},{7,6},{8,9},{9,8},{10,11... | collective-permute-start | bytes 2949128 | tf_op jit(solution)/shard_map/ppermute | solution.py:347
  35.0 7.6 %collective-permute-start.13 = (bf16[136,768]{1,0:T(8,128)(2,1)S(1)}, bf16[136,768]{1,0:T(8,128)(2,1)S(1)}, u32[]{:S(2)}, u32[]{:S(2)}) collective-permute-start(bf16[136,768]{1,0:T(8,128)(2,1)S(1)} %get-tuple-element.56), channel_id=1, source_target_pairs={{0,8},{4,12},{8,0},{12,4},{16,24},{20,28},{24,16},{28,20},{1,9},{5... | collective-permute-start | bytes 626696 | tf_op jit(solution)/shard_map/ppermute | solution.py:341
  37.7 17.3 %collective-permute-start.16 = (bf16[160,768]{1,0:T(8,128)(2,1)S(1)}, bf16[160,768]{1,0:T(8,128)(2,1)S(1)}, u32[]{:S(2)}, u32[]{:S(2)}) collective-permute-start(bf16[160,768]{1,0:T(8,128)(2,1)S(1)} %get-tuple-element.61), channel_id=1, source_target_pairs={{0,2},{1,3},{2,0},{3,1},{4,6},{5,7},{6,4},{7,5},{8,10},{9,11},{10,... | collective-permute-start | bytes 737288 | tf_op jit(solution)/shard_map/ppermute | solution.py:350
  39.3 15.7 %collective-permute-start.17 = (bf16[160,768]{1,0:T(8,128)(2,1)S(1)}, bf16[160,768]{1,0:T(8,128)(2,1)S(1)}, u32[]{:S(2)}, u32[]{:S(2)}) collective-permute-start(bf16[160,768]{1,0:T(8,128)(2,1)S(1)} %get-tuple-element.62), channel_id=1, source_target_pairs={{0,4},{4,0},{8,12},{12,8},{16,20},{20,16},{24,28},{28,24},{1,5},{5... | collective-permute-start | bytes 737288 | tf_op jit(solution)/shard_map/ppermute | solution.py:344
  40.8 14.2 %collective-permute-start.18 = (bf16[160,768]{1,0:T(8,128)(2,1)S(1)}, bf16[160,768]{1,0:T(8,128)(2,1)S(1)}, u32[]{:S(2)}, u32[]{:S(2)}) collective-permute-start(bf16[160,768]{1,0:T(8,128)(2,1)S(1)} %get-tuple-element.63), channel_id=1, source_target_pairs={{0,6},{1,7},{2,4},{3,5},{4,2},{5,3},{6,0},{7,1},{8,14},{9,15},{10,... | collective-permute-start | bytes 737288 | tf_op jit(solution)/shard_map/ppermute | solution.py:353
  42.7 12.2 %collective-permute-start.14 = (bf16[136,768]{1,0:T(8,128)(2,1)S(1)}, bf16[136,768]{1,0:T(8,128)(2,1)S(1)}, u32[]{:S(2)}, u32[]{:S(2)}) collective-permute-start(bf16[136,768]{1,0:T(8,128)(2,1)S(1)} %join.1), channel_id=1, source_target_pairs={{0,16},{4,20},{8,24},{12,28},{16,0},{20,4},{24,8},{28,12},{1,17},{... | collective-permute-start | bytes 626696 | tf_op jit(solution)/shard_map/ppermute | solution.py:341
  44.6 10.4 %collective-permute-start.15 = (bf16[136,768]{1,0:T(8,128)(2,1)S(1)}, bf16[136,768]{1,0:T(8,128)(2,1)S(1)}, u32[]{:S(2)}, u32[]{:S(2)}) collective-permute-start(bf16[136,768]{1,0:T(8,128)(2,1)S(1)} %first_terms.3), channel_id=1, source_target_pairs={{0,8},{4,12},{8,0},{12,4},{16,24},{20,28},{24,16},{28,20},{1,9},{5... | collective-permute-start | bytes 626696 | tf_op jit(solution)/shard_map/ppermute | solution.py:341

commit v8 on v7

--- a/solution.py
+++ b/solution.py
@@ -316,14 +316,16 @@
     out[...] = a[...] + b[...].astype(jnp.float32)
 
 
-def finish(t, g, own, s0, s1, s2, loss, query_grad, weight_grad):
-    f32 = jnp.float32
+def finish_labels(own, s0, s1, s2, weight_grad):
+    total = own[...] + sum(s[...].astype(jnp.float32) for s in (s0, s1, s2))
+    weight_grad[...] = total.astype(weight_grad.dtype)
+
+
+def finish_queries(t, g, loss, query_grad):
     rows = query_grad.shape[0]
-    total = t[...] + g[...].astype(f32)
+    total = t[...] + g[...].astype(jnp.float32)
     query_grad[...] = total[:rows].astype(query_grad.dtype)
     loss[...] = total[rows + 1 : rows + 2, :rows] - total[rows : rows + 1, :rows]
-    total = own[...] + sum(s[...].astype(f32) for s in (s0, s1, s2))
-    weight_grad[...] = total.astype(weight_grad.dtype)
 
 
 def dense_plan(queries, weights, counts, hits, positive_offset, cluster_shard):
@@ -435,12 +437,14 @@
     t1 = first_part(near_a, far_a, lines_a, bf16)
     g1, g2 = swap(t1, 1), swap(joined, 2)
     s0, s1, s2 = side(to_side), pair(to_pair), corner(to_corner)
+    weight_grad = call(
+        finish_labels, shape((part, width), bf16), 0, 4, 0, 12 * part * width, (), "finish_labels"
+    )(own, s0, s1, s2)
+    g2, weight_grad = lax.optimization_barrier((g2, weight_grad))
     both = call(add, shape((rows + 8, width), f32), 0, 2, 0, rows * width * 10, (), "add")(t0, g2)
-    loss, query_grad, weight_grad = call(
-        finish,
-        (shape((1, rows), f32), shape((rows, width), bf16), shape((part, width), bf16)),
-        0, 6, 0, 10 * (rows + part) * width, (), "finish",
-    )(both, g1, own, s0, s1, s2)
+    loss, query_grad = call(
+        finish_queries, (shape((1, rows), f32), shape((rows, width), bf16)), 0, 2, 0, 8 * rows * width, (), "finish_queries"
+    )(both, g1)
     return loss[0], query_grad, weight_grad
 
 

time: 56.1 us -> 56 us (level)
  waiting for transfers between devices: 18.8 us -> 17.9 us
  Pallas kernels: 10.1 us -> 10.8 us
    ppermute x9, waiting for transfers between devices: 12.3 us -> 5.29 us  [swap(): return lax.ppermute(x, 'label', [(i, i ^ 2 * k) for i in range(n)])]
    ppermute x4, waiting for transfers between devices: 5.06 us -> 10.8 us  [pair(): return lax.ppermute(x, 'label', [(i, i ^ 1) for i in range(n)])]
    pallas_call x1 -> x2, Pallas kernels: 0.85 us -> 1.53 us  [the longest x1 0.81 us: dense_plan(): call(finish_labels, shape((part, width), bf16), 0, 4, 0, 12 * part * widt...]
  transfers between devices with their start and end apart: 19 -> 19, of which waited for: 10 -> 12; matrix products, arithmetic and copies ran while one was open for 4% -> 4% of each run, Pallas kernels for 13% -> 14%
where the time goes in v8:
time: 56 us; the launch traced here: 55.7 us
  starting transfers between devices  22.8 us (41%)
  waiting for transfers between devices  17.9 us (32%)
  Pallas kernels  10.8 us (19%)
  local copies, waits for them, and re-layouts  1.9 us (3%)
  other arithmetic  1.54 us (3%)
  between operations  0.76 us (1%)
    ppermute x9, starting transfers between devices, swap(): return lax.ppermute(x, 'label', [(i, i ^ 2 * k) for i in range(n)])  15.5 us
    ppermute x4, waiting for transfers between devices, pair(): return lax.ppermute(x, 'label', [(i, i ^ 1) for i in range(n)])  10.8 us
    ppermute x9, waiting for transfers between devices, swap(): return lax.ppermute(x, 'label', [(i, i ^ 2 * k) for i in range(n)])  5.29 us
    ppermute x4, starting transfers between devices, pair(): return lax.ppermute(x, 'label', [(i, i ^ 1) for i in range(n)])  5.13 us
    pallas_call x1, Pallas kernels, dense_plan(): call(functools.partial(first_scores, cuts), (shape((2 * labels, width), b...  1.7 us
    ppermute x1, starting transfers between devices, side(): return lax.ppermute(x, 'dp', [(i, i ^ 2) for i in range(dp)])  1.56 us
    ppermute x4, waiting for transfers between devices, core(): return lax.ppermute(x, 'dp', [(i, i ^ 1) for i in range(dp)])  1.41 us
    pallas_call x1, Pallas kernels, dense_plan(): call(functools.partial(send_terms, labels), (shape((labels, width), bf16)...  1.3 us
  transfers between devices with their start and end apart: 19, of which 12 were waited for; matrix products, arithmetic and copies ran while one was open for 4% of the time, Pallas kernels for 14%

profile of v8, /device:TPU:0, one launch (start us, length us, event | category | flops | bytes accessed | tf_op | source)
XLA Modules:
  0.0 55.7 jit_solution(9769210225561463659)
XLA Ops:
  0.6 4.1 %collective-permute-start = (bf16[128,768]{1,0:T(8,128)(2,1)}, bf16[128,768]{1,0:T(8,128)(2,1)S(1)}, u32[]{:S(2)}, u32[]{:S(2)}) collective-permute-start(bf16[128,768]{1,0:T(8,128)(2,1)} %qa.1), channel_id=1, source_target_pairs={{0,16},{4,20},{8,24},{12,28},{16,0},{20,4},{24,8},{28,12},{1,17},{... | collective-permute-start | bytes 589832 | tf_op jit(solution)/shard_map/ppermute | solution.py:343
  5.5 1.2 %copy-done = bf16[640,768]{1,0:T(8,128)(2,1)S(1)} copy-done((bf16[640,768]{1,0:T(8,128)(2,1)S(1)}, bf16[640,768]{1,0:T(8,128)(2,1)}, u32[]{:S(2)}) %copy-start) | copy-done | bytes 983064
  7.3 1.6 %collective-permute-start.2 = (bf16[96,768]{1,0:T(8,128)(2,1)S(1)}, bf16[96,768]{1,0:T(8,128)(2,1)S(1)}, u32[]{:S(2)}, u32[]{:S(2)}) collective-permute-start(bf16[96,768]{1,0:T(8,128)(2,1)S(1)} %get-tuple-element.36), channel_id=1, source_target_pairs={{0,4},{4,0},{8,12},{12,8},{16,20},{20,16},{24,28},{28,24},{1,5},{5... | collective-permute-start | bytes 442376 | tf_op jit(solution)/shard_map/ppermute | solution.py:346
  9.4 1.5 %collective-permute-start.4 = (bf16[144,768]{1,0:T(8,128)(2,1)S(1)}, bf16[144,768]{1,0:T(8,128)(2,1)S(1)}, u32[]{:S(2)}, u32[]{:S(2)}) collective-permute-start(bf16[144,768]{1,0:T(8,128)(2,1)S(1)} %get-tuple-element.38), channel_id=1, source_target_pairs={{0,4},{4,0},{8,12},{12,8},{16,20},{20,16},{24,28},{28,24},{1,5},{5... | collective-permute-start | bytes 663560 | tf_op jit(solution)/shard_map/ppermute | solution.py:346
  10.9 0.8 %select_reduce_fusion = s32[128,4]{0,1:T(4,128)S(1)} fusion(s32[8]{0:T(128)} %param.11, s32[128,4]{0,1:T(4,128)} %param.9), kind=kLoop, calls=%fused_computation | loop fusion | flops 11776 | bytes 4128 | tf_op jit(solution)/shard_map/reduce_sum | solution.py:384
  12.4 1.8 %collective-permute-done.2.refs_1_ = bf16[96,768]{1,0:T(8,128)(2,1)S(1)} collective-permute-done((bf16[96,768]{1,0:T(8,128)(2,1)S(1)}, bf16[96,768]{1,0:T(8,128)(2,1)S(1)}, u32[]{:S(2)}, u32[]{:S(2)}) %collective-permute-start.2) | collective-permute-done | bytes 147488 | tf_op jit(solution)/shard_map/ppermute | solution.py:346
  14.1 1.6 %collective-permute-start.3 = (bf16[128,768]{1,0:T(8,128)(2,1)}, bf16[128,768]{1,0:T(8,128)(2,1)S(1)}, u32[]{:S(2)}, u32[]{:S(2)}) collective-permute-start(bf16[128,768]{1,0:T(8,128)(2,1)} %qa.1), channel_id=1, source_target_pairs={{0,8},{4,12},{8,0},{12,4},{16,24},{20,28},{24,16},{28,20},{1,9},{5... | collective-permute-start | bytes 589832 | tf_op jit(solution)/shard_map/ppermute | solution.py:343
  15.7 1.6 %collective-permute-done.5.refs_2_ = bf16[96,768]{1,0:T(8,128)(2,1)S(1)} collective-permute-done((bf16[96,768]{1,0:T(8,128)(2,1)S(1)}, bf16[96,768]{1,0:T(8,128)(2,1)S(1)}, u32[]{:S(2)}, u32[]{:S(2)}) %collective-permute-start.5) | collective-permute-done | bytes 147488 | tf_op jit(solution)/shard_map/ppermute | solution.py:346
  17.3 1.6 %collective-permute-start.1 = (bf16[128,768]{1,0:T(8,128)(2,1)S(1)}, bf16[128,768]{1,0:T(8,128)(2,1)S(1)}, u32[]{:S(2)}, u32[]{:S(2)}) collective-permute-start(bf16[128,768]{1,0:T(8,128)(2,1)S(1)} %collective-permute-done.qb), channel_id=1, source_target_pairs={{0,8},{4,12},{8,0},{12,4},{16,24},{20,28},{24,16},{28,20},{1,9},{5... | collective-permute-start | bytes 589832 | tf_op jit(solution)/shard_map/ppermute | solution.py:343
  18.9 1.7 %collective-permute-done.4.refs_0_ = bf16[144,768]{1,0:T(8,128)(2,1)S(1)} collective-permute-done((bf16[144,768]{1,0:T(8,128)(2,1)S(1)}, bf16[144,768]{1,0:T(8,128)(2,1)S(1)}, u32[]{:S(2)}, u32[]{:S(2)}) %collective-permute-start.4) | collective-permute-done | bytes 221216 | tf_op jit(solution)/shard_map/ppermute | solution.py:346
  20.6 1.4 %collective-permute-done.6.refs_3_ = bf16[144,768]{1,0:T(8,128)(2,1)S(1)} collective-permute-done((bf16[144,768]{1,0:T(8,128)(2,1)S(1)}, bf16[144,768]{1,0:T(8,128)(2,1)S(1)}, u32[]{:S(2)}, u32[]{:S(2)}) %collective-permute-start.6) | collective-permute-done | bytes 221216 | tf_op jit(solution)/shard_map/ppermute | solution.py:349
  22.1 1.7 %first_scores.1 = (bf16[1280,768]{1,0:T(8,128)(2,1)S(1)}, bf16[256,768]{1,0:T(8,128)(2,1)S(1)}, f32[1280,256]{1,0:T(8,128)S(1)}, f32[1280,256]{1,0:T(8,128)S(1)}...) custom-call(s32[2]{0:T(128)S(1)} %pad_add_fusion.where, bf16[128,768]{1,0:T(8,128)(2,1)S(1)} %collective-permute-done.3.qa, ...), custom_call_target="tpu_custom_call" | custom-call | flops 503316480 | bytes 4587520 | tf_op jit(solution)/shard_map/first_scores/pallas_call | solution.py:393
  23.8 0.9 %collective-permute-done.1.qb = bf16[128,768]{1,0:T(8,128)(2,1)S(1)} collective-permute-done((bf16[128,768]{1,0:T(8,128)(2,1)S(1)}, bf16[128,768]{1,0:T(8,128)(2,1)S(1)}, u32[]{:S(2)}, u32[]{:S(2)}) %collective-permute-start.1) | collective-permute-done | bytes 196640 | tf_op jit(solution)/shard_map/ppermute | solution.py:343
  24.6 1.0 %last_scores.1 = (bf16[256,768]{1,0:T(8,128)(2,1)S(1)}, f32[1280,256]{1,0:T(8,128)S(1)}, f32[1280,256]{1,0:T(8,128)S(1)}, f32[24,128]{1,0:T(8,128)S(1)}) custom-call(bf16[128,768]{1,0:T(8,128)(2,1)S(1)} %copy-done.1, bf16[128,768]{1,0:T(8,128)(2,1)S(1)} %collective-permute-done.1.qb, bf16[1280,768]{1,0:T(8,128)(2,1)S(1)} %get-tuple-element.40.held, ...), custom_call_target="tpu_custom_call" | custom-call | flops 503316480 | bytes 4587520 | tf_op jit(solution)/shard_map/last_scores/pallas_call | solution.py:398
  25.6 1.5 %collective-permute-start.11 = (f32[24,128]{1,0:T(8,128)S(1)}, f32[24,128]{1,0:T(8,128)S(1)}, u32[]{:S(2)}, u32[]{:S(2)}) collective-permute-start(f32[24,128]{1,0:T(8,128)S(1)} %get-tuple-element.43.m0), channel_id=1, source_target_pairs={{0,24},{4,28},{8,16},{12,20},{16,8},{20,12},{24,0},{28,4},{1,25},{... | collective-permute-start | bytes 36872 | tf_op jit(solution)/shard_map/ppermute | solution.py:343
  27.1 1.6 %collective-permute-start.10 = (f32[24,128]{1,0:T(8,128)S(1)}, f32[24,128]{1,0:T(8,128)S(1)}, u32[]{:S(2)}, u32[]{:S(2)}) collective-permute-start(f32[24,128]{1,0:T(8,128)S(1)} %get-tuple-element.43.m0), channel_id=1, source_target_pairs={{0,16},{4,20},{8,24},{12,28},{16,0},{20,4},{24,8},{28,12},{1,17},{... | collective-permute-start | bytes 36872 | tf_op jit(solution)/shard_map/ppermute | solution.py:343
  28.7 1.3 %collective-permute-start.9 = (f32[24,128]{1,0:T(8,128)S(1)}, f32[24,128]{1,0:T(8,128)S(1)}, u32[]{:S(2)}, u32[]{:S(2)}) collective-permute-start(f32[24,128]{1,0:T(8,128)S(1)} %get-tuple-element.43.m0), channel_id=1, source_target_pairs={{0,8},{4,12},{8,0},{12,4},{16,24},{20,28},{24,16},{28,20},{1,9},{5... | collective-permute-start | bytes 36872 | tf_op jit(solution)/shard_map/ppermute | solution.py:343
  30.0 1.1 %collective-permute-done.11.m3 = f32[24,128]{1,0:T(8,128)S(1)} collective-permute-done((f32[24,128]{1,0:T(8,128)S(1)}, f32[24,128]{1,0:T(8,128)S(1)}, u32[]{:S(2)}, u32[]{:S(2)}) %collective-permute-start.11) | collective-permute-done | bytes 12320 | tf_op jit(solution)/shard_map/ppermute | solution.py:343
  31.7 0.7 %collective-permute-done.9.m1 = f32[24,128]{1,0:T(8,128)S(1)} collective-permute-done((f32[24,128]{1,0:T(8,128)S(1)}, f32[24,128]{1,0:T(8,128)S(1)}, u32[]{:S(2)}, u32[]{:S(2)}) %collective-permute-start.9) | collective-permute-done | bytes 12320 | tf_op jit(solution)/shard_map/ppermute | solution.py:343
  32.4 1.3 %send_terms.1 = (bf16[640,768]{1,0:T(8,128)(2,1)S(1)}, bf16[640,256]{1,0:T(8,128)(2,1)S(1)}, bf16[640,256]{1,0:T(8,128)(2,1)S(1)}) custom-call(s32[2]{0:T(128)S(1)} %pad_add_fusion.where, f32[24,128]{1,0:T(8,128)S(1)} %get-tuple-element.43.m0, f32[24,128]{1,0:T(8,128)S(1)} %collective-permute-done.9.m1, f32[24,128]{1,0:T(8,128)S(1)} %collective-permute-done.10.m2, ...), custom_call_target="tpu_custom_call" | custom-call | flops 503316480 | bytes 4587520 | tf_op jit(solution)/shard_map/send_terms/pallas_call | solution.py:415
  33.8 1.3 %far_block.1 = (bf16[136,768]{1,0:T(8,128)(2,1)S(1)}, f32[2,256]{1,0:T(2,128)S(1)}, bf16[640,256]{1,0:T(8,128)(2,1)S(1)}) custom-call(s32[2]{0:T(128)S(1)} %pad_add_fusion.where, f32[24,128]{1,0:T(8,128)S(1)} %get-tuple-element.43.m0, f32[24,128]{1,0:T(8,128)S(1)} %collective-permute-done.9.m1, f32[24,128]{1,0:T(8,128)S(1)} %collective-permute-done.10.m2, ...), custom_call_target="tpu_custom_call" | custom-call | flops 251658240 | bytes 4587520 | tf_op jit(solution)/shard_map/far_block/pallas_call | solution.py:421
  35.0 1.4 %collective-permute-start.13 = (bf16[136,768]{1,0:T(8,128)(2,1)S(1)}, bf16[136,768]{1,0:T(8,128)(2,1)S(1)}, u32[]{:S(2)}, u32[]{:S(2)}) collective-permute-start(bf16[136,768]{1,0:T(8,128)(2,1)S(1)} %get-tuple-element.57), channel_id=1, source_target_pairs={{0,8},{4,12},{8,0},{12,4},{16,24},{20,28},{24,16},{28,20},{1,9},{5... | collective-permute-start | bytes 626696 | tf_op jit(solution)/shard_map/ppermute | solution.py:343
  36.5 1.2 %keep_terms.1 = (f32[160,768]{1,0:T(8,128)S(1)}, bf16[160,768]{1,0:T(8,128)(2,1)S(1)}, bf16[160,768]{1,0:T(8,128)(2,1)S(1)}, bf16[160,768]{1,0:T(8,128)(2,1)S(1)}, bf16[640,256]{1,0:T(8,128)(2,1)S(1)}) custom-call(s32[2]{0:T(128)S(1)} %pad_add_fusion.where, f32[24,128]{1,0:T(8,128)S(1)} %get-tuple-element.43.m0, f32[24,128]{1,0:T(8,128)S(1)} %collective-permute-done.9.m1, ...), custom_call_target="tpu_custom_call" | custom-call | flops 503316480 | bytes 4587520 | tf_op jit(solution)/shard_map/keep_terms/pallas_call | solution.py:426
  37.7 1.6 %collective-permute-start.15 = (bf16[160,768]{1,0:T(8,128)(2,1)S(1)}, bf16[160,768]{1,0:T(8,128)(2,1)S(1)}, u32[]{:S(2)}, u32[]{:S(2)}) collective-permute-start(bf16[160,768]{1,0:T(8,128)(2,1)S(1)} %get-tuple-element.61), channel_id=1, source_target_pairs={{0,2},{1,3},{2,0},{3,1},{4,6},{5,7},{6,4},{7,5},{8,10},{9,11},{10,... | collective-permute-start | bytes 737288 | tf_op jit(solution)/shard_map/ppermute | solution.py:352
  39.3 1.5 %collective-permute-start.16 = (bf16[160,768]{1,0:T(8,128)(2,1)S(1)}, bf16[160,768]{1,0:T(8,128)(2,1)S(1)}, u32[]{:S(2)}, u32[]{:S(2)}) collective-permute-start(bf16[160,768]{1,0:T(8,128)(2,1)S(1)} %get-tuple-element.62), channel_id=1, source_target_pairs={{0,4},{4,0},{8,12},{12,8},{16,20},{20,16},{24,28},{28,24},{1,5},{5... | collective-permute-start | bytes 737288 | tf_op jit(solution)/shard_map/ppermute | solution.py:346
  41.3 1.1 %next_block.1 = (bf16[136,768]{1,0:T(8,128)(2,1)S(1)}, f32[2,256]{1,0:T(2,128)S(1)}) custom-call(s32[2]{0:T(128)S(1)} %pad_add_fusion.where, f32[24,128]{1,0:T(8,128)S(1)} %get-tuple-element.43.m0, f32[24,128]{1,0:T(8,128)S(1)} %collective-permute-done.9.m1, f32[24,128]{1,0:T(8,128)S(1)} %collective-permute-done.10.m2, ...), custom_call_target="tpu_custom_call" | custom-call | flops 251658240 | bytes 4587520 | tf_op jit(solution)/shard_map/next_block/pallas_call | solution.py:431
  42.7 1.4 %collective-permute-start.14 = (bf16[136,768]{1,0:T(8,128)(2,1)S(1)}, bf16[136,768]{1,0:T(8,128)(2,1)S(1)}, u32[]{:S(2)}, u32[]{:S(2)}) collective-permute-start(bf16[136,768]{1,0:T(8,128)(2,1)S(1)} %join.1), channel_id=1, source_target_pairs={{0,16},{4,20},{8,24},{12,28},{16,0},{20,4},{24,8},{28,12},{1,17},{... | collective-permute-start | bytes 626696 | tf_op jit(solution)/shard_map/ppermute | solution.py:343
  44.6 1.0 %collective-permute-start.18 = (bf16[136,768]{1,0:T(8,128)(2,1)S(1)}, bf16[136,768]{1,0:T(8,128)(2,1)S(1)}, u32[]{:S(2)}, u32[]{:S(2)}) collective-permute-start(bf16[136,768]{1,0:T(8,128)(2,1)S(1)} %first_terms.3), channel_id=1, source_target_pairs={{0,8},{4,12},{8,0},{12,4},{16,24},{20,28},{24,16},{28,20},{1,9},{5... | collective-permute-start | bytes 626696 | tf_op jit(solution)/shard_map/ppermute | solution.py:343
  46.6 5.8 %collective-permute-done.16.s1 = bf16[160,768]{1,0:T(8,128)(2,1)S(1)} collective-permute-done((bf16[160,768]{1,0:T(8,128)(2,1)S(1)}, bf16[160,768]{1,0:T(8,128)(2,1)S(1)}, u32[]{:S(2)}, u32[]{:S(2)}) %collective-permute-start.16) | collective-permute-done | bytes 245792 | tf_op jit(solution)/shard_map/ppermute | solution.py:346
  52.3 0.8 %finish_labels.1 = bf16[160,768]{1,0:T(8,128)(2,1)} custom-call(f32[160,768]{1,0:T(8,128)S(1)} %get-tuple-element.60.own, bf16[160,768]{1,0:T(8,128)(2,1)S(1)} %collective-permute-done.15.s0, bf16[160,768]{1,0:T(8,128)(2,1)S(1)} %collective-permute-done.16.s1, bf16[160,768]{1,0:T(8,128)(2,1)S(1)} %collective-permute-done.17.s2), custom_call_target="tpu_custom_call" | custom-call | bytes 1474560 | tf_op jit(solution)/shard_map/finish_labels/pallas_call | solution.py:440
  53.2 1.8 %collective-permute-done.14.b = bf16[136,768]{1,0:T(8,128)(2,1)S(1)} collective-permute-done((bf16[136,768]{1,0:T(8,128)(2,1)S(1)}, bf16[136,768]{1,0:T(8,128)(2,1)S(1)}, u32[]{:S(2)}, u32[]{:S(2)}) %collective-permute-start.14) | collective-permute-done | bytes 208928 | tf_op jit(solution)/shard_map/ppermute | solution.py:343
  55.0 0.7 %finish_queries.1 = (f32[1,128]{1,0:T(1,128)}, bf16[128,768]{1,0:T(8,128)(2,1)}) custom-call(f32[136,768]{1,0:T(8,128)S(1)} %add.14.t, bf16[136,768]{1,0:T(8,128)(2,1)S(1)} %collective-permute-done.18.g), custom_call_target="tpu_custom_call" | custom-call | bytes 786432 | tf_op jit(solution)/shard_map/finish_queries/pallas_call | solution.py:445
  (30 shorter events, 5.4 us)
Async XLA Ops:
  0.6 16.7 %collective-permute-start = (bf16[128,768]{1,0:T(8,128)(2,1)}, bf16[128,768]{1,0:T(8,128)(2,1)S(1)}, u32[]{:S(2)}, u32[]{:S(2)}) collective-permute-start(bf16[128,768]{1,0:T(8,128)(2,1)} %qa.1), channel_id=1, source_target_pairs={{0,16},{4,20},{8,24},{12,28},{16,0},{20,4},{24,8},{28,12},{1,17},{... | collective-permute-start | bytes 589832 | tf_op jit(solution)/shard_map/ppermute | solution.py:343
  5.5 1.2 %copy-start = (bf16[640,768]{1,0:T(8,128)(2,1)S(1)}, bf16[640,768]{1,0:T(8,128)(2,1)}, u32[]{:S(2)}) copy-start(bf16[640,768]{1,0:T(8,128)(2,1)} %weights.3) | copy-start | bytes 2949124
  7.3 17.3 %copy-start.1 = (bf16[128,768]{1,0:T(8,128)(2,1)S(1)}, bf16[128,768]{1,0:T(8,128)(2,1)}, u32[]{:S(2)}) copy-start(bf16[128,768]{1,0:T(8,128)(2,1)} %qa.1) | copy-start | bytes 589828
  7.3 6.8 %collective-permute-start.2 = (bf16[96,768]{1,0:T(8,128)(2,1)S(1)}, bf16[96,768]{1,0:T(8,128)(2,1)S(1)}, u32[]{:S(2)}, u32[]{:S(2)}) collective-permute-start(bf16[96,768]{1,0:T(8,128)(2,1)S(1)} %get-tuple-element.36), channel_id=1, source_target_pairs={{0,4},{4,0},{8,12},{12,8},{16,20},{20,16},{24,28},{28,24},{1,5},{5... | collective-permute-start | bytes 442376 | tf_op jit(solution)/shard_map/ppermute | solution.py:346
  8.9 8.4 %collective-permute-start.5 = (bf16[96,768]{1,0:T(8,128)(2,1)S(1)}, bf16[96,768]{1,0:T(8,128)(2,1)S(1)}, u32[]{:S(2)}, u32[]{:S(2)}) collective-permute-start(bf16[96,768]{1,0:T(8,128)(2,1)S(1)} %get-tuple-element.39), channel_id=1, source_target_pairs={{0,4},{4,0},{8,12},{12,8},{16,20},{20,16},{24,28},{28,24},{1,5},{5... | collective-permute-start | bytes 442376 | tf_op jit(solution)/shard_map/ppermute | solution.py:346
  9.4 11.2 %collective-permute-start.4 = (bf16[144,768]{1,0:T(8,128)(2,1)S(1)}, bf16[144,768]{1,0:T(8,128)(2,1)S(1)}, u32[]{:S(2)}, u32[]{:S(2)}) collective-permute-start(bf16[144,768]{1,0:T(8,128)(2,1)S(1)} %get-tuple-element.38), channel_id=1, source_target_pairs={{0,4},{4,0},{8,12},{12,8},{16,20},{20,16},{24,28},{28,24},{1,5},{5... | collective-permute-start | bytes 663560 | tf_op jit(solution)/shard_map/ppermute | solution.py:346
  14.1 6.5 %collective-permute-start.3 = (bf16[128,768]{1,0:T(8,128)(2,1)}, bf16[128,768]{1,0:T(8,128)(2,1)S(1)}, u32[]{:S(2)}, u32[]{:S(2)}) collective-permute-start(bf16[128,768]{1,0:T(8,128)(2,1)} %qa.1), channel_id=1, source_target_pairs={{0,8},{4,12},{8,0},{12,4},{16,24},{20,28},{24,16},{28,20},{1,9},{5... | collective-permute-start | bytes 589832 | tf_op jit(solution)/shard_map/ppermute | solution.py:343
  15.7 4.9 %collective-permute-start.7 = (bf16[96,768]{1,0:T(8,128)(2,1)S(1)}, bf16[96,768]{1,0:T(8,128)(2,1)S(1)}, u32[]{:S(2)}, u32[]{:S(2)}) collective-permute-start(bf16[96,768]{1,0:T(8,128)(2,1)S(1)} %collective-permute-done.2.refs_1_), channel_id=1, source_target_pairs={{0,1},{1,0},{2,3},{3,2},{4,5},{5,4},{6,7},{7,6},{8,9},{9,8},{10,11... | collective-permute-start | bytes 442376 | tf_op jit(solution)/shard_map/ppermute | solution.py:349
  17.3 3.3 %collective-permute-start.8 = (bf16[96,768]{1,0:T(8,128)(2,1)S(1)}, bf16[96,768]{1,0:T(8,128)(2,1)S(1)}, u32[]{:S(2)}, u32[]{:S(2)}) collective-permute-start(bf16[96,768]{1,0:T(8,128)(2,1)S(1)} %collective-permute-done.5.refs_2_), channel_id=1, source_target_pairs={{0,1},{1,0},{2,3},{3,2},{4,5},{5,4},{6,7},{7,6},{8,9},{9,8},{10,11... | collective-permute-start | bytes 442376 | tf_op jit(solution)/shard_map/ppermute | solution.py:349
  17.3 7.3 %collective-permute-start.1 = (bf16[128,768]{1,0:T(8,128)(2,1)S(1)}, bf16[128,768]{1,0:T(8,128)(2,1)S(1)}, u32[]{:S(2)}, u32[]{:S(2)}) collective-permute-start(bf16[128,768]{1,0:T(8,128)(2,1)S(1)} %collective-permute-done.qb), channel_id=1, source_target_pairs={{0,8},{4,12},{8,0},{12,4},{16,24},{20,28},{24,16},{28,20},{1,9},{5... | collective-permute-start | bytes 589832 | tf_op jit(solution)/shard_map/ppermute | solution.py:343
  20.6 1.5 %collective-permute-start.6 = (bf16[144,768]{1,0:T(8,128)(2,1)S(1)}, bf16[144,768]{1,0:T(8,128)(2,1)S(1)}, u32[]{:S(2)}, u32[]{:S(2)}) collective-permute-start(bf16[144,768]{1,0:T(8,128)(2,1)S(1)} %collective-permute-done.4.refs_0_), channel_id=1, source_target_pairs={{0,1},{1,0},{2,3},{3,2},{4,5},{5,4},{6,7},{7,6},{8,9},{9,8},{10,11... | collective-permute-start | bytes 663560 | tf_op jit(solution)/shard_map/ppermute | solution.py:349
  25.6 5.6 %collective-permute-start.11 = (f32[24,128]{1,0:T(8,128)S(1)}, f32[24,128]{1,0:T(8,128)S(1)}, u32[]{:S(2)}, u32[]{:S(2)}) collective-permute-start(f32[24,128]{1,0:T(8,128)S(1)} %get-tuple-element.43.m0), channel_id=1, source_target_pairs={{0,24},{4,28},{8,16},{12,20},{16,8},{20,12},{24,0},{28,4},{1,25},{... | collective-permute-start | bytes 36872 | tf_op jit(solution)/shard_map/ppermute | solution.py:343
  27.1 4.6 %collective-permute-start.10 = (f32[24,128]{1,0:T(8,128)S(1)}, f32[24,128]{1,0:T(8,128)S(1)}, u32[]{:S(2)}, u32[]{:S(2)}) collective-permute-start(f32[24,128]{1,0:T(8,128)S(1)} %get-tuple-element.43.m0), channel_id=1, source_target_pairs={{0,16},{4,20},{8,24},{12,28},{16,0},{20,4},{24,8},{28,12},{1,17},{... | collective-permute-start | bytes 36872 | tf_op jit(solution)/shard_map/ppermute | solution.py:343
  28.7 3.7 %collective-permute-start.9 = (f32[24,128]{1,0:T(8,128)S(1)}, f32[24,128]{1,0:T(8,128)S(1)}, u32[]{:S(2)}, u32[]{:S(2)}) collective-permute-start(f32[24,128]{1,0:T(8,128)S(1)} %get-tuple-element.43.m0), channel_id=1, source_target_pairs={{0,8},{4,12},{8,0},{12,4},{16,24},{20,28},{24,16},{28,20},{1,9},{5... | collective-permute-start | bytes 36872 | tf_op jit(solution)/shard_map/ppermute | solution.py:343
  33.7 2.8 %collective-permute-start.12 = (bf16[640,768]{1,0:T(8,128)(2,1)S(1)}, bf16[640,768]{1,0:T(8,128)(2,1)S(1)}, u32[]{:S(2)}, u32[]{:S(2)}) collective-permute-start(bf16[640,768]{1,0:T(8,128)(2,1)S(1)} %get-tuple-element.53), channel_id=1, source_target_pairs={{0,1},{1,0},{2,3},{3,2},{4,5},{5,4},{6,7},{7,6},{8,9},{9,8},{10,11... | collective-permute-start | bytes 2949128 | tf_op jit(solution)/shard_map/ppermute | solution.py:349
  35.0 7.6 %collective-permute-start.13 = (bf16[136,768]{1,0:T(8,128)(2,1)S(1)}, bf16[136,768]{1,0:T(8,128)(2,1)S(1)}, u32[]{:S(2)}, u32[]{:S(2)}) collective-permute-start(bf16[136,768]{1,0:T(8,128)(2,1)S(1)} %get-tuple-element.57), channel_id=1, source_target_pairs={{0,8},{4,12},{8,0},{12,4},{16,24},{20,28},{24,16},{28,20},{1,9},{5... | collective-permute-start | bytes 626696 | tf_op jit(solution)/shard_map/ppermute | solution.py:343
  37.7 8.9 %collective-permute-start.15 = (bf16[160,768]{1,0:T(8,128)(2,1)S(1)}, bf16[160,768]{1,0:T(8,128)(2,1)S(1)}, u32[]{:S(2)}, u32[]{:S(2)}) collective-permute-start(bf16[160,768]{1,0:T(8,128)(2,1)S(1)} %get-tuple-element.61), channel_id=1, source_target_pairs={{0,2},{1,3},{2,0},{3,1},{4,6},{5,7},{6,4},{7,5},{8,10},{9,11},{10,... | collective-permute-start | bytes 737288 | tf_op jit(solution)/shard_map/ppermute | solution.py:352
  39.3 13.1 %collective-permute-start.16 = (bf16[160,768]{1,0:T(8,128)(2,1)S(1)}, bf16[160,768]{1,0:T(8,128)(2,1)S(1)}, u32[]{:S(2)}, u32[]{:S(2)}) collective-permute-start(bf16[160,768]{1,0:T(8,128)(2,1)S(1)} %get-tuple-element.62), channel_id=1, source_target_pairs={{0,4},{4,0},{8,12},{12,8},{16,20},{20,16},{24,28},{28,24},{1,5},{5... | collective-permute-start | bytes 737288 | tf_op jit(solution)/shard_map/ppermute | solution.py:346
  40.8 11.5 %collective-permute-start.17 = (bf16[160,768]{1,0:T(8,128)(2,1)S(1)}, bf16[160,768]{1,0:T(8,128)(2,1)S(1)}, u32[]{:S(2)}, u32[]{:S(2)}) collective-permute-start(bf16[160,768]{1,0:T(8,128)(2,1)S(1)} %get-tuple-element.63), channel_id=1, source_target_pairs={{0,6},{1,7},{2,4},{3,5},{4,2},{5,3},{6,0},{7,1},{8,14},{9,15},{10,... | collective-permute-start | bytes 737288 | tf_op jit(solution)/shard_map/ppermute | solution.py:355
  42.7 12.2 %collective-permute-start.14 = (bf16[136,768]{1,0:T(8,128)(2,1)S(1)}, bf16[136,768]{1,0:T(8,128)(2,1)S(1)}, u32[]{:S(2)}, u32[]{:S(2)}) collective-permute-start(bf16[136,768]{1,0:T(8,128)(2,1)S(1)} %join.1), channel_id=1, source_target_pairs={{0,16},{4,20},{8,24},{12,28},{16,0},{20,4},{24,8},{28,12},{1,17},{... | collective-permute-start | bytes 626696 | tf_op jit(solution)/shard_map/ppermute | solution.py:343
  44.6 10.4 %collective-permute-start.18 = (bf16[136,768]{1,0:T(8,128)(2,1)S(1)}, bf16[136,768]{1,0:T(8,128)(2,1)S(1)}, u32[]{:S(2)}, u32[]{:S(2)}) collective-permute-start(bf16[136,768]{1,0:T(8,128)(2,1)S(1)} %first_terms.3), channel_id=1, source_target_pairs={{0,8},{4,12},{8,0},{12,4},{16,24},{20,28},{24,16},{28,20},{1,9},{5... | collective-permute-start | bytes 626696 | tf_op jit(solution)/shard_map/ppermute | solution.py:343
